TPU v7x, 32 devices: a whole 2x2x4 slice. The times are simulated.
32 devices in a mesh: batch: 4 (over y, x), mp: 8 (over z, core).
Axes of the slice: x: 2, y: 2, z: 4, core: 2. Of those that a mesh axis runs over, the one named last changes fastest.
Arguments:
- input_maps: bfloat16 [2048, 2, 256, 169], P('batch', None, 'mp'), may hold values from -18 to 18
- dense_weight: bfloat16 [2, 9216, 4096], P(None, 'mp'), may hold values from -0.0625 to 0.0625
- dense_bias: float32 [2, 4096], P(None, 'mp'), may hold values from -3 to 3
- stitch_in: float32 [2, 2, 256], P(None, None, 'mp'), may hold values from 0.1 to 0.9
- stitch_out: float32 [2, 2, 4096], P(None, None, 'mp'), may hold values from 0.1 to 0.9
- weight_moment: float32 [2, 9216, 4096], P(None, 'mp'), may hold values from -6 to 6
- bias_moment: float32 [2, 4096], P(None, 'mp'), may hold values from -6 to 6
- stitch_in_moment: float32 [2, 2, 256], P(None, None, 'mp'), may hold values from -6 to 6
- stitch_out_moment: float32 [2, 2, 4096], P(None, None, 'mp'), may hold values from -6 to 6
- cotangent: bfloat16 [2048, 2, 4096], P('batch', None, 'mp'), may hold values from -6 to 6
- live_rows: int32 [4], replicated, may hold values from 1 to 512, 1536 in all
Outputs:
- activations: bfloat16 [2048, 2, 4096], P('batch', None, 'mp')
- maps_grad: bfloat16 [2048, 2, 256, 169], P('batch', None, 'mp')
- weight_grad: float32 [2, 9216, 4096], P(None, 'mp')
- bias_grad: float32 [2, 4096], P(None, 'mp')
- stitch_in_grad: float32 [2, 2, 256], P(None, None, 'mp')
- stitch_out_grad: float32 [2, 2, 4096], P(None, None, 'mp')
- weight_next: bfloat16 [2, 9216, 4096], P(None, 'mp')
- bias_next: float32 [2, 4096], P(None, 'mp')
- stitch_in_next: float32 [2, 2, 256], P(None, None, 'mp')
- stitch_out_next: float32 [2, 2, 4096], P(None, None, 'mp')
- weight_moment_next: float32 [2, 9216, 4096], P(None, 'mp')
- bias_moment_next: float32 [2, 4096], P(None, 'mp')
- stitch_in_moment_next: float32 [2, 2, 256], P(None, None, 'mp')
- stitch_out_moment_next: float32 [2, 2, 4096], P(None, None, 'mp')
Inputs may be any that keep to these rules, and one draw needn't show every extreme that they name: `live_rows`: the counts sum to 1536, and at least one group uses all 512 slots.
All inputs are finite; a program needn't handle non-finite values.
Results may differ from a plain program's by a relative error of at most 0.0061.
Values may be sent and summed in bfloat16 or wider, within the bound.
A program may use at most 384 MiB of HBM per device.

v0:
```python
import jax
import jax.numpy as jnp
from jax import lax
from jax.sharding import PartitionSpec as P

MOMENTUM = 0.9
DENSE_RATE = 0.01
STITCH_RATE = 0.1


def pool_table():
    pixels = jnp.arange(169, dtype=jnp.int32)
    cells = jnp.arange(36, dtype=jnp.int32)
    pixel_row = (pixels // 13)[:, None]
    pixel_col = (pixels % 13)[:, None]
    cell_row = (cells // 6)[None, :]
    cell_col = (cells % 6)[None, :]
    inside = (
        (pixel_row >= 2 * cell_row)
        & (pixel_row <= 2 * cell_row + 2)
        & (pixel_col >= 2 * cell_col)
        & (pixel_col <= 2 * cell_col + 2)
    )
    return inside.astype(jnp.float32)


def gelu_tanh(value):
    return jax.nn.gelu(value, approximate=True)


def head(summed, cotangent, keep, dense_bias, stitch_out):
    hidden = summed + dense_bias[None]
    active, gelu_pull = jax.vjp(gelu_tanh, hidden)
    mixed = stitch_out[None, :, 0] * active[:, 0:1] + stitch_out[None, :, 1] * active[:, 1:2]
    activations = (mixed * keep[:, None, None]).astype(jnp.bfloat16)
    pulled = cotangent.astype(jnp.float32) * keep[:, None, None]
    stitch_out_grad = jnp.einsum("nio,njo->ijo", pulled, active, precision=lax.Precision.HIGHEST)
    active_grad = stitch_out[0][None] * pulled[:, 0:1] + stitch_out[1][None] * pulled[:, 1:2]
    hidden_grad = gelu_pull(active_grad)[0]
    bias_grad = jnp.sum(hidden_grad, axis=0)
    return (activations, hidden_grad.astype(jnp.bfloat16), bias_grad, stitch_out_grad)


def rows_layer(features, cotangent, keep, dense_weight, dense_bias, stitch_out):
    terms = jnp.einsum("ntk,tko->nto", features, dense_weight, preferred_element_type=jnp.float32)
    summed = lax.psum_scatter(terms, "mp", scatter_dimension=2, tiled=True)
    activations, summed_grad, bias_grad, stitch_out_grad = head(
        summed, cotangent, keep, dense_bias, stitch_out
    )
    piece = lax.all_gather(summed_grad, "mp", axis=2, tiled=True)
    inputs_grad = jnp.einsum(
        "nto,tko->ntk", piece, dense_weight, preferred_element_type=jnp.float32
    )
    update = jnp.einsum("ntk,nto->tko", features, piece, preferred_element_type=jnp.float32)
    weight_grad = update
    inputs_grad, weight_grad = (inputs_grad, weight_grad)
    return (activations, inputs_grad.astype(jnp.bfloat16), weight_grad, bias_grad, stitch_out_grad)


def dense_layer(features, cotangent, keep, dense_weight, dense_bias, stitch_out):
    return rows_layer(features, cotangent, keep, dense_weight, dense_bias, stitch_out)


def shards(
    input_maps,
    dense_weight,
    dense_bias,
    stitch_in,
    stitch_out,
    weight_moment,
    bias_moment,
    stitch_in_moment,
    stitch_out_moment,
    cotangent,
    live_rows,
):
    rows = input_maps.shape[0]
    chans = input_maps.shape[2]
    width = chans * 36
    group = lax.axis_index("batch")
    positions = jnp.arange(rows, dtype=jnp.int32)
    keep = (positions < live_rows[group]).astype(jnp.float32)
    table = pool_table()
    pooled = (
        jnp.einsum(
            "ntck,kq->ntcq",
            input_maps,
            table.astype(jnp.bfloat16),
            preferred_element_type=jnp.float32,
        )
        / 9.0
    )
    stitched = (
        stitch_in[None, :, 0, :, None] * pooled[:, 0:1]
        + stitch_in[None, :, 1, :, None] * pooled[:, 1:2]
    )
    features = stitched.reshape(rows, 2, width).astype(jnp.bfloat16)
    activations, inputs_grad, weight_grad, bias_grad, stitch_out_grad = dense_layer(
        features, cotangent, keep, dense_weight, dense_bias, stitch_out
    )
    stitched_grad = inputs_grad.astype(jnp.float32).reshape(rows, 2, chans, 36)
    stitch_in_grad = jnp.einsum(
        "nicq,njcq->ijc", stitched_grad, pooled, precision=lax.Precision.HIGHEST
    )
    pooled_grad = (
        stitch_in[0][None, :, :, None] * stitched_grad[:, 0:1]
        + stitch_in[1][None, :, :, None] * stitched_grad[:, 1:2]
    )
    maps_grad = jnp.einsum(
        "ntcq,kq->ntck", pooled_grad / 9.0, table, precision=lax.Precision.HIGHEST
    ).astype(jnp.bfloat16)
    weight_grad, bias_grad, stitch_in_grad, stitch_out_grad = lax.psum(
        (weight_grad, bias_grad, stitch_in_grad, stitch_out_grad), "batch"
    )
    weight_moment_next = MOMENTUM * weight_moment + weight_grad
    weight_next = (dense_weight.astype(jnp.float32) - DENSE_RATE * weight_moment_next).astype(
        jnp.bfloat16
    )
    bias_moment_next = MOMENTUM * bias_moment + bias_grad
    bias_next = dense_bias - DENSE_RATE * bias_moment_next
    stitch_in_moment_next = MOMENTUM * stitch_in_moment + stitch_in_grad
    stitch_in_next = stitch_in - STITCH_RATE * stitch_in_moment_next
    stitch_out_moment_next = MOMENTUM * stitch_out_moment + stitch_out_grad
    stitch_out_next = stitch_out - STITCH_RATE * stitch_out_moment_next
    return (
        activations,
        maps_grad,
        weight_grad,
        bias_grad,
        stitch_in_grad,
        stitch_out_grad,
        weight_next,
        bias_next,
        stitch_in_next,
        stitch_out_next,
        weight_moment_next,
        bias_moment_next,
        stitch_in_moment_next,
        stitch_out_moment_next,
    )


def solution(mesh):
    in_specs = (
        P("batch", None, "mp", None),
        P(None, "mp", None),
        P(None, "mp"),
        P(None, None, "mp"),
        P(None, None, "mp"),
        P(None, "mp", None),
        P(None, "mp"),
        P(None, None, "mp"),
        P(None, None, "mp"),
        P("batch", None, "mp"),
        P(),
    )
    out_specs = (
        P("batch", None, "mp"),
        P("batch", None, "mp", None),
        P(None, "mp", None),
        P(None, "mp"),
        P(None, None, "mp"),
        P(None, None, "mp"),
        P(None, "mp", None),
        P(None, "mp"),
        P(None, None, "mp"),
        P(None, None, "mp"),
        P(None, "mp", None),
        P(None, "mp"),
        P(None, None, "mp"),
        P(None, None, "mp"),
    )
    return jax.shard_map(shards, mesh=mesh, in_specs=in_specs, out_specs=out_specs, check_vma=False)
```

profile of v0, /device:TPU:0, one launch (start us, length us, event | category | flops | bytes accessed | tf_op | source)
XLA Modules:
  0.0 1055.8 jit_solution(1155175549289408483)
XLA Ops:
  8.4 12.2 %multiply_bitcast_fusion = f32[512,2,32,36]{0,3,2,1:T(8,128)S(1)} fusion(bf16[512,2,32,169]{0,2,3,1:T(8,128)(2,1)} %param.11, s32[169]{0:T(256)S(1)} %get-tuple-element.100, s32[169]{0:T(256)S(1)} %get-tuple-element.101, s32[36]{0:T(128)S(1)} %get-tuple-element.104, s32[36]{0:T(128)S(1)} %get-tuple-element.102, s32[36]{0:T(128)S(1)} %get-tuple-element.105, ...), kind=kOutput, calls=%fused_computation.10 | convolution fusion | flops 399955424 | bytes 15796104 | tf_op jit(solution)/shard_map/ntck,kq->ntcq/dot_general | solution.py:85
  20.6 3.2 fusion.45
  24.5 2.5 mul.288
  27.0 3.4 mul.295
  30.4 19.5 %convolution_bitcast_fusion = f32[512,2,4096]{2,0,1:T(8,128)} fusion(bf16[2,1152,4096]{2,1,0:T(8,128)(2,1)} %param.12, f32[512,1152]{0,1:T(8,128)} %mul.295, f32[2,1152]{1,0:T(2,128)S(1)} %mul.293, f32[512,1152]{0,1:T(8,128)S(1)} %mul.288, f32[2,1152]{1,0:T(2,128)S(1)} %mul.284), kind=kOutput, calls=%fused_computation.4 | convolution fusion | flops 9668395008 | bytes 40388608 | tf_op jit(solution)/shard_map/ntk,tko->nto/dot_general | solution.py:45
  52.0 1.3 copy-done.2
  54.5 166.5 %reduce-scatter.2.cloned.1.call-done = f32[512,2,512]{2,0,1:T(8,128)} async-done(((f32[512,2,4096]{2,0,1:T(8,128)}), f32[512,2,512]{2,0,1:T(8,128)}) %reduce-scatter.2.cloned.1.call-update) | async-done | bytes 2097168 | tf_op jit(solution)/shard_map/reduce_scatter | solution.py:46
  221.0 4.4 fusion.43
  225.5 80.5 %all-gather.2.cloned.1.call-done = bf16[512,2,4096]{2,0,1:T(8,128)(2,1)} async-done(((bf16[512,2,512]{2,0,1:T(8,128)(2,1)}), bf16[512,2,4096]{2,0,1:T(8,128)(2,1)}) %all-gather.2.cloned.1.call-update) | async-done | bytes 8388624 | tf_op jit(solution)/shard_map/all_gather | solution.py:50
  306.0 20.2 %fusion.9 = f32[2,1152,4096]{2,1,0:T(8,128)} fusion(bf16[512,2,4096]{2,0,1:T(8,128)(2,1)} %all-gather.2.cloned.1.call-done, f32[512,1152]{0,1:T(8,128)} %mul.295, f32[2,1152]{1,0:T(2,128)S(1)} %mul.293, f32[512,1152]{0,1:T(8,128)S(1)} %mul.288, f32[2,1152]{1,0:T(2,128)S(1)} %mul.284), kind=kOutput, calls=%fused_computation.18 | convolution fusion | flops 9668395008 | bytes 50874368 | tf_op jit(solution)/shard_map/ntk,nto->tko/dot_general | solution.py:54
  326.2 4.3 copy.103
  330.5 2.4 copy.102
  332.9 20.6 %fusion.49 = f32[512,2,2]{2,1,0:T(2,128)S(1)} fusion(f32[512,2,512]{0,1,2:T(2,128)} %copy.102, f32[512,2,512]{0,1,2:T(2,128)} %copy.103), kind=kOutput, calls=%fused_computation.88 | convolution fusion | flops 12582912 | bytes 4202496 | tf_op jit(solution)/shard_map/nio,njo->ijo/dot_general | solution.py:37
  354.2 2.0 copy.105
  356.3 18.3 %fusion.8 = bf16[512,2,1152]{2,0,1:T(8,128)(2,1)} fusion(bf16[512,2,4096]{2,0,1:T(8,128)(2,1)} %all-gather.2.cloned.1.call-done, bf16[2,1152,4096]{2,1,0:T(8,128)(2,1)} %param.12), kind=kOutput, calls=%fused_computation.15 | convolution fusion | flops 9664856064 | bytes 29622272 | tf_op jit(solution)/shard_map/nto,tko->ntk/dot_general | solution.py:51
  374.6 5.8 copy.95
  380.4 26.9 %fusion.31 = f32[32,2,2]{2,1,0:T(2,128)S(1)} fusion(bf16[512,2,32,36]{0,1,3,2:T(2,128)(2,1)S(1)} %bitcast.66, f32[512,2,32,36]{0,3,2,1:T(8,128)} %copy-done), kind=kOutput, calls=%fused_computation.43 | convolution fusion | flops 28311552 | bytes 7078400 | tf_op jit(solution)/shard_map/nicq,njcq->ijc/dot_general | solution.py:102
  407.4 3.2 fusion.46
  411.3 10.7 %convolution_convert_fusion = bf16[512,2,32,169]{0,3,2,1:T(8,128)(2,1)S(1)} fusion(f32[512,32,36]{0,2,1:T(8,128)S(1)} %bitcast.65, f32[2,32]{1,0:T(2,128)S(1)} %get-tuple-element.97, f32[512,32,36]{0,2,1:T(8,128)S(1)} %bitcast.64, f32[2,32]{1,0:T(2,128)S(1)} %get-tuple-element.96, s32[169]{0:T(256)S(1)} %get-tuple-element.100, ...), kind=kOutput, calls=%fused_computation.5 | convolution fusion | flops 2402625024 | bytes 15796616 | tf_op jit(solution)/shard_map/ntcq,kq->ntck/dot_general | solution.py:109
  422.1 14.8 %copy.106 = bf16[512,2,32,169]{0,2,3,1:T(8,128)(2,1)} copy(bf16[512,2,32,169]{0,3,2,1:T(8,128)(2,1)S(1)} %convolution_convert_fusion) | data formatting | bytes 22151168
  436.8 16.5 %all-reduce = (f32[2,512]{1,0:T(2,128)S(1)}, f32[2,2,32]{2,1,0:T(2,128)S(1)}, f32[2,2,512]{2,1,0:T(2,128)S(1)}) all-reduce(f32[2,512]{1,0:T(2,128)S(1)} %get-tuple-element.81, f32[2,2,32]{2,1,0:T(2,128)S(1)} %bitcast.69, f32[2,2,512]{2,1,0:T(2,128)S(1)} %bitcast.68), channel_id=1, replica_groups=mesh['batch'=4,'mp'=8] {'batch'}, use_global_device_ids=true, to_apply=%region_3.4 | all-reduce | flops 3200 | bytes 25600 | tf_op jit(solution)/shard_map/psum | solution.py:112
  455.1 516.5 %all-reduce.3.cloned.1.call-done = f32[2,1152,4096]{2,1,0:T(8,128)} async-done(((f32[2,1152,4096]{2,1,0:T(8,128)}), f32[2,1152,4096]{2,1,0:T(8,128)}) %all-reduce.3.cloned.1.call-update) | async-done | bytes 37748752 | tf_op jit(solution)/shard_map/psum | solution.py:112
  971.7 49.8 %subtract_convert_fusion = (bf16[2,1152,4096]{2,1,0:T(8,128)(2,1)}, f32[2,1152,4096]{2,1,0:T(8,128)}) fusion(bf16[2,1152,4096]{2,1,0:T(8,128)(2,1)} %param.12, f32[2,1152,4096]{2,1,0:T(8,128)} %all-reduce.3.cloned.1.call-done, f32[2,1152,4096]{2,1,0:T(8,128)} %param.16), kind=kLoop, calls=%fused_computation | loop fusion | flops 56623104 | bytes 150994944 | tf_op jit(solution)/shard_map/convert_element_type | solution.py:116
  1021.5 27.4 %copy.131 = f32[2,1152,4096]{2,1,0:T(8,128)} copy(f32[2,1152,4096]{2,1,0:T(8,128)} %all-reduce.3.cloned.1.call-done) | data formatting | bytes 75497472
  (58 shorter events, 8.5 us)
Async XLA Ops:
  7.2 213.8 %reduce-scatter.2.cloned.1.call-start = ((), (), s32[]{:S(2)}) async-start(), calls=%async_computation.1 | async-start | bytes 18874368 | tf_op jit(solution)/shard_map/reduce_scatter | solution.py:46
  20.6 3.9 copy-start
  49.9 0.7 copy-start.13
  49.9 1.9 copy-start.4
  49.9 1.9 copy-start.3
  49.9 256.1 %all-gather.2.cloned.1.call-start = ((), (), s32[]{:S(2)}) async-start(), calls=%async_computation.2 | async-start | bytes 9437184 | tf_op jit(solution)/shard_map/all_gather | solution.py:50
  52.0 1.3 copy-start.2
  53.4 167.7 %copy-start.6 = (f32[2,512]{1,0:T(2,128)S(1)}, f32[2,512]{1,0:T(2,128)}, u32[]{:S(2)}) copy-start(f32[2,512]{1,0:T(2,128)} %param.13) | copy-start | bytes 12292
  225.4 746.2 %all-reduce.3.cloned.1.call-start = ((), (), s32[]{:S(2)}) async-start(), calls=%async_computation.3 | async-start | bytes 75497472 | tf_op jit(solution)/shard_map/psum | solution.py:112
  326.2 4.3 copy-start.5
  326.2 4.3 copy-start.1
  422.0 31.3 %copy-start.11 = (f32[2,2,32]{2,1,0:T(2,128)S(1)}, f32[2,2,32]{2,1,0:T(2,128)}, u32[]{:S(2)}) copy-start(f32[2,2,32]{2,1,0:T(2,128)} %param.18) | copy-start | bytes 1540
  422.0 31.9 %copy-start.9 = (f32[2,512]{1,0:T(2,128)S(1)}, f32[2,512]{1,0:T(2,128)}, u32[]{:S(2)}) copy-start(f32[2,512]{1,0:T(2,128)} %param.17) | copy-start | bytes 12292
  422.0 32.5 %copy-start.7 = (f32[2,2,512]{2,1,0:T(2,128)S(1)}, f32[2,2,512]{2,1,0:T(2,128)}, u32[]{:S(2)}) copy-start(f32[2,2,512]{2,1,0:T(2,128)} %param.19) | copy-start | bytes 24580
  453.3 568.1 %copy-start.8 = (f32[2,2,512]{2,1,0:T(2,128)}, f32[2,2,512]{2,1,0:T(2,128)S(1)}, u32[]{:S(2)}) copy-start(f32[2,2,512]{2,1,0:T(2,128)S(1)} %get-tuple-element.116) | copy-start | bytes 24580
  453.3 568.1 %copy-start.10 = (f32[2,512]{1,0:T(2,128)}, f32[2,512]{1,0:T(2,128)S(1)}, u32[]{:S(2)}) copy-start(f32[2,512]{1,0:T(2,128)S(1)} %get-tuple-element.114) | copy-start | bytes 12292
  453.3 568.1 %copy-start.12 = (f32[2,2,32]{2,1,0:T(2,128)}, f32[2,2,32]{2,1,0:T(2,128)S(1)}, u32[]{:S(2)}) copy-start(f32[2,2,32]{2,1,0:T(2,128)S(1)} %get-tuple-element.115) | copy-start | bytes 1540
Sparse Core Ops, SparseCore 0:
  50.0 170.9 reduce-scatter.1
  225.6 80.3 all-gather.1
  326.3 645.3 all-reduce.2
where the time goes:
time: 1070 us; the launch traced here: 1060 us
  waiting for transfers between devices  764 us (71%)
  matrix products  128 us (12%)
  local copies, waits for them, and re-layouts  75.5 us (7%)
  other arithmetic  57.2 us (5%)
  blocking collectives  16.5 us (2%)
  between operations  14.5 us (1%)
    psum x1, waiting for transfers between devices, shards(): lax.psum((weight_grad, bias_grad, stitch_in_grad, stitch_out_grad), 'batch')  517 us
    reduce_scatter x1, waiting for transfers between devices, rows_layer(): summed = lax.psum_scatter(terms, 'mp', scatter_dimension=2, tiled=True)  167 us
    all_gather x1, waiting for transfers between devices, rows_layer(): piece = lax.all_gather(summed_grad, 'mp', axis=2, tiled=True)  80.5 us
    convert_element_type x1, other arithmetic, shards(): (dense_weight.astype(jnp.float32) - DENSE_RATE * weight_moment_next).asty...  49.8 us
    unnamed x32, local copies, waits for them, and re-layouts  46.7 us
    dot_general x1, matrix products, shards(): jnp.einsum('nicq,njcq->ijc', stitched_grad, pooled, precision=lax.Precisi...  26.9 us
  transfers between devices with their start and end apart: 3, of which 3 were waited for; matrix products, arithmetic and copies ran while one was open for 11% of the time, Pallas kernels for 0%

commit v1 on v0

--- a/solution.py
+++ b/solution.py
@@ -1,7 +1,16 @@
+import functools
+
 import jax
 import jax.numpy as jnp
 from jax import lax
+from jax.experimental import pallas as pl
+from jax.experimental.pallas import tpu as pltpu
 from jax.sharding import PartitionSpec as P
+
+MESH = pl.DeviceIdType.MESH
+BF16 = jnp.bfloat16
+F32 = jnp.float32
+VMEM_LIMIT = 60 * 1024 * 1024
 
 MOMENTUM = 0.9
 DENSE_RATE = 0.01
@@ -140,6 +149,392 @@
     )
 
 
+def params():
+    return pltpu.CompilerParams(vmem_limit_bytes=VMEM_LIMIT)
+
+
+def full(shape):
+    return pl.BlockSpec(shape, lambda *_: (0,) * len(shape))
+
+
+def fill_order(order, chans, inverse):
+    size = order.shape[0]
+    rows = lax.broadcasted_iota(jnp.int32, (size, size), 0)
+    cols = lax.broadcasted_iota(jnp.int32, (size, size), 1)
+    natural, cells = (cols, rows) if inverse else (rows, cols)
+    shift = chans.bit_length() - 1
+    hit = natural == 36 * (cells & (chans - 1)) + (cells >> shift)
+    order[...] = jnp.where(hit, 1.0, 0.0).astype(BF16)
+
+
+def pooled_row(maps_ref, tower, i):
+    sums = None
+    for dy in range(3):
+        line = [maps_ref[tower, 26 * i + 13 * dy + x].astype(F32) for x in range(13)]
+        cells = [line[2 * j] + line[2 * j + 1] + line[2 * j + 2] for j in range(6)]
+        sums = cells if sums is None else [a + b for a, b in zip(sums, cells)]
+    return [s * (1.0 / 9.0) for s in sums]
+
+
+def pool_kernel(chans, maps_ref, mix_ref, ft_ref, f_ref, order, cells):
+    @pl.when(pl.program_id(0) == 0)
+    def _():
+        fill_order(order, chans, False)
+
+    def row(i, carry):
+        first = pooled_row(maps_ref, 0, i)
+        second = pooled_row(maps_ref, 1, i)
+        for t in range(2):
+            for j in range(6):
+                value = mix_ref[t, 0] * first[j] + mix_ref[t, 1] * second[j]
+                start = pl.multiple_of((6 * i + j) * chans, chans)
+                cells[t, pl.ds(start, chans), :] = value.astype(BF16)
+        return carry
+
+    lax.fori_loop(0, 6, row, 0)
+    for t in range(2):
+        moved = jnp.dot(order[...], cells[t], preferred_element_type=F32)
+        ft_ref[t] = moved.astype(BF16)
+        f_ref[t] = moved.T.astype(BF16)
+
+
+def pool_forward(maps, mix):
+    _, cells, chans, rows = maps.shape
+    width = chans * 36
+    tile = 256
+    return pl.pallas_call(
+        functools.partial(pool_kernel, chans),
+        grid=(rows // tile,),
+        in_specs=[
+            pl.BlockSpec((2, cells, chans, tile), lambda n: (0, 0, 0, n)),
+            full((2, 2, chans, 1)),
+        ],
+        out_specs=[
+            pl.BlockSpec((2, width, tile), lambda n: (0, 0, n)),
+            pl.BlockSpec((2, tile, width), lambda n: (0, n, 0)),
+        ],
+        out_shape=[
+            jax.ShapeDtypeStruct((2, width, rows), BF16),
+            jax.ShapeDtypeStruct((2, rows, width), BF16),
+        ],
+        scratch_shapes=[pltpu.VMEM((width, width), BF16), pltpu.VMEM((2, width, tile), BF16)],
+        compiler_params=params(),
+        name="pool_forward",
+    )(maps, mix)
+
+
+def dense_kernel(f_ref, w_ref, o_ref):
+    o_ref[0, 0] = jnp.dot(f_ref[0], w_ref[0], preferred_element_type=F32).astype(BF16)
+
+
+def dense_forward(f, weight, parts):
+    _, rows, width = f.shape
+    outs = weight.shape[2] // parts
+    return pl.pallas_call(
+        dense_kernel,
+        grid=(2, parts),
+        in_specs=[
+            pl.BlockSpec((1, rows, width), lambda t, j: (t, 0, 0)),
+            pl.BlockSpec((1, width, outs), lambda t, j: (t, 0, j)),
+        ],
+        out_specs=pl.BlockSpec((1, 1, rows, outs), lambda t, j: (j, t, 0, 0)),
+        out_shape=jax.ShapeDtypeStruct((parts, 2, rows, outs), BF16),
+        compiler_params=params(),
+        name="dense_forward",
+    )(f, weight)
+
+
+def gelu_parts(v):
+    root = 0.7978845608028654
+    square = v * v
+    tanh = jnp.tanh(root * v * (1.0 + 0.044715 * square))
+    half = 0.5 * (1.0 + tanh)
+    slope = half + 0.5 * v * (1.0 - tanh * tanh) * root * (1.0 + 3.0 * 0.044715 * square)
+    return v * half, slope
+
+
+def head_kernel(s_ref, cot_ref, keep_ref, bias_ref, mix_ref, act_ref, grad_ref, sums_ref):
+    keep = keep_ref[...]
+    active, slope, pulled = [], [], []
+    for t in range(2):
+        value, rate = gelu_parts(s_ref[t].astype(F32) + bias_ref[t])
+        active.append(value)
+        slope.append(rate)
+        pulled.append(cot_ref[t].astype(F32) * keep)
+    for i in range(2):
+        mixed = mix_ref[2 * i] * active[0] + mix_ref[2 * i + 1] * active[1]
+        act_ref[i] = (mixed * keep).astype(BF16)
+    for j in range(2):
+        pull = mix_ref[j] * pulled[0] + mix_ref[2 + j] * pulled[1]
+        grad = pull * slope[j]
+        grad_ref[j] = grad.astype(BF16)
+        sums_ref[4 + j] = jnp.sum(grad, axis=0, keepdims=True)
+        for i in range(2):
+            sums_ref[2 * i + j] = jnp.sum(pulled[i] * active[j], axis=0, keepdims=True)
+
+
+def dense_head(summed, cot, keep, bias, mix):
+    _, rows, outs = summed.shape
+    tile = 256
+    wide = pl.BlockSpec((2, rows, tile), lambda o: (0, 0, o))
+    return pl.pallas_call(
+        head_kernel,
+        grid=(outs // tile,),
+        in_specs=[
+            wide,
+            wide,
+            full((rows, 1)),
+            pl.BlockSpec((2, 1, tile), lambda o: (0, 0, o)),
+            pl.BlockSpec((4, 1, tile), lambda o: (0, 0, o)),
+        ],
+        out_specs=[wide, wide, pl.BlockSpec((6, 1, tile), lambda o: (0, 0, o))],
+        out_shape=[
+            jax.ShapeDtypeStruct((2, rows, outs), BF16),
+            jax.ShapeDtypeStruct((2, rows, outs), BF16),
+            jax.ShapeDtypeStruct((6, 1, outs), F32),
+        ],
+        compiler_params=params(),
+        name="dense_head",
+    )(summed, cot, keep, bias, mix)
+
+
+def back_kernel(parts, group_ref, w_ref, s_ref, o_ref, total):
+    j = pl.program_id(1)
+    part = lax.dot_general(
+        w_ref[0], s_ref[0, 0, 0], (((1,), (1,)), ((), ())), preferred_element_type=F32
+    )
+
+    @pl.when(j == 0)
+    def _():
+        total[...] = part
+
+    @pl.when(j > 0)
+    def _():
+        total[...] += part
+
+    @pl.when(j == parts - 1)
+    def _():
+        o_ref[0] = total[...].astype(BF16)
+
+
+def dense_backward(group, weight, gathered):
+    _, parts, _, rows, outs = gathered.shape
+    width = weight.shape[1]
+    spec = pltpu.PrefetchScalarGridSpec(
+        num_scalar_prefetch=1,
+        grid=(2, parts),
+        in_specs=[
+            pl.BlockSpec((1, width, outs), lambda t, j, g: (t, 0, j)),
+            pl.BlockSpec((1, 1, 1, rows, outs), lambda t, j, g: (g[0], j, t, 0, 0)),
+        ],
+        out_specs=pl.BlockSpec((1, width, rows), lambda t, j, g: (t, 0, 0)),
+        scratch_shapes=[pltpu.VMEM((width, rows), F32)],
+    )
+    return pl.pallas_call(
+        functools.partial(back_kernel, parts),
+        grid_spec=spec,
+        out_shape=jax.ShapeDtypeStruct((2, width, rows), BF16),
+        compiler_params=params(),
+        name="dense_backward",
+    )(group, weight, gathered)
+
+
+def unpool_kernel(chans, maps_ref, mix_ref, g_ref, out_ref, sums_ref, order, cells, above, total):
+    @pl.when(pl.program_id(0) == 0)
+    def _():
+        fill_order(order, chans, True)
+        total[...] = jnp.zeros_like(total)
+
+    for t in range(2):
+        cells[t] = jnp.dot(order[...], g_ref[t], preferred_element_type=F32)
+    above[...] = jnp.zeros_like(above)
+
+    def row(i, carry):
+        pooled = [pooled_row(maps_ref, t, i) for t in range(2)]
+        for j in range(6):
+            start = pl.multiple_of((6 * i + j) * chans, chans)
+            for t in range(2):
+                grad = cells[t, pl.ds(start, chans), :]
+                for s in range(2):
+                    total[2 * t + s] += grad * pooled[s][j]
+        for t in range(2):
+            mixed = []
+            for j in range(6):
+                start = pl.multiple_of((6 * i + j) * chans, chans)
+                value = mix_ref[0, t] * cells[0, pl.ds(start, chans), :]
+                value += mix_ref[1, t] * cells[1, pl.ds(start, chans), :]
+                mixed.append(value * (1.0 / 9.0))
+            line = []
+            for x in range(13):
+                if x % 2 == 1:
+                    line.append(mixed[x // 2])
+                elif x == 0:
+                    line.append(mixed[0])
+                elif x == 12:
+                    line.append(mixed[5])
+                else:
+                    line.append(mixed[x // 2 - 1] + mixed[x // 2])
+            for x in range(13):
+                out_ref[t, 26 * i + x] = (line[x] + above[t, x]).astype(BF16)
+                out_ref[t, 26 * i + 13 + x] = line[x].astype(BF16)
+                above[t, x] = line[x]
+        return carry
+
+    lax.fori_loop(0, 6, row, 0)
+    for t in range(2):
+        for x in range(13):
+            out_ref[t, 156 + x] = above[t, x].astype(BF16)
+
+    @pl.when(pl.program_id(0) == pl.num_programs(0) - 1)
+    def _():
+        for k in range(4):
+            summed = jnp.sum(total[k], axis=1, keepdims=True)
+            sums_ref[k] = jnp.broadcast_to(summed, sums_ref.shape[1:])
+
+
+def pool_backward(maps, mix, grads):
+    _, cells, chans, rows = maps.shape
+    width = chans * 36
+    tile = 256
+    return pl.pallas_call(
+        functools.partial(unpool_kernel, chans),
+        grid=(rows // tile,),
+        in_specs=[
+            pl.BlockSpec((2, cells, chans, tile), lambda n: (0, 0, 0, n)),
+            full((2, 2, chans, 1)),
+            pl.BlockSpec((2, width, tile), lambda n: (0, 0, n)),
+        ],
+        out_specs=[
+            pl.BlockSpec((2, cells, chans, tile), lambda n: (0, 0, 0, n)),
+            full((4, chans, 128)),
+        ],
+        out_shape=[
+            jax.ShapeDtypeStruct((2, cells, chans, rows), BF16),
+            jax.ShapeDtypeStruct((4, chans, 128), F32),
+        ],
+        scratch_shapes=[
+            pltpu.VMEM((width, width), BF16),
+            pltpu.VMEM((2, width, tile), F32),
+            pltpu.VMEM((2, 13, chans, tile), F32),
+            pltpu.VMEM((4, chans, tile), F32),
+        ],
+        compiler_params=params(),
+        name="pool_backward",
+    )(maps, mix, grads)
+
+
+def update_kernel(groups, ft_ref, s_ref, m_ref, w_ref, grad_ref, next_ref, moment_ref):
+    grad = jnp.dot(ft_ref[0, 0], s_ref[0, 0, 0], preferred_element_type=F32)
+    for b in range(1, groups):
+        grad += jnp.dot(ft_ref[b, 0], s_ref[b, 0, 0], preferred_element_type=F32)
+    grad_ref[0] = grad
+    moment = MOMENTUM * m_ref[0] + grad
+    moment_ref[0] = moment
+    next_ref[0] = (w_ref[0].astype(F32) - DENSE_RATE * moment).astype(BF16)
+
+
+def weight_update(ft_all, gathered, moment, weight):
+    groups, parts, _, rows, outs = gathered.shape
+    width = weight.shape[1]
+    halves = 2
+    tile = outs // halves
+    wide = pl.BlockSpec((1, width, tile), lambda t, j: (t, 0, j))
+    return pl.pallas_call(
+        functools.partial(update_kernel, groups),
+        grid=(2, parts * halves),
+        in_specs=[
+            pl.BlockSpec((groups, 1, width, rows), lambda t, j: (0, t, 0, 0)),
+            pl.BlockSpec(
+                (groups, 1, 1, rows, tile), lambda t, j: (0, j // halves, t, 0, j % halves)
+            ),
+            wide,
+            wide,
+        ],
+        out_specs=[wide, wide, wide],
+        out_shape=[
+            jax.ShapeDtypeStruct(moment.shape, F32),
+            jax.ShapeDtypeStruct(moment.shape, BF16),
+            jax.ShapeDtypeStruct(moment.shape, F32),
+        ],
+        compiler_params=params(),
+        name="weight_update",
+    )(ft_all, gathered, moment, weight)
+
+
+def fast_shards(
+    mesh,
+    input_maps,
+    dense_weight,
+    dense_bias,
+    stitch_in,
+    stitch_out,
+    weight_moment,
+    bias_moment,
+    stitch_in_moment,
+    stitch_out_moment,
+    cotangent,
+    live_rows,
+):
+    rows, _, chans, _ = input_maps.shape
+    outs = dense_bias.shape[1]
+    parts = mesh.shape["mp"]
+    group = lax.axis_index("batch")
+    positions = jnp.arange(rows, dtype=jnp.int32)
+    keep = (positions < live_rows[group]).astype(F32)[:, None]
+    maps = jnp.transpose(input_maps, (1, 3, 2, 0))
+    cot = jnp.transpose(cotangent, (1, 0, 2))
+    mix_in = stitch_in[..., None]
+    mix_out = stitch_out.reshape(4, 1, outs)
+    ft, f = pool_forward(maps, mix_in)
+    ft_all = lax.all_gather(ft, "batch", axis=0, tiled=False)
+    terms = dense_forward(f, dense_weight, parts)
+    summed = lax.psum_scatter(terms, "mp", scatter_dimension=0, tiled=False)
+    acts, grads, sums = dense_head(summed, cot, keep, dense_bias[:, None], mix_out)
+    activations = jnp.transpose(acts, (1, 0, 2))
+    gathered = lax.all_gather(grads, ("batch", "mp"), axis=0, tiled=False)
+    gathered = gathered.reshape((mesh.shape["batch"], parts) + grads.shape)
+    inputs_grad = dense_backward(group[None], dense_weight, gathered)
+    maps_out, mix_sums = pool_backward(maps, mix_in, inputs_grad)
+    maps_grad = jnp.transpose(maps_out, (3, 0, 2, 1))
+    sums, mix_sums = lax.psum((sums, mix_sums[:, :, 0]), "batch")
+    weight_grad, weight_next, weight_moment_next = weight_update(
+        ft_all, gathered, weight_moment, dense_weight
+    )
+    stitch_out_grad = sums[:4].reshape(2, 2, outs)
+    bias_grad = sums[4:].reshape(2, outs)
+    stitch_in_grad = mix_sums.reshape(2, 2, chans)
+    bias_moment_next = MOMENTUM * bias_moment + bias_grad
+    bias_next = dense_bias - DENSE_RATE * bias_moment_next
+    stitch_in_moment_next = MOMENTUM * stitch_in_moment + stitch_in_grad
+    stitch_in_next = stitch_in - STITCH_RATE * stitch_in_moment_next
+    stitch_out_moment_next = MOMENTUM * stitch_out_moment + stitch_out_grad
+    stitch_out_next = stitch_out - STITCH_RATE * stitch_out_moment_next
+    return (
+        activations,
+        maps_grad,
+        weight_grad,
+        bias_grad,
+        stitch_in_grad,
+        stitch_out_grad,
+        weight_next,
+        bias_next,
+        stitch_in_next,
+        stitch_out_next,
+        weight_moment_next,
+        bias_moment_next,
+        stitch_in_moment_next,
+        stitch_out_moment_next,
+    )
+
+
+def choose(mesh, *args):
+    rows, _, chans, _ = args[0].shape
+    outs = args[2].shape[1]
+    if rows % 256 == 0 and outs % 256 == 0 and chans == 32:
+        return fast_shards(mesh, *args)
+    return shards(*args)
+
+
 def solution(mesh):
     in_specs = (
         P("batch", None, "mp", None),
@@ -170,4 +565,5 @@
         P(None, None, "mp"),
         P(None, None, "mp"),
     )
-    return jax.shard_map(shards, mesh=mesh, in_specs=in_specs, out_specs=out_specs, check_vma=False)
+    body = functools.partial(choose, mesh)
+    return jax.shard_map(body, mesh=mesh, in_specs=in_specs, out_specs=out_specs, check_vma=False)

time: 1070 us -> 528 us (0.49); the launches traced: 1060 us -> 526 us
  waiting for transfers between devices: 764 us -> 316 us
  Pallas kernels: 0 us -> 169 us
  matrix products: 128 us -> 0 us
  local copies, waits for them, and re-layouts: 75.5 us -> 8.64 us
  other arithmetic: 57.2 us -> 3.18 us
    psum x1 -> x0, waiting for transfers between devices: 517 us -> none  [shards(): lax.psum((weight_grad, bias_grad, stitch_in_grad, stitch_out_grad), 'batch')]
    pallas_call x0 -> x6, Pallas kernels: none -> 169 us  [the longest x1 88.1 us: weight_update(): pl.pallas_call(functools.partial(update_kernel, groups), grid=(2, parts *...]
    all_gather x1 -> x2, waiting for transfers between devices: 80.5 us -> 227 us  [the longest x1 189 us: fast_shards(): gathered = lax.all_gather(grads, ('batch', 'mp'), axis=0, tiled=False)]
    dot_general x7 -> x0, matrix products: 128 us -> none  [the longest x1 26.9 us: shards(): jnp.einsum('nicq,njcq->ijc', stitched_grad, pooled, precision=lax.Precisi...]
    reduce_scatter x1, waiting for transfers between devices: 167 us -> 88.1 us  [fast_shards(): summed = lax.psum_scatter(terms, 'mp', scatter_dimension=0, tiled=False)]
    convert_element_type x3 -> x1, other arithmetic: 50.8 us -> 1.38 us  [fast_shards(): keep = (positions < live_rows[group]).astype(F32)[:, None]]
    unnamed x32 -> x24, local copies, waits for them, and re-layouts: 46.7 us -> 4.46 us
    mul x14 -> x0, local copies, waits for them, and re-layouts: 14.9 us -> none  [the longest x1 4.26 us: head(): pulled = cotangent.astype(jnp.float32) * keep[:, None, None]]
  transfers between devices with their start and end apart: 3 -> 3, of which waited for: 3 -> 3; matrix products, arithmetic and copies ran while one was open for 11% -> 2% of each run, Pallas kernels for 0% -> 8%
where the time goes in v1:
time: 528 us; the launch traced here: 526 us
  waiting for transfers between devices  316 us (60%)
  Pallas kernels  169 us (32%)
  blocking collectives  15.6 us (3%)
  between operations  13.9 us (3%)
  local copies, waits for them, and re-layouts  8.64 us (2%)
    all_gather x1, waiting for transfers between devices, fast_shards(): gathered = lax.all_gather(grads, ('batch', 'mp'), axis=0, tiled=False)  189 us
    reduce_scatter x1, waiting for transfers between devices, fast_shards(): summed = lax.psum_scatter(terms, 'mp', scatter_dimension=0, tiled=False)  88.1 us
    pallas_call x1, Pallas kernels, weight_update(): pl.pallas_call(functools.partial(update_kernel, groups), grid=(2, parts *...  88.1 us
    all_gather x1, waiting for transfers between devices, fast_shards(): ft_all = lax.all_gather(ft, 'batch', axis=0, tiled=False)  37.8 us
    pallas_call x1, Pallas kernels, dense_backward(): pl.pallas_call(functools.partial(back_kernel, parts), grid_spec=spec, out...  23.4 us
    pallas_call x1, Pallas kernels, dense_forward(): pl.pallas_call(dense_kernel, grid=(2, parts), in_specs=[pl.BlockSpec((1,...  21.2 us
    pallas_call x1, Pallas kernels, pool_backward(): pl.pallas_call(functools.partial(unpool_kernel, chans), grid=(rows // til...  17.9 us
    psum x1, blocking collectives, fast_shards(): sums, mix_sums = lax.psum((sums, mix_sums[:, :, 0]), 'batch')  15.6 us
  transfers between devices with their start and end apart: 3, of which 3 were waited for; matrix products, arithmetic and copies ran while one was open for 2% of the time, Pallas kernels for 8%

profile of v1, /device:TPU:0, one launch (start us, length us, event | category | flops | bytes accessed | tf_op | source)
XLA Modules:
  0.0 526.0 jit_solution(8722185472238560912)
XLA Ops:
  7.2 1.4 copy.33.mix_ref
  8.6 11.5 %pool_forward.1 = (bf16[2,1152,512]{2,1,0:T(8,128)(2,1)}, bf16[2,512,1152]{2,1,0:T(8,128)(2,1)}) custom-call(bf16[2,169,32,512]{3,2,1,0:T(8,128)(2,1)} %bitcast.18, f32[2,2,32,1]{3,2,1,0:T(8,128)} %copy.33.mix_ref), custom_call_target="tpu_custom_call" | custom-call | tf_op jit(solution)/shard_map/pool_forward/pallas_call | solution.py:205
  20.1 21.2 %dense_forward.1 = bf16[8,2,512,512]{3,2,1,0:T(8,128)(2,1)} custom-call(bf16[2,512,1152]{2,1,0:T(8,128)(2,1)} %get-tuple-element.24.f_ref, bf16[2,1152,4096]{2,1,0:T(8,128)(2,1)} %w_ref.5), custom_call_target="tpu_custom_call" | custom-call | tf_op jit(solution)/shard_map/dense_forward/pallas_call | solution.py:233
  41.4 0.0 all-gather.5.cloned.1.call-start
  41.5 0.6 broadcast_in_dim.11.bias_ref
  42.1 0.6 reshape.53.mix_ref
  42.7 1.1 copy.42
  43.8 0.6 dynamic_slice.3
  44.4 1.4 fusion.keep_ref
  45.8 88.1 %reduce-scatter.2.cloned.1.call-done = bf16[1,2,512,512]{3,2,1,0:T(8,128)(2,1)} async-done(((bf16[8,2,512,512]{3,2,1,0:T(8,128)(2,1)}), bf16[1,2,512,512]{3,2,1,0:T(8,128)(2,1)}) %reduce-scatter.2.cloned.1.call-update) | async-done | bytes 1048592 | tf_op jit(solution)/shard_map/reduce_scatter | solution.py:491
  133.9 6.7 %dense_head.1 = (bf16[2,512,512]{2,1,0:T(8,128)(2,1)}, bf16[2,512,512]{2,1,0:T(8,128)(2,1)}, f32[6,1,512]{2,1,0:T(1,128)}) custom-call(bf16[2,512,512]{2,1,0:T(8,128)(2,1)} %bitcast.22, bf16[2,512,512]{2,1,0:T(8,128)(2,1)} %bitcast.21, f32[512,1]{1,0:T(8,128)} %fusion.keep_ref, f32[2,1,512]{2,1,0:T(1,128)} %broadcast_in_dim.11.bias_ref, ...), custom_call_target="tpu_custom_call" | custom-call | tf_op jit(solution)/shard_map/dense_head/pallas_call | solution.py:280
  140.6 0.0 all-gather.7.cloned.1.call-start
  140.6 0.7 all-gather.7.cloned.1.call-update
  141.3 3.3 copy.36
  144.6 189.3 %all-gather.5.cloned.1.call-done = bf16[64,512,512]{2,1,0:T(8,128)(2,1)} async-done(((bf16[2,512,512]{2,1,0:T(8,128)(2,1)}), bf16[64,512,512]{2,1,0:T(8,128)(2,1)}) %all-gather.5.cloned.1.call-update) | async-done | bytes 33554448 | tf_op jit(solution)/shard_map/all_gather | solution.py:494
  333.9 23.4 %dense_backward.1.g_ref = bf16[2,1152,512]{2,1,0:T(8,128)(2,1)} custom-call(s32[1]{0:T(128)} %bitcast.6.group_ref, bf16[2,1152,4096]{2,1,0:T(8,128)(2,1)} %w_ref.5, bf16[4,8,2,512,512]{4,3,2,1,0:T(8,128)(2,1)} %bitcast.16), custom_call_target="tpu_custom_call" | custom-call | tf_op jit(solution)/shard_map/dense_backward/pallas_call | solution.py:333
  357.3 17.9 %pool_backward.1 = (bf16[2,169,32,512]{3,2,1,0:T(8,128)(2,1)}, f32[4,32,128]{2,1,0:T(8,128)}) custom-call(bf16[2,169,32,512]{3,2,1,0:T(8,128)(2,1)} %bitcast.19, f32[2,2,32,1]{3,2,1,0:T(8,128)} %copy.33.mix_ref, bf16[2,1152,512]{2,1,0:T(8,128)(2,1)} %dense_backward.1.g_ref), custom_call_target="tpu_custom_call" | custom-call | tf_op jit(solution)/shard_map/pool_backward/pallas_call | solution.py:399
  375.1 0.9 slice_reduce_fusion
  376.1 15.6 %all-reduce = (f32[6,1,512]{2,1,0:T(1,128)S(1)}, f32[2,2,32]{2,1,0:T(2,128)S(1)}) all-reduce(f32[6,1,512]{2,1,0:T(1,128)S(1)} %copy-done.4, f32[2,2,32]{2,1,0:T(2,128)S(1)} %bitcast.25), channel_id=1, replica_groups=mesh['batch'=4,'mp'=8] {'batch'}, use_global_device_ids=true, to_apply=%region_1.0 | all-reduce | flops 3200 | bytes 25600 | tf_op jit(solution)/shard_map/psum | solution.py:499
  391.8 0.6 multiply_subtract_fusion.2
  392.4 0.6 multiply_subtract_fusion.1
  393.0 0.6 multiply_subtract_fusion
  393.6 37.8 %all-gather.7.cloned.1.call-done = bf16[8,1152,512]{2,1,0:T(8,128)(2,1)} async-done(((bf16[2,1152,512]{2,1,0:T(8,128)(2,1)}), bf16[8,1152,512]{2,1,0:T(8,128)(2,1)}) %all-gather.7.cloned.1.call-update) | async-done | bytes 9437200 | tf_op jit(solution)/shard_map/all_gather | solution.py:489
  431.3 88.1 %weight_update.1 = (f32[2,1152,4096]{2,1,0:T(8,128)}, bf16[2,1152,4096]{2,1,0:T(8,128)(2,1)}, f32[2,1152,4096]{2,1,0:T(8,128)}) custom-call(bf16[4,2,1152,512]{3,2,1,0:T(8,128)(2,1)} %bitcast.20, bf16[4,8,2,512,512]{4,3,2,1,0:T(8,128)(2,1)} %bitcast.17, f32[2,1152,4096]{2,1,0:T(8,128)} %m_ref.1, bf16[2,1152,4096]{2,1,0:T(8,128)(2,1)} %w_ref.5), custom_call_target="tpu_custom_call" | custom-call | tf_op jit(solution)/shard_map/weight_update/pallas_call | solution.py:442
  (28 shorter events, 0.2 us)
Async XLA Ops:
  7.2 126.7 %reduce-scatter.2.cloned.1.call-start = ((), (), s32[]{:S(2)}) async-start(), calls=%async_computation.1 | async-start | bytes 9437184 | tf_op jit(solution)/shard_map/reduce_scatter | solution.py:491
  20.1 21.3 %copy-start.3 = (f32[2,512]{1,0:T(2,128)S(1)}, f32[2,512]{1,0:T(2,128)}, u32[]{:S(2)}) copy-start(f32[2,512]{1,0:T(2,128)} %param.13) | copy-start | bytes 12292
  20.1 21.9 %copy-start.1 = (f32[2,2,512]{2,1,0:T(2,128)S(1)}, f32[2,2,512]{2,1,0:T(2,128)}, u32[]{:S(2)}) copy-start(f32[2,2,512]{2,1,0:T(2,128)} %param.15) | copy-start | bytes 24580
  20.1 22.5 %copy-start = (bf16[512,2,512]{2,1,0:T(2,128)(2,1)S(1)}, bf16[512,2,512]{2,1,0:T(2,128)(2,1)}, u32[]{:S(2)}) copy-start(bf16[512,2,512]{2,1,0:T(2,128)(2,1)} %param.20) | copy-start | bytes 3145732
  20.1 23.7 %copy-start.10 = (s32[4]{0:T(128)S(1)}, s32[4]{0:T(128)}, u32[]{:S(2)}) copy-start(s32[4]{0:T(128)} %param.21) | copy-start | bytes 52
  41.4 292.5 %all-gather.5.cloned.1.call-start = ((), (), s32[]{:S(2)}) async-start(), calls=%async_computation.2 | async-start | bytes 34603008 | tf_op jit(solution)/shard_map/all_gather | solution.py:494
  140.6 290.8 %all-gather.7.cloned.1.call-start = ((), (), s32[]{:S(2)}) async-start(), calls=%async_computation.3 | async-start | bytes 11796480 | tf_op jit(solution)/shard_map/all_gather | solution.py:489
  357.2 18.8 %copy-start.4 = (f32[6,1,512]{2,1,0:T(1,128)S(1)}, f32[6,1,512]{2,1,0:T(1,128)}, u32[]{:S(2)}) copy-start(f32[6,1,512]{2,1,0:T(1,128)} %get-tuple-element.30) | copy-start | bytes 36868
  357.2 34.5 %copy-start.6 = (f32[2,2,32]{2,1,0:T(2,128)S(1)}, f32[2,2,32]{2,1,0:T(2,128)}, u32[]{:S(2)}) copy-start(f32[2,2,32]{2,1,0:T(2,128)} %param.14) | copy-start | bytes 1540
  357.2 34.5 %copy-start.8 = (f32[2,2,32]{2,1,0:T(2,128)S(1)}, f32[2,2,32]{2,1,0:T(2,128)}, u32[]{:S(2)}) copy-start(f32[2,2,32]{2,1,0:T(2,128)} %param.18) | copy-start | bytes 1540
  357.2 35.1 %copy-start.7 = (f32[2,512]{1,0:T(2,128)S(1)}, f32[2,512]{1,0:T(2,128)}, u32[]{:S(2)}) copy-start(f32[2,512]{1,0:T(2,128)} %param.17) | copy-start | bytes 12292
  357.3 35.7 %copy-start.5 = (f32[2,2,512]{2,1,0:T(2,128)S(1)}, f32[2,2,512]{2,1,0:T(2,128)}, u32[]{:S(2)}) copy-start(f32[2,2,512]{2,1,0:T(2,128)} %param.19) | copy-start | bytes 24580
  391.7 127.7 %copy-start.9 = (f32[2,2,32]{2,1,0:T(2,128)}, f32[2,2,32]{2,1,0:T(2,128)S(1)}, u32[]{:S(2)}) copy-start(f32[2,2,32]{2,1,0:T(2,128)S(1)} %get-tuple-element.77) | copy-start | bytes 1540
  391.7 127.7 %copy-start.2 = (f32[2,2,512]{2,1,0:T(2,128)}, f32[2,2,512]{2,1,0:T(2,128)S(1)}, u32[]{:S(2)}) copy-start(f32[2,2,512]{2,1,0:T(2,128)S(1)} %reshape.57) | copy-start | bytes 24580
Sparse Core Ops, SparseCore 0:
  41.5 92.3 reduce-scatter.1
  140.7 193.1 all-gather.4
  336.3 95.0 all-gather.6

commit v2 on v0

--- a/solution.py
+++ b/solution.py
@@ -1,7 +1,16 @@
+import functools
+
 import jax
 import jax.numpy as jnp
 from jax import lax
+from jax.experimental import pallas as pl
+from jax.experimental.pallas import tpu as pltpu
 from jax.sharding import PartitionSpec as P
+
+MESH = pl.DeviceIdType.MESH
+BF16 = jnp.bfloat16
+F32 = jnp.float32
+VMEM_LIMIT = 60 * 1024 * 1024
 
 MOMENTUM = 0.9
 DENSE_RATE = 0.01
@@ -140,6 +149,817 @@
     )
 
 
+def params():
+    return pltpu.CompilerParams(vmem_limit_bytes=VMEM_LIMIT)
+
+
+def full(shape):
+    return pl.BlockSpec(shape, lambda *_: (0,) * len(shape))
+
+
+def fill_order(order, chans, inverse):
+    size = order.shape[0]
+    rows = lax.broadcasted_iota(jnp.int32, (size, size), 0)
+    cols = lax.broadcasted_iota(jnp.int32, (size, size), 1)
+    natural, cells = (cols, rows) if inverse else (rows, cols)
+    shift = chans.bit_length() - 1
+    hit = natural == 36 * (cells & (chans - 1)) + (cells >> shift)
+    order[...] = jnp.where(hit, 1.0, 0.0).astype(BF16)
+
+
+def spread_mix(mix_ref, wide):
+    chans = wide.shape[1]
+    rows = lax.broadcasted_iota(jnp.int32, (chans, chans), 0)
+    cols = lax.broadcasted_iota(jnp.int32, (chans, chans), 1)
+    for k in range(4):
+        line = jnp.broadcast_to(mix_ref[k // 2, pl.ds(k % 2, 1), :], (chans, chans))
+        column = jnp.sum(jnp.where(rows == cols, line, 0.0), axis=1, keepdims=True)
+        wide[k] = jnp.broadcast_to(column, wide.shape[1:])
+
+
+def pooled_row(maps_ref, tower, i, lanes):
+    sums = None
+    for dy in range(3):
+        line = [maps_ref[tower, 26 * i + 13 * dy + x, :, lanes].astype(F32) for x in range(13)]
+        cells = [line[2 * j] + line[2 * j + 1] + line[2 * j + 2] for j in range(6)]
+        sums = cells if sums is None else [a + b for a, b in zip(sums, cells)]
+    return [s * (1.0 / 9.0) for s in sums]
+
+
+def pool_kernel(chans, maps_ref, mix_ref, ft_ref, f_ref, order, cells, wide):
+    @pl.when(pl.program_id(0) == 0)
+    def _():
+        fill_order(order, chans, False)
+        spread_mix(mix_ref, wide)
+
+    tile = cells.shape[2]
+
+    def row(step, carry):
+        i = step // (tile // 128)
+        lanes = pl.ds(pl.multiple_of(step % (tile // 128) * 128, 128), 128)
+        first = pooled_row(maps_ref, 0, i, lanes)
+        second = pooled_row(maps_ref, 1, i, lanes)
+        for t in range(2):
+            for j in range(6):
+                value = wide[2 * t] * first[j] + wide[2 * t + 1] * second[j]
+                start = pl.multiple_of((6 * i + j) * chans, chans)
+                cells[t, pl.ds(start, chans), lanes] = value.astype(BF16)
+        return carry
+
+    lax.fori_loop(0, 6 * (tile // 128), row, 0)
+    for t in range(2):
+        moved = jnp.dot(order[...], cells[t], preferred_element_type=F32)
+        ft_ref[t] = moved.astype(BF16)
+        f_ref[t] = moved.T.astype(BF16)
+
+
+def pool_forward(maps, mix):
+    _, cells, chans, rows = maps.shape
+    width = chans * 36
+    tile = 256
+    return pl.pallas_call(
+        functools.partial(pool_kernel, chans),
+        grid=(rows // tile,),
+        in_specs=[
+            pl.BlockSpec((2, cells, chans, tile), lambda n: (0, 0, 0, n)),
+            full((2, 2, chans)),
+        ],
+        out_specs=[
+            pl.BlockSpec((2, width, tile), lambda n: (0, 0, n)),
+            pl.BlockSpec((2, tile, width), lambda n: (0, n, 0)),
+        ],
+        out_shape=[
+            jax.ShapeDtypeStruct((2, width, rows), BF16),
+            jax.ShapeDtypeStruct((2, rows, width), BF16),
+        ],
+        scratch_shapes=[
+            pltpu.VMEM((width, width), BF16),
+            pltpu.VMEM((2, width, tile), BF16),
+            pltpu.VMEM((4, chans, 128), F32),
+        ],
+        compiler_params=params(),
+        name="pool_forward",
+    )(maps, mix)
+
+
+def gelu_parts(v):
+    root = 0.7978845608028654
+    square = v * v
+    tanh = jnp.tanh(root * v * (1.0 + 0.044715 * square))
+    half = 0.5 * (1.0 + tanh)
+    slope = half + 0.5 * v * (1.0 - tanh * tanh) * root * (1.0 + 3.0 * 0.044715 * square)
+    return v * half, slope
+
+
+def neighbours():
+    b, m = lax.axis_index("batch"), lax.axis_index("mp")
+    columns = (b, b + 1 - 2 * (b % 2), b + 2 - 4 * (b // 2), 3 - b)
+    return b, m, m // 2, m % 2, columns
+
+
+def greet(columns, m, z, c, nz):
+    b, bx, by, _ = columns
+    sibling = m + 1 - 2 * c
+    barrier = pltpu.get_barrier_semaphore()
+
+    def signal(bb, mm):
+        pl.semaphore_signal(barrier, inc=1, device_id=(bb, mm), device_id_type=MESH)
+
+    signal(bx, m)
+    signal(by, m)
+    signal(b, sibling)
+    pl.when(z > 0)(lambda: signal(b, m - 2))
+    pl.when(z < nz - 1)(lambda: signal(b, m + 2))
+    pl.semaphore_wait(barrier, 3 + jnp.where(z > 0, 1, 0) + jnp.where(z < nz - 1, 1, 0))
+
+
+def remote(src, dst, send, recv, device):
+    return pltpu.make_async_remote_copy(
+        src_ref=src, dst_ref=dst, send_sem=send, recv_sem=recv, device_id=device, device_id_type=MESH
+    )
+
+
+def unpool_row(chans, i, lanes, maps_ref, out_ref, cells, above, total, wide):
+    spans = [pl.ds(pl.multiple_of((6 * i + j) * chans, chans), chans) for j in range(6)]
+    pooled = [pooled_row(maps_ref, t, i, lanes) for t in range(2)]
+    sums = [total[k] for k in range(4)]
+    for j in range(6):
+        for t in range(2):
+            grad = cells[t, spans[j], lanes]
+            for s in range(2):
+                sums[2 * t + s] += grad * pooled[s][j]
+    for k in range(4):
+        total[k] = sums[k]
+    for t in range(2):
+        mixed = []
+        for j in range(6):
+            value = wide[t] * cells[0, spans[j], lanes] + wide[2 + t] * cells[1, spans[j], lanes]
+            mixed.append(value * (1.0 / 9.0))
+        for x in range(13):
+            if x % 2 == 1 or x == 0:
+                value = mixed[x // 2]
+            elif x == 12:
+                value = mixed[5]
+            else:
+                value = mixed[x // 2 - 1] + mixed[x // 2]
+            out_ref[t, 26 * i + x, :, lanes] = (value + above[t, x, :, lanes]).astype(BF16)
+            out_ref[t, 26 * i + 13 + x, :, lanes] = value.astype(BF16)
+            above[t, x, :, lanes] = value
+
+
+def gather_kernel(nz, cut, s_ref, sums_ref, w_ref, maps_ref, mix_ref,
+                  g_ref, out_ref, total_ref, mixed_ref,
+                  keep_sem, line_send, line_recv, cross_send, cross_recv,
+                  half_send, half_recv, core_send, core_recv, small_send, small_recv,
+                  maps_sem, out_sem, w_sem, col_sem,
+                  maps_in, maps_out, wbuf, col, grads, cells, order, above, mix_total, wide,
+                  sums_in, sums_mid, mix_in, mix_mid):
+    b, m, z, c, columns = neighbours()
+    rows = s_ref.shape[1]
+    spans = (pl.ds(0, cut), pl.ds(cut, rows - cut))
+    sibling = m + 1 - 2 * c
+    load_maps = pltpu.make_async_copy(maps_ref, maps_in, maps_sem)
+    load_maps.start()
+    greet(columns, m, z, c, nz)
+
+    def small(kind, axis, src, dst):
+        return remote(src, dst, small_send.at[kind, axis], small_recv.at[kind, axis], (columns[1 + axis], m))
+
+    def place(p, r, zz):
+        return g_ref.at[columns[r], 2 * zz + c, :, spans[p], :]
+
+    def half(p, r, zz, t):
+        return g_ref.at[columns[r], 2 * zz + c, t, spans[p], :]
+
+    def line(k, zz, up, own=False):
+        p, r = (0, 0) if k == 0 else (1, k - 1)
+        src = s_ref.at[:, spans[p], :] if own else place(p, r, zz)
+        side = 1 if up else 0
+        to = m + 2 if up else m - 2
+        return remote(src, place(p, r, zz), line_send.at[side, k, zz], line_recv.at[k, zz], (b, to))
+
+    def cross(p, axis, zz, own=False):
+        src = s_ref.at[:, spans[p], :] if own else place(p, 0, zz)
+        slot = zz if p == 0 else nz
+        return remote(
+            src, place(p, 0, zz), cross_send.at[axis, slot], cross_recv.at[axis, slot], (columns[1 + axis], m)
+        )
+
+    def cross_wait(p, axis, zz):
+        slot = zz if p == 0 else nz
+        here = place(p, 1 + axis, zz)
+        remote(here, here, cross_send.at[axis, slot], cross_recv.at[axis, slot], (columns[1 + axis], m)).wait_recv()
+
+    def diagonal(p, axis, zz):
+        slot = zz if p == 0 else nz
+        block = half(p, 2 - axis, zz, 1 - axis)
+        return remote(block, block, half_send.at[axis, slot], half_recv.at[axis, slot], (columns[1 + axis], m))
+
+    def diagonal_wait(p, axis, zz):
+        slot = zz if p == 0 else nz
+        block = half(p, 3, zz, 1 - axis)
+        remote(block, block, half_send.at[axis, slot], half_recv.at[axis, slot], (columns[1 + axis], m)).wait_recv()
+
+    def core(p, r, zz, own=False):
+        src = s_ref.at[:, spans[p], :] if own else place(p, r, zz)
+        return remote(src, place(p, r, zz), core_send.at[p, r, zz], core_recv.at[p, r, zz], (b, sibling))
+
+    def core_wait(p, r, zz):
+        block = g_ref.at[columns[r], 2 * zz + 1 - c, :, spans[p], :]
+        remote(block, block, core_send.at[p, r, zz], core_recv.at[p, r, zz], (b, sibling)).wait_recv()
+
+    def sides(d, body):
+        if d == 0:
+            body(z, None)
+            return
+        pl.when(z + d < nz)(lambda: body(z + d, False))
+        pl.when(z - d >= 0)(lambda: body(z - d, True))
+
+    def onward(k, zz, up):
+        if up:
+            pl.when(z < nz - 1)(lambda: line(k, zz, True).start())
+        else:
+            pl.when(z > 0)(lambda: line(k, zz, False).start())
+
+    mine = pltpu.make_async_copy(s_ref, g_ref.at[b, m], keep_sem)
+    cross(1, 0, z, True).start()
+    cross(1, 1, z, True).start()
+    pl.when(z < nz - 1)(lambda: line(0, z, True, True).start())
+    pl.when(z > 0)(lambda: line(0, z, False, True).start())
+    cross(0, 0, z, True).start()
+    cross(0, 1, z, True).start()
+    pl.when(z < nz - 1)(lambda: line(1, z, True, True).start())
+    pl.when(z > 0)(lambda: line(1, z, False, True).start())
+    first_sums = small(0, 0, sums_ref, sums_in.at[0])
+    first_sums.start()
+    core(0, 0, z, True).start()
+    core(1, 0, z, True).start()
+    mine.start()
+
+    def pass_cross(p, zz):
+        for axis in range(2):
+            cross_wait(p, axis, zz)
+            diagonal(p, 1 - axis, zz).start()
+            core(p, 1 + axis, zz).start()
+
+    def end_diagonal(p, zz):
+        for axis in range(2):
+            diagonal_wait(p, axis, zz)
+        core(p, 3, zz).start()
+
+    def arrive(zz, up):
+        line(0, zz, up).wait_recv()
+        onward(0, zz, up)
+        cross(0, 0, zz).start()
+        cross(0, 1, zz).start()
+        core(0, 0, zz).start()
+        line(1, zz, up).wait_recv()
+        onward(1, zz, up)
+        core(1, 0, zz).start()
+
+    def late(zz, up):
+        for k in range(2, 5):
+            line(k, zz, up).wait_recv()
+            onward(k, zz, up)
+            core(1, k - 1, zz).start()
+
+    def spread():
+        for k in range(2, 5):
+            pl.when(z < nz - 1)(lambda k=k: line(k, z, True).start())
+            pl.when(z > 0)(lambda k=k: line(k, z, False).start())
+
+    pass_cross(1, z)
+    sides(1, arrive)
+    pass_cross(0, z)
+    end_diagonal(1, z)
+    for d in range(2, nz):
+        sides(d, arrive)
+        if d == 2:
+            spread()
+    mine.wait()
+    width, chans = w_ref.shape[1], maps_ref.shape[2]
+    outs = s_ref.shape[2]
+    piece = wbuf.shape[1]
+    pieces = width // piece
+
+    def weights(k):
+        t, at = k // pieces, k % pieces * piece
+        return pltpu.make_async_copy(w_ref.at[t, pl.ds(at, piece), :], wbuf.at[k % 2], w_sem.at[k % 2])
+
+    def column(t, j):
+        return pltpu.make_async_copy(
+            g_ref.at[b, j, t], col.at[:, pl.ds(j * outs, outs)], col_sem.at[j]
+        )
+
+    def features_grad(t):
+        for k in range(t * pieces, (t + 1) * pieces):
+            if k + 1 < 2 * pieces:
+                weights(k + 1).start()
+            weights(k).wait()
+            if k == t * pieces:
+                for j in range(2 * nz):
+                    column(t, j).wait()
+            value = lax.dot_general(
+                wbuf[k % 2], col[...], (((1,), (1,)), ((), ())), preferred_element_type=F32
+            )
+            grads[pl.ds(k % pieces * piece, piece), :] = value.astype(BF16)
+        cells[t] = jnp.dot(order[...], grads[...], preferred_element_type=F32)
+
+    blocks = rows // 128
+
+    def maps_back(step, carry):
+        i = step // blocks
+        lanes = pl.ds(pl.multiple_of(step % blocks * 128, 128), 128)
+        unpool_row(chans, i, lanes, maps_in, maps_out, cells, above, mix_total, wide)
+        return carry
+
+    weights(0).start()
+    fill_order(order, chans, True)
+    spread_mix(mix_ref, wide)
+    above[...] = jnp.zeros_like(above)
+    mix_total[...] = jnp.zeros_like(mix_total)
+    first_sums.wait()
+    sums_mid[...] = sums_ref[...] + sums_in[0]
+    second_sums = small(0, 1, sums_mid, sums_in.at[1])
+    second_sums.start()
+    sides(1, lambda zz, up: pass_cross(0, zz))
+    for zz in range(nz):
+        for p in range(2):
+            core_wait(p, 0, zz)
+    for j in range(2 * nz):
+        column(0, j).start()
+    features_grad(0)
+    for j in range(2 * nz):
+        column(1, j).start()
+    sides(1, late)
+    features_grad(1)
+    end_diagonal(0, z)
+    load_maps.wait()
+    sides(2, lambda zz, up: pass_cross(0, zz))
+    lax.fori_loop(0, 3 * blocks, maps_back, 0)
+    sides(2, late)
+    sides(1, lambda zz, up: end_diagonal(0, zz))
+    lax.fori_loop(3 * blocks, 6 * blocks, maps_back, 0)
+    for t in range(2):
+        for x in range(13):
+            maps_out[t, 156 + x] = above[t, x].astype(BF16)
+    store_maps = pltpu.make_async_copy(maps_out, out_ref, out_sem)
+    store_maps.start()
+    for k in range(4):
+        mix_in[0, k] = jnp.broadcast_to(jnp.sum(mix_total[k], axis=1, keepdims=True), (chans, 128))
+    first_mix = small(1, 0, mix_in.at[0], mix_in.at[1])
+    first_mix.start()
+    for d in range(3, nz):
+        sides(d, lambda zz, up: pass_cross(0, zz))
+        sides(d, late)
+        sides(d - 1, lambda zz, up: end_diagonal(0, zz))
+    first_mix.wait()
+    mix_mid[...] = mix_in[0] + mix_in[1]
+    second_mix = small(1, 1, mix_mid, mix_in.at[2])
+    second_mix.start()
+    sides(nz - 1, lambda zz, up: end_diagonal(0, zz))
+    second_sums.wait()
+    total_ref[...] = sums_mid[...] + sums_in[1]
+    second_mix.wait()
+    mixed_ref[...] = mix_mid[...] + mix_in[2]
+    store_maps.wait()
+
+    for zz in range(nz):
+        for r in range(4):
+            for p in range(2):
+                if r > 0:
+                    core_wait(p, r, zz)
+                core(p, r, zz).wait_send()
+        for axis in range(2):
+            cross(0, axis, zz).wait_send()
+            diagonal(0, axis, zz).wait_send()
+        for k in range(5):
+            pl.when((z < nz - 1) & (z >= zz))(lambda k=k, zz=zz: line(k, zz, True).wait_send())
+            pl.when((z > 0) & (z <= zz))(lambda k=k, zz=zz: line(k, zz, False).wait_send())
+    for axis in range(2):
+        cross(1, axis, z).wait_send()
+        diagonal(1, axis, z).wait_send()
+
+
+def gather_all(mesh, grads, sums, weight, maps, mix):
+    groups, parts = mesh.shape["batch"], mesh.shape["mp"]
+    nz = parts // 2
+    _, rows, outs = grads.shape
+    _, cells, chans, _ = maps.shape
+    width = weight.shape[1]
+    piece = width // 3
+    cut = rows * 25 // 32
+    dma = pltpu.SemaphoreType.DMA
+    here = pl.BlockSpec(memory_space=pltpu.VMEM)
+    far = pl.BlockSpec(memory_space=pl.ANY)
+    return pl.pallas_call(
+        functools.partial(gather_kernel, nz, cut),
+        in_specs=[far, here, far, far, here],
+        out_specs=[far, far, here, here],
+        out_shape=[
+            jax.ShapeDtypeStruct((groups, parts) + grads.shape, BF16),
+            jax.ShapeDtypeStruct(maps.shape, BF16),
+            jax.ShapeDtypeStruct(sums.shape, F32),
+            jax.ShapeDtypeStruct((4, chans, 128), F32),
+        ],
+        scratch_shapes=[
+            dma,
+            dma((2, 5, nz)),
+            dma((5, nz)),
+            dma((2, nz + 1)),
+            dma((2, nz + 1)),
+            dma((2, nz + 1)),
+            dma((2, nz + 1)),
+            dma((2, 4, nz)),
+            dma((2, 4, nz)),
+            dma((2, 2)),
+            dma((2, 2)),
+            dma,
+            dma,
+            dma((2,)),
+            dma((parts,)),
+            pltpu.VMEM(maps.shape, BF16),
+            pltpu.VMEM(maps.shape, BF16),
+            pltpu.VMEM((2, piece, parts * outs), BF16),
+            pltpu.VMEM((rows, parts * outs), BF16),
+            pltpu.VMEM((width, rows), BF16),
+            pltpu.VMEM((2, width, rows), F32),
+            pltpu.VMEM((width, width), BF16),
+            pltpu.VMEM((2, 13, chans, rows), F32),
+            pltpu.VMEM((4, chans, 128), F32),
+            pltpu.VMEM((4, chans, 128), F32),
+            pltpu.VMEM((2,) + sums.shape, F32),
+            pltpu.VMEM(sums.shape, F32),
+            pltpu.VMEM((3, 4, chans, 128), F32),
+            pltpu.VMEM((4, chans, 128), F32),
+        ],
+        compiler_params=pltpu.CompilerParams(
+            collective_id=1, has_side_effects=True, vmem_limit_bytes=VMEM_LIMIT
+        ),
+        name="gather_all",
+    )(grads, sums, weight, maps, mix)
+
+
+def head_rows(hidden, cot, keep, mix, act_ref, grad_ref, here, lanes):
+    active, slope, pulled = [], [], []
+    for t in range(2):
+        value, rate = gelu_parts(hidden[t])
+        active.append(value)
+        slope.append(rate)
+        pulled.append(cot[t] * keep)
+    for i in range(2):
+        mixed = mix[2 * i] * active[0] + mix[2 * i + 1] * active[1]
+        act_ref[i, here, lanes] = (mixed * keep).astype(BF16)
+    terms = [pulled[i] * active[j] for i in range(2) for j in range(2)]
+    for j in range(2):
+        grad = (mix[j] * pulled[0] + mix[2 + j] * pulled[1]) * slope[j]
+        grad_ref[j, here, lanes] = grad.astype(BF16)
+        terms.append(grad)
+    return terms
+
+
+def forward_kernel(nz, live_ref, f_ref, ft_ref, w_ref, cot_ref, bias_ref, mix_ref,
+                   fta_ref, grad_ref, act_ref, sums_ref,
+                   wbuf, pb, sb, rb, inb, w_sem, core_send, core_recv, line_send, line_recv,
+                   cross_send, cross_recv, half_send, half_recv, keep_sem):
+    b, m, z, c, columns = neighbours()
+    sibling = m + 1 - 2 * c
+    rows, outs = f_ref.shape[1], pb.shape[3]
+    live = live_ref[b]
+
+    def features(r, t):
+        return fta_ref.at[t, :, pl.ds(pl.multiple_of(columns[r] * rows, rows), rows)]
+
+    near = jnp.where(z < nz // 2, 1, 0)
+
+    def weights(i, t, own):
+        zd = near * (nz - 1 - i) + (1 - near) * i
+        j = 2 * zd + (c if own else 1 - c)
+        lanes = pl.ds(pl.multiple_of(j * outs, outs), outs)
+        k = 2 * t + own
+        return pltpu.make_async_copy(w_ref.at[t, :, lanes], wbuf.at[k], w_sem.at[k])
+
+    for t in range(2):
+        for own in range(2):
+            weights(0, t, own).start()
+    mine = [pltpu.make_async_copy(ft_ref.at[t], features(0, t), keep_sem.at[t]) for t in range(2)]
+    greet(columns, m, z, c, nz)
+
+    def cross(axis, t):
+        return remote(ft_ref.at[t], features(0, t), cross_send.at[axis, t], cross_recv.at[axis, t],
+                      (columns[1 + axis], m))
+
+    def cross_wait(axis, t):
+        here = features(1 + axis, t)
+        remote(here, here, cross_send.at[axis, t], cross_recv.at[axis, t], (columns[1 + axis], m)).wait_recv()
+
+    def diagonal(axis):
+        here = features(2 - axis, 1 - axis)
+        return remote(here, here, half_send.at[axis], half_recv.at[axis], (columns[1 + axis], m))
+
+    def diagonal_wait(axis):
+        here = features(3, 1 - axis)
+        remote(here, here, half_send.at[axis], half_recv.at[axis], (columns[1 + axis], m)).wait_recv()
+
+    for k in range(2):
+        cross(0, k).start()
+        cross(1, 1 - k).start()
+    for copy in mine:
+        copy.start()
+
+    def swap(d, t):
+        return remote(sb.at[d, t], rb.at[d, t], core_send.at[d, t], core_recv.at[d, t], (b, sibling))
+
+    def hop(up, d, t):
+        return remote(rb.at[d, t], inb.at[up, d, t], line_send.at[d, t], line_recv.at[up, d, t],
+                      (b, m + 4 * up - 2))
+
+    step = 64
+
+    def relay(up, dm, t, first):
+        zm = up * z + (1 - up) * (nz - 1 - z)
+        d = up * dm + (1 - up) * (nz - 1 - dm)
+
+        def go():
+            swap(d, t).wait_recv()
+            if not first:
+                hop(up, d, t).wait_recv()
+
+            def add(k, carry):
+                here = pl.ds(pl.multiple_of(k * step, step), step)
+                value = pb[d, t, here, :] + rb[d, t, here, :].astype(F32)
+                if not first:
+                    value += inb[up, d, t, here, :].astype(F32)
+                rb[d, t, here, :] = value.astype(BF16)
+                return carry
+
+            lax.fori_loop(0, rows // step, add, 0)
+            hop(up, d, t).start()
+
+        pl.when((zm == 0 if first else zm > 0) & (zm < dm))(go)
+
+    def produce(i, carry):
+        zd = near * (nz - 1 - i) + (1 - near) * i
+        for t in range(2):
+            for own in range(2):
+                weights(i, t, own).wait()
+                part = jnp.dot(f_ref[t], wbuf[2 * t + own], preferred_element_type=F32)
+                if own:
+                    pb[zd, t] = part
+                else:
+                    sb[zd, t] = part.astype(BF16)
+                    swap(zd, t).start()
+                pl.when(i < nz - 1)(lambda t=t, own=own: weights(i + 1, t, own).start())
+            relay(near, nz - 1 - i, t, True)
+        return carry
+
+    lax.fori_loop(0, nz, produce, 0)
+    for dm in range(nz - 1, 0, -1):
+        for t in range(2):
+            relay(near, dm, t, False)
+            relay(1 - near, dm, t, False)
+        if dm == nz - 1:
+            for axis in range(2):
+                cross_wait(1 - axis, 1 - axis)
+                diagonal(axis).start()
+
+    for t in range(2):
+        swap(z, t).wait_recv()
+        pl.when(z > 0)(lambda t=t: hop(1, z, t).wait_recv())
+        pl.when(z < nz - 1)(lambda t=t: hop(0, z, t).wait_recv())
+
+        def gather(k, carry, t=t):
+            here = pl.ds(pl.multiple_of(k * step, step), step)
+            pb[z, t, here, :] += rb[z, t, here, :].astype(F32)
+            for up in range(2):
+                inside = z > 0 if up else z < nz - 1
+
+                @pl.when(inside)
+                def _(up=up):
+                    pb[z, t, here, :] += inb[up, z, t, here, :].astype(F32)
+
+            return carry
+
+        lax.fori_loop(0, rows // step, gather, 0)
+    tile, high = 256, 16
+    for lane in range(outs // tile):
+        lanes = pl.ds(lane * tile, tile)
+        bias = [bias_ref[pl.ds(t, 1), lanes] for t in range(2)]
+        mix = [mix_ref[k // 2, pl.ds(k % 2, 1), lanes] for k in range(4)]
+
+        def block(k, totals, lanes=lanes, bias=bias, mix=mix):
+            here = pl.ds(pl.multiple_of(k * high, high), high)
+            hidden = [pb[z, t, here, lanes] + bias[t] for t in range(2)]
+            cot = [cot_ref[t, here, lanes].astype(F32) for t in range(2)]
+            place = k * high + lax.broadcasted_iota(jnp.int32, (high, tile), 0)
+            keep = jnp.where(place < live, 1.0, 0.0)
+            terms = head_rows(hidden, cot, keep, mix, act_ref, grad_ref, here, lanes)
+            return tuple(a + v[:8] + v[8:] for a, v in zip(totals, terms))
+
+        zero = jnp.zeros((8, tile), F32)
+        totals = lax.fori_loop(0, rows // high, block, (zero,) * 6)
+        for k in range(6):
+            sums_ref[k, :, lanes] = jnp.sum(totals[k], axis=0, keepdims=True)
+
+    for copy in mine:
+        copy.wait()
+    for axis in range(2):
+        cross_wait(axis, 1 - axis)
+        diagonal_wait(axis)
+        diagonal(axis).wait_send()
+        for t in range(2):
+            cross(axis, t).wait_send()
+    for d in range(nz):
+        for t in range(2):
+            swap(d, t).wait_send()
+            pl.when(z < d)(lambda d=d, t=t: hop(1, d, t).wait_send())
+            pl.when(z > d)(lambda d=d, t=t: hop(0, d, t).wait_send())
+
+
+def forward_all(mesh, live, f, ft, weight, cot, bias, mix):
+    groups, parts = mesh.shape["batch"], mesh.shape["mp"]
+    nz = parts // 2
+    _, rows, width = f.shape
+    outs = weight.shape[2] // parts
+    dma = pltpu.SemaphoreType.DMA
+    here = pl.BlockSpec(memory_space=pltpu.VMEM)
+    far = pl.BlockSpec(memory_space=pl.ANY)
+    return pl.pallas_call(
+        functools.partial(forward_kernel, nz),
+        in_specs=[pl.BlockSpec(memory_space=pltpu.SMEM), here, far, far, here, here, here],
+        out_specs=[far, here, here, here],
+        out_shape=[
+            jax.ShapeDtypeStruct((2, width, groups * rows), BF16),
+            jax.ShapeDtypeStruct((2, rows, outs), BF16),
+            jax.ShapeDtypeStruct((2, rows, outs), BF16),
+            jax.ShapeDtypeStruct((6, 1, outs), F32),
+        ],
+        scratch_shapes=[
+            pltpu.VMEM((4, width, outs), BF16),
+            pltpu.VMEM((nz, 2, rows, outs), F32),
+            pltpu.VMEM((nz, 2, rows, outs), BF16),
+            pltpu.VMEM((nz, 2, rows, outs), BF16),
+            pltpu.VMEM((2, nz, 2, rows, outs), BF16),
+            dma((4,)),
+            dma((nz, 2)),
+            dma((nz, 2)),
+            dma((nz, 2)),
+            dma((2, nz, 2)),
+            dma((2, 2)),
+            dma((2, 2)),
+            dma((2,)),
+            dma((2,)),
+            dma((2,)),
+        ],
+        compiler_params=pltpu.CompilerParams(
+            collective_id=0, has_side_effects=True, vmem_limit_bytes=VMEM_LIMIT
+        ),
+        name="forward_all",
+    )(live, f, ft, weight, cot, bias, mix)
+
+
+def turn_mix(wide):
+    chans = wide.shape[0]
+    rows = lax.broadcasted_iota(jnp.int32, (chans, chans), 0)
+    cols = lax.broadcasted_iota(jnp.int32, (chans, chans), 1)
+    return jnp.sum(jnp.where(rows == cols, wide[:, :chans], 0.0), axis=0, keepdims=True)
+
+
+def update_kernel(ft_ref, s_ref, m_ref, w_ref, sums_ref, mixed_ref, bias_ref, bias_m_ref, in_ref, in_m_ref,
+                  out_ref, out_m_ref, grad_ref, next_ref, moment_ref, bias_g, bias_n, bias_mn,
+                  in_g, in_n, in_mn, out_g, out_n, out_mn):
+    @pl.when((pl.program_id(0) == 0) & (pl.program_id(1) == 0))
+    def _():
+        def step(grad, value, moment, rate, at, grad_to, next_to, moment_to):
+            after = MOMENTUM * moment[at] + grad
+            grad_to[at] = grad
+            moment_to[at] = after
+            next_to[at] = value[at] - rate * after
+
+        for i in range(2):
+            at = (pl.ds(i, 1), slice(None))
+            step(sums_ref[4 + i], bias_ref, bias_m_ref, DENSE_RATE, at, bias_g, bias_n, bias_mn)
+            for j in range(2):
+                at = (i, pl.ds(j, 1), slice(None))
+                step(sums_ref[2 * i + j], out_ref, out_m_ref, STITCH_RATE, at, out_g, out_n, out_mn)
+                step(turn_mix(mixed_ref[2 * i + j]), in_ref, in_m_ref, STITCH_RATE, at, in_g, in_n, in_mn)
+
+    groups, _, _, rows, tile = s_ref.shape
+    grad = jnp.dot(ft_ref[0], s_ref[...].reshape(groups * rows, tile), preferred_element_type=F32)
+    grad_ref[0] = grad
+    moment = MOMENTUM * m_ref[0] + grad
+    moment_ref[0] = moment
+    next_ref[0] = (w_ref[0].astype(F32) - DENSE_RATE * moment).astype(BF16)
+
+
+def weight_update(ft_all, gathered, moment, weight, sums, mixed, bias, bias_m, mix_in, mix_in_m, mix_out, mix_out_m):
+    groups, parts, _, rows, outs = gathered.shape
+    width = weight.shape[1]
+    tile = 512 if outs % 512 == 0 else 256
+    split = outs // tile
+    wide = pl.BlockSpec((1, width, tile), lambda t, j: (t, 0, j))
+    smalls = [bias, mix_in, mix_out]
+    return pl.pallas_call(
+        update_kernel,
+        grid=(2, parts * split),
+        in_specs=[
+            pl.BlockSpec((1, width, groups * rows), lambda t, j: (t, 0, 0)),
+            pl.BlockSpec((groups, 1, 1, rows, tile), lambda t, j: (0, j // split, t, 0, j % split)),
+            wide,
+            wide,
+            full(sums.shape),
+            full(mixed.shape),
+        ]
+        + [full(a.shape) for a in smalls for _ in range(2)],
+        out_specs=[wide, wide, wide] + [full(a.shape) for a in smalls for _ in range(3)],
+        out_shape=[
+            jax.ShapeDtypeStruct(moment.shape, F32),
+            jax.ShapeDtypeStruct(moment.shape, BF16),
+            jax.ShapeDtypeStruct(moment.shape, F32),
+        ]
+        + [jax.ShapeDtypeStruct(a.shape, F32) for a in smalls for _ in range(3)],
+        compiler_params=params(),
+        name="weight_update",
+    )(ft_all, gathered, moment, weight, sums, mixed, bias, bias_m, mix_in, mix_in_m, mix_out, mix_out_m)
+
+
+def fast_shards(
+    mesh,
+    input_maps,
+    dense_weight,
+    dense_bias,
+    stitch_in,
+    stitch_out,
+    weight_moment,
+    bias_moment,
+    stitch_in_moment,
+    stitch_out_moment,
+    cotangent,
+    live_rows,
+):
+    maps = jnp.transpose(input_maps, (1, 3, 2, 0))
+    cot = jnp.transpose(cotangent, (1, 0, 2))
+    ft, f = pool_forward(maps, stitch_in)
+    ft_all, grads, acts, sums = forward_all(
+        mesh, live_rows, f, ft, dense_weight, cot, dense_bias, stitch_out
+    )
+    activations = jnp.transpose(acts, (1, 0, 2))
+    gathered, maps_out, sums, mixed = gather_all(mesh, grads, sums, dense_weight, maps, stitch_in)
+    maps_grad = jnp.transpose(maps_out, (3, 0, 2, 1))
+    (
+        weight_grad,
+        weight_next,
+        weight_moment_next,
+        bias_grad,
+        bias_next,
+        bias_moment_next,
+        stitch_in_grad,
+        stitch_in_next,
+        stitch_in_moment_next,
+        stitch_out_grad,
+        stitch_out_next,
+        stitch_out_moment_next,
+    ) = weight_update(
+        ft_all,
+        gathered,
+        weight_moment,
+        dense_weight,
+        sums,
+        mixed,
+        dense_bias,
+        bias_moment,
+        stitch_in,
+        stitch_in_moment,
+        stitch_out,
+        stitch_out_moment,
+    )
+    return (
+        activations,
+        maps_grad,
+        weight_grad,
+        bias_grad,
+        stitch_in_grad,
+        stitch_out_grad,
+        weight_next,
+        bias_next,
+        stitch_in_next,
+        stitch_out_next,
+        weight_moment_next,
+        bias_moment_next,
+        stitch_in_moment_next,
+        stitch_out_moment_next,
+    )
+
+
+def choose(mesh, *args):
+    rows, _, chans, _ = args[0].shape
+    outs = args[2].shape[1]
+    shape = mesh.shape["batch"] == 4 and mesh.shape["mp"] == 8
+    if shape and rows % 512 == 0 and outs % 256 == 0 and chans == 32:
+        return fast_shards(mesh, *args)
+    return shards(*args)
+
+
 def solution(mesh):
     in_specs = (
         P("batch", None, "mp", None),
@@ -170,4 +990,5 @@
         P(None, None, "mp"),
         P(None, None, "mp"),
     )
-    return jax.shard_map(shards, mesh=mesh, in_specs=in_specs, out_specs=out_specs, check_vma=False)
+    body = functools.partial(choose, mesh)
+    return jax.shard_map(body, mesh=mesh, in_specs=in_specs, out_specs=out_specs, check_vma=False)

time: 1070 us -> 320 us (0.30); the launches traced: 1060 us -> 320 us
  waiting for transfers between devices: 764 us -> 0 us
  Pallas kernels: 0 us -> 303 us
  matrix products: 128 us -> 0 us
  local copies, waits for them, and re-layouts: 75.5 us -> 16.1 us
  other arithmetic: 57.2 us -> 0 us
  blocking collectives: 16.5 us -> 0 us
  between operations: 14.5 us -> 0.67 us
    psum x1 -> x0, waiting for transfers between devices: 517 us -> none  [shards(): lax.psum((weight_grad, bias_grad, stitch_in_grad, stitch_out_grad), 'batch')]
    pallas_call x0 -> x4, Pallas kernels: none -> 303 us  [the longest x1 123 us: gather_all(): pl.pallas_call(functools.partial(gather_kernel, nz, cut), in_specs=[far,...]
    reduce_scatter x1 -> x0, waiting for transfers between devices: 167 us -> none  [rows_layer(): summed = lax.psum_scatter(terms, 'mp', scatter_dimension=2, tiled=True)]
    dot_general x7 -> x0, matrix products: 128 us -> none  [the longest x1 26.9 us: shards(): jnp.einsum('nicq,njcq->ijc', stitched_grad, pooled, precision=lax.Precisi...]
    all_gather x1 -> x0, waiting for transfers between devices: 80.5 us -> none  [rows_layer(): piece = lax.all_gather(summed_grad, 'mp', axis=2, tiled=True)]
    convert_element_type x3 -> x0, other arithmetic: 50.8 us -> none  [the longest x1 49.8 us: shards(): (dense_weight.astype(jnp.float32) - DENSE_RATE * weight_moment_next).asty...]
    unnamed x32 -> x3, local copies, waits for them, and re-layouts: 46.7 us -> 16.1 us
    psum x1 -> x0, blocking collectives: 16.5 us -> none  [shards(): lax.psum((weight_grad, bias_grad, stitch_in_grad, stitch_out_grad), 'batch')]
  transfers between devices with their start and end apart: 3 -> 0, of which waited for: 3 -> 0; matrix products, arithmetic and copies ran while one was open for 11% -> 0% of each run, Pallas kernels for 0% -> 0%
where the time goes in v2:
time: 320 us
  Pallas kernels  303 us (95%)
  local copies, waits for them, and re-layouts  16.1 us (5%)
    pallas_call x1, Pallas kernels, gather_all(): pl.pallas_call(functools.partial(gather_kernel, nz, cut), in_specs=[far,...  123 us
    pallas_call x1, Pallas kernels, forward_all(): pl.pallas_call(functools.partial(forward_kernel, nz), in_specs=[pl.BlockS...  85 us
    pallas_call x1, Pallas kernels, weight_update(): pl.pallas_call(update_kernel, grid=(2, parts * split), in_specs=[pl.Block...  82.2 us
    unnamed x3, local copies, waits for them, and re-layouts  16.1 us
    pallas_call x1, Pallas kernels, pool_forward(): pl.pallas_call(functools.partial(pool_kernel, chans), grid=(rows // tile,...  13 us

profile of v2, /device:TPU:0, one launch (start us, length us, event | category | flops | bytes accessed | tf_op | source)
XLA Modules:
  0.0 319.8 jit_solution(3527094386185160112)
XLA Ops:
  0.6 2.4 copy.28
  3.0 13.0 %pool_forward.1 = (bf16[2,1152,512]{2,1,0:T(8,128)(2,1)}, bf16[2,512,1152]{2,1,0:T(8,128)(2,1)}) custom-call(bf16[2,169,32,512]{3,2,1,0:T(8,128)(2,1)} %bitcast.6, f32[2,2,32]{2,1,0:T(2,128)} %in_ref.1), custom_call_target="tpu_custom_call" | custom-call | tf_op jit(solution)/shard_map/pool_forward/pallas_call | solution.py:220
  16.0 85.0 %forward_all.1 = (bf16[2,1152,2048]{2,1,0:T(8,128)(2,1)}, bf16[2,512,512]{2,1,0:T(8,128)(2,1)}, bf16[2,512,512]{2,1,0:T(8,128)(2,1)}, f32[6,1,512]{2,1,0:T(1,128)}) custom-call(s32[4]{0:T(128)} %live_ref.1, bf16[2,512,1152]{2,1,0:T(8,128)(2,1)} %get-tuple-element.36.f_ref, bf16[2,1152,512]{2,1,0:T(8,128)(2,1)} %get-tuple-element.37.ft_ref, ...), custom_call_target="tpu_custom_call" | custom-call | tf_op jit(solution)/shard_map/forward_all/pallas_call | solution.py:787
  101.0 3.3 %copy.26 = bf16[512,2,512]{2,1,0:T(2,128)(2,1)} copy(bf16[512,2,512]{2,0,1:T(8,128)(2,1)} %bitcast.10) | data formatting | bytes 2097152
  104.3 122.8 %gather_all.1 = (bf16[4,8,2,512,512]{4,3,2,1,0:T(8,128)(2,1)}, bf16[2,169,32,512]{3,2,1,0:T(8,128)(2,1)}, f32[6,1,512]{2,1,0:T(1,128)}, f32[4,32,128]{2,1,0:T(8,128)}) custom-call(bf16[2,512,512]{2,1,0:T(8,128)(2,1)} %get-tuple-element.39.s_ref, f32[6,1,512]{2,1,0:T(1,128)} %get-tuple-element.40.sums_ref, bf16[2,1152,4096]{2,1,0:T(8,128)(2,1)} %w_ref.5, ...), custom_call_target="tpu_custom_call" | custom-call | tf_op jit(solution)/shard_map/gather_all/pallas_call | solution.py:555
  227.1 82.2 %weight_update.1 = (f32[2,1152,4096]{2,1,0:T(8,128)}, bf16[2,1152,4096]{2,1,0:T(8,128)(2,1)}, f32[2,1152,4096]{2,1,0:T(8,128)}, f32[2,512]{1,0:T(2,128)}, f32[2,...) custom-call(bf16[2,1152,2048]{2,1,0:T(8,128)(2,1)} %get-tuple-elemen, ...), custom_call_target="tpu_custom_call" | custom-call | tf_op jit(solution)/shard_map/weight_update/pallas_call | solution.py:862
  309.4 10.4 %copy.30 = bf16[512,2,32,169]{0,2,3,1:T(8,128)(2,1)} copy(bf16[512,2,32,169]{0,2,3,1:T(8,128)(2,1)} %bitcast.8) | data formatting | bytes 22151168

commit v3 on v2

--- a/solution.py
+++ b/solution.py
@@ -186,62 +186,6 @@
     return [s * (1.0 / 9.0) for s in sums]
 
 
-def pool_kernel(chans, maps_ref, mix_ref, ft_ref, f_ref, order, cells, wide):
-    @pl.when(pl.program_id(0) == 0)
-    def _():
-        fill_order(order, chans, False)
-        spread_mix(mix_ref, wide)
-
-    tile = cells.shape[2]
-
-    def row(step, carry):
-        i = step // (tile // 128)
-        lanes = pl.ds(pl.multiple_of(step % (tile // 128) * 128, 128), 128)
-        first = pooled_row(maps_ref, 0, i, lanes)
-        second = pooled_row(maps_ref, 1, i, lanes)
-        for t in range(2):
-            for j in range(6):
-                value = wide[2 * t] * first[j] + wide[2 * t + 1] * second[j]
-                start = pl.multiple_of((6 * i + j) * chans, chans)
-                cells[t, pl.ds(start, chans), lanes] = value.astype(BF16)
-        return carry
-
-    lax.fori_loop(0, 6 * (tile // 128), row, 0)
-    for t in range(2):
-        moved = jnp.dot(order[...], cells[t], preferred_element_type=F32)
-        ft_ref[t] = moved.astype(BF16)
-        f_ref[t] = moved.T.astype(BF16)
-
-
-def pool_forward(maps, mix):
-    _, cells, chans, rows = maps.shape
-    width = chans * 36
-    tile = 256
-    return pl.pallas_call(
-        functools.partial(pool_kernel, chans),
-        grid=(rows // tile,),
-        in_specs=[
-            pl.BlockSpec((2, cells, chans, tile), lambda n: (0, 0, 0, n)),
-            full((2, 2, chans)),
-        ],
-        out_specs=[
-            pl.BlockSpec((2, width, tile), lambda n: (0, 0, n)),
-            pl.BlockSpec((2, tile, width), lambda n: (0, n, 0)),
-        ],
-        out_shape=[
-            jax.ShapeDtypeStruct((2, width, rows), BF16),
-            jax.ShapeDtypeStruct((2, rows, width), BF16),
-        ],
-        scratch_shapes=[
-            pltpu.VMEM((width, width), BF16),
-            pltpu.VMEM((2, width, tile), BF16),
-            pltpu.VMEM((4, chans, 128), F32),
-        ],
-        compiler_params=params(),
-        name="pool_forward",
-    )(maps, mix)
-
-
 def gelu_parts(v):
     root = 0.7978845608028654
     square = v * v
@@ -307,11 +251,11 @@
             above[t, x, :, lanes] = value
 
 
-def gather_kernel(nz, cut, s_ref, sums_ref, w_ref, maps_ref, mix_ref,
-                  g_ref, out_ref, total_ref, mixed_ref,
+def gather_kernel(nz, cut, s_ref, acts_ref, sums_ref, w_ref, maps_ref, mix_ref,
+                  g_ref, acts_to, out_ref, total_ref, mixed_ref,
                   keep_sem, line_send, line_recv, cross_send, cross_recv,
                   half_send, half_recv, core_send, core_recv, small_send, small_recv,
-                  maps_sem, out_sem, w_sem, col_sem,
+                  maps_sem, out_sem, w_sem, col_sem, acts_sem, acts_in, acts_out,
                   maps_in, maps_out, wbuf, col, grads, cells, order, above, mix_total, wide,
                   sums_in, sums_mid, mix_in, mix_mid):
     b, m, z, c, columns = neighbours()
@@ -319,6 +263,8 @@
     spans = (pl.ds(0, cut), pl.ds(cut, rows - cut))
     sibling = m + 1 - 2 * c
     load_maps = pltpu.make_async_copy(maps_ref, maps_in, maps_sem)
+    load_acts = pltpu.make_async_copy(acts_ref, acts_in, acts_sem.at[0])
+    load_acts.start()
     load_maps.start()
     greet(columns, m, z, c, nz)
 
@@ -428,7 +374,17 @@
             pl.when(z < nz - 1)(lambda k=k: line(k, z, True).start())
             pl.when(z > 0)(lambda k=k: line(k, z, False).start())
 
+    def join_towers(k, carry):
+        here = pl.ds(pl.multiple_of(k * 16, 16), 16)
+        both = jnp.stack([acts_in[t, here, :].astype(F32) for t in range(2)], axis=1)
+        acts_out[here, :, :] = both.astype(BF16)
+        return carry
+
     pass_cross(1, z)
+    load_acts.wait()
+    lax.fori_loop(0, rows // 16, join_towers, 0)
+    store_acts = pltpu.make_async_copy(acts_out, acts_to, acts_sem.at[1])
+    store_acts.start()
     sides(1, arrive)
     pass_cross(0, z)
     end_diagonal(1, z)
@@ -495,10 +451,12 @@
     features_grad(1)
     end_diagonal(0, z)
     load_maps.wait()
-    sides(2, lambda zz, up: pass_cross(0, zz))
+    outer = (z == 0) | (z == nz - 1)
+    inner = (z > 0) & (z < nz - 1)
+    pl.when(inner)(lambda: sides(2, late))
+    pl.when(outer)(lambda: sides(2, lambda zz, up: pass_cross(0, zz)))
     lax.fori_loop(0, 3 * blocks, maps_back, 0)
-    sides(2, late)
-    sides(1, lambda zz, up: end_diagonal(0, zz))
+    pl.when(outer)(lambda: sides(2, late))
     lax.fori_loop(3 * blocks, 6 * blocks, maps_back, 0)
     for t in range(2):
         for x in range(13):
@@ -509,20 +467,22 @@
         mix_in[0, k] = jnp.broadcast_to(jnp.sum(mix_total[k], axis=1, keepdims=True), (chans, 128))
     first_mix = small(1, 0, mix_in.at[0], mix_in.at[1])
     first_mix.start()
-    for d in range(3, nz):
-        sides(d, lambda zz, up: pass_cross(0, zz))
-        sides(d, late)
-        sides(d - 1, lambda zz, up: end_diagonal(0, zz))
+    pl.when(inner)(lambda: sides(2, lambda zz, up: pass_cross(0, zz)))
+    sides(1, lambda zz, up: end_diagonal(0, zz))
+    sides(3, lambda zz, up: pass_cross(0, zz))
     first_mix.wait()
     mix_mid[...] = mix_in[0] + mix_in[1]
     second_mix = small(1, 1, mix_mid, mix_in.at[2])
     second_mix.start()
-    sides(nz - 1, lambda zz, up: end_diagonal(0, zz))
+    sides(2, lambda zz, up: end_diagonal(0, zz))
+    sides(3, late)
+    sides(3, lambda zz, up: end_diagonal(0, zz))
     second_sums.wait()
     total_ref[...] = sums_mid[...] + sums_in[1]
     second_mix.wait()
     mixed_ref[...] = mix_mid[...] + mix_in[2]
     store_maps.wait()
+    store_acts.wait()
 
     for zz in range(nz):
         for r in range(4):
@@ -541,7 +501,7 @@
         diagonal(1, axis, z).wait_send()
 
 
-def gather_all(mesh, grads, sums, weight, maps, mix):
+def gather_all(mesh, grads, acts, sums, weight, maps, mix):
     groups, parts = mesh.shape["batch"], mesh.shape["mp"]
     nz = parts // 2
     _, rows, outs = grads.shape
@@ -554,10 +514,11 @@
     far = pl.BlockSpec(memory_space=pl.ANY)
     return pl.pallas_call(
         functools.partial(gather_kernel, nz, cut),
-        in_specs=[far, here, far, far, here],
-        out_specs=[far, far, here, here],
+        in_specs=[far, far, here, far, far, here],
+        out_specs=[far, far, far, here, here],
         out_shape=[
             jax.ShapeDtypeStruct((groups, parts) + grads.shape, BF16),
+            jax.ShapeDtypeStruct((rows, 2, outs), BF16),
             jax.ShapeDtypeStruct(maps.shape, BF16),
             jax.ShapeDtypeStruct(sums.shape, F32),
             jax.ShapeDtypeStruct((4, chans, 128), F32),
@@ -578,6 +539,9 @@
             dma,
             dma((2,)),
             dma((parts,)),
+            dma((2,)),
+            pltpu.VMEM((2, rows, outs), BF16),
+            pltpu.VMEM((rows, 2, outs), BF16),
             pltpu.VMEM(maps.shape, BF16),
             pltpu.VMEM(maps.shape, BF16),
             pltpu.VMEM((2, piece, parts * outs), BF16),
@@ -597,7 +561,7 @@
             collective_id=1, has_side_effects=True, vmem_limit_bytes=VMEM_LIMIT
         ),
         name="gather_all",
-    )(grads, sums, weight, maps, mix)
+    )(grads, acts, sums, weight, maps, mix)
 
 
 def head_rows(hidden, cot, keep, mix, act_ref, grad_ref, here, lanes):
@@ -618,17 +582,26 @@
     return terms
 
 
-def forward_kernel(nz, live_ref, f_ref, ft_ref, w_ref, cot_ref, bias_ref, mix_ref,
+def forward_kernel(nz, live_ref, maps_ref, w_ref, cot_raw, bias_ref, mix_ref, mix_in_ref,
                    fta_ref, grad_ref, act_ref, sums_ref,
-                   wbuf, pb, sb, rb, inb, w_sem, core_send, core_recv, line_send, line_recv,
+                   maps_in, cells, order, wide, f_ref, ft_ref, cot_in, cot_ref, wbuf, pb, sb, rb, inb,
+                   maps_sem, cot_sem, w_sem, core_send, core_recv, line_send, line_recv,
                    cross_send, cross_recv, half_send, half_recv, keep_sem):
     b, m, z, c, columns = neighbours()
     sibling = m + 1 - 2 * c
     rows, outs = f_ref.shape[1], pb.shape[3]
     live = live_ref[b]
 
-    def features(r, t):
-        return fta_ref.at[t, :, pl.ds(pl.multiple_of(columns[r] * rows, rows), rows)]
+    chans, span = maps_in.shape[2], cells.shape[2]
+    halves = rows // span
+
+    def features(r, t, h):
+        start = pl.multiple_of(columns[r] * rows + h * span, span)
+        return fta_ref.at[t, :, pl.ds(start, span)]
+
+    def load_maps(h):
+        lanes = pl.ds(h * span, span)
+        return pltpu.make_async_copy(maps_ref.at[:, :, :, lanes], maps_in.at[:, :, :, lanes], maps_sem.at[h])
 
     near = jnp.where(z < nz // 2, 1, 0)
 
@@ -639,33 +612,66 @@
         k = 2 * t + own
         return pltpu.make_async_copy(w_ref.at[t, :, lanes], wbuf.at[k], w_sem.at[k])
 
+    for h in range(halves):
+        load_maps(h).start()
     for t in range(2):
         for own in range(2):
             weights(0, t, own).start()
-    mine = [pltpu.make_async_copy(ft_ref.at[t], features(0, t), keep_sem.at[t]) for t in range(2)]
+    load_cot = pltpu.make_async_copy(cot_raw, cot_in, cot_sem)
+    load_cot.start()
+    fill_order(order, chans, False)
+    spread_mix(mix_in_ref, wide)
     greet(columns, m, z, c, nz)
 
-    def cross(axis, t):
-        return remote(ft_ref.at[t], features(0, t), cross_send.at[axis, t], cross_recv.at[axis, t],
-                      (columns[1 + axis], m))
-
-    def cross_wait(axis, t):
-        here = features(1 + axis, t)
-        remote(here, here, cross_send.at[axis, t], cross_recv.at[axis, t], (columns[1 + axis], m)).wait_recv()
-
-    def diagonal(axis):
-        here = features(2 - axis, 1 - axis)
-        return remote(here, here, half_send.at[axis], half_recv.at[axis], (columns[1 + axis], m))
-
-    def diagonal_wait(axis):
-        here = features(3, 1 - axis)
-        remote(here, here, half_send.at[axis], half_recv.at[axis], (columns[1 + axis], m)).wait_recv()
-
-    for k in range(2):
-        cross(0, k).start()
-        cross(1, 1 - k).start()
-    for copy in mine:
-        copy.start()
+    def mine(t, h):
+        return pltpu.make_async_copy(ft_ref.at[t, :, pl.ds(h * span, span)], features(0, t, h), keep_sem.at[t, h])
+
+    def cross(axis, t, h):
+        return remote(ft_ref.at[t, :, pl.ds(h * span, span)], features(0, t, h), cross_send.at[axis, t, h],
+                      cross_recv.at[axis, t, h], (columns[1 + axis], m))
+
+    def cross_wait(axis, t, h):
+        here = features(1 + axis, t, h)
+        remote(here, here, cross_send.at[axis, t, h], cross_recv.at[axis, t, h], (columns[1 + axis], m)).wait_recv()
+
+    def diagonal(axis, h):
+        here = features(2 - axis, 1 - axis, h)
+        return remote(here, here, half_send.at[axis, h], half_recv.at[axis, h], (columns[1 + axis], m))
+
+    def diagonal_wait(axis, h):
+        here = features(3, 1 - axis, h)
+        remote(here, here, half_send.at[axis, h], half_recv.at[axis, h], (columns[1 + axis], m)).wait_recv()
+
+    def onward(h):
+        for axis in range(2):
+            cross_wait(1 - axis, 1 - axis, h)
+            diagonal(axis, h).start()
+
+    narrow = span // 128
+    for h in range(halves):
+
+        def pool_row(step, carry, h=h):
+            i = step // narrow
+            at = pl.multiple_of(step % narrow * 128, 128)
+            lanes = pl.ds(pl.multiple_of(h * span + at, 128), 128)
+            first = pooled_row(maps_in, 0, i, lanes)
+            second = pooled_row(maps_in, 1, i, lanes)
+            for t in range(2):
+                for j in range(6):
+                    value = wide[2 * t] * first[j] + wide[2 * t + 1] * second[j]
+                    start = pl.multiple_of((6 * i + j) * chans, chans)
+                    cells[t, pl.ds(start, chans), pl.ds(at, 128)] = value.astype(BF16)
+            return carry
+
+        load_maps(h).wait()
+        lax.fori_loop(0, 6 * narrow, pool_row, 0)
+        for t in range(2):
+            moved = jnp.dot(order[...], cells[t], preferred_element_type=F32).astype(BF16)
+            ft_ref[t, :, pl.ds(h * span, span)] = moved
+            f_ref[t, pl.ds(h * span, span), :] = moved.T
+        for k in range(2):
+            cross(0, k, h).start()
+            cross(1, 1 - k, h).start()
 
     def swap(d, t):
         return remote(sb.at[d, t], rb.at[d, t], core_send.at[d, t], core_recv.at[d, t], (b, sibling))
@@ -714,14 +720,27 @@
         return carry
 
     lax.fori_loop(0, nz, produce, 0)
+    onward(0)
+    for t in range(2):
+        for h in range(halves):
+            mine(t, h).start()
+    load_cot.wait()
+
+    def part_towers(k, carry):
+        here = pl.ds(pl.multiple_of(k * 16, 16), 16)
+        both = cot_in[here, :, :].astype(F32)
+        for t in range(2):
+            cot_ref[t, here, :] = both[:, t, :].astype(BF16)
+        return carry
+
+    lax.fori_loop(0, rows // 16, part_towers, 0)
     for dm in range(nz - 1, 0, -1):
         for t in range(2):
             relay(near, dm, t, False)
             relay(1 - near, dm, t, False)
         if dm == nz - 1:
-            for axis in range(2):
-                cross_wait(1 - axis, 1 - axis)
-                diagonal(axis).start()
+            for h in range(1, halves):
+                onward(h)
 
     for t in range(2):
         swap(z, t).wait_recv()
@@ -761,14 +780,15 @@
         for k in range(6):
             sums_ref[k, :, lanes] = jnp.sum(totals[k], axis=0, keepdims=True)
 
-    for copy in mine:
-        copy.wait()
-    for axis in range(2):
-        cross_wait(axis, 1 - axis)
-        diagonal_wait(axis)
-        diagonal(axis).wait_send()
+    for h in range(halves):
+        for axis in range(2):
+            cross_wait(axis, 1 - axis, h)
+            diagonal_wait(axis, h)
+            diagonal(axis, h).wait_send()
+            for t in range(2):
+                cross(axis, t, h).wait_send()
         for t in range(2):
-            cross(axis, t).wait_send()
+            mine(t, h).wait()
     for d in range(nz):
         for t in range(2):
             swap(d, t).wait_send()
@@ -776,17 +796,20 @@
             pl.when(z > d)(lambda d=d, t=t: hop(0, d, t).wait_send())
 
 
-def forward_all(mesh, live, f, ft, weight, cot, bias, mix):
+def forward_all(mesh, live, maps, weight, cot, bias, mix, mix_in):
     groups, parts = mesh.shape["batch"], mesh.shape["mp"]
     nz = parts // 2
-    _, rows, width = f.shape
+    chans, rows = maps.shape[2:]
+    width = weight.shape[1]
     outs = weight.shape[2] // parts
+    span = 256
+    halves = rows // span
     dma = pltpu.SemaphoreType.DMA
     here = pl.BlockSpec(memory_space=pltpu.VMEM)
     far = pl.BlockSpec(memory_space=pl.ANY)
     return pl.pallas_call(
         functools.partial(forward_kernel, nz),
-        in_specs=[pl.BlockSpec(memory_space=pltpu.SMEM), here, far, far, here, here, here],
+        in_specs=[pl.BlockSpec(memory_space=pltpu.SMEM), far, far, far, here, here, here],
         out_specs=[far, here, here, here],
         out_shape=[
             jax.ShapeDtypeStruct((2, width, groups * rows), BF16),
@@ -795,27 +818,37 @@
             jax.ShapeDtypeStruct((6, 1, outs), F32),
         ],
         scratch_shapes=[
+            pltpu.VMEM(maps.shape, BF16),
+            pltpu.VMEM((2, width, span), BF16),
+            pltpu.VMEM((width, width), BF16),
+            pltpu.VMEM((4, chans, 128), F32),
+            pltpu.VMEM((2, rows, width), BF16),
+            pltpu.VMEM((2, width, rows), BF16),
+            pltpu.VMEM(cot.shape, BF16),
+            pltpu.VMEM((2, rows, outs), BF16),
             pltpu.VMEM((4, width, outs), BF16),
             pltpu.VMEM((nz, 2, rows, outs), F32),
             pltpu.VMEM((nz, 2, rows, outs), BF16),
             pltpu.VMEM((nz, 2, rows, outs), BF16),
             pltpu.VMEM((2, nz, 2, rows, outs), BF16),
+            dma((halves,)),
+            dma,
             dma((4,)),
             dma((nz, 2)),
             dma((nz, 2)),
             dma((nz, 2)),
             dma((2, nz, 2)),
-            dma((2, 2)),
-            dma((2, 2)),
-            dma((2,)),
-            dma((2,)),
-            dma((2,)),
+            dma((2, 2, halves)),
+            dma((2, 2, halves)),
+            dma((2, halves)),
+            dma((2, halves)),
+            dma((2, halves)),
         ],
         compiler_params=pltpu.CompilerParams(
             collective_id=0, has_side_effects=True, vmem_limit_bytes=VMEM_LIMIT
         ),
         name="forward_all",
-    )(live, f, ft, weight, cot, bias, mix)
+    )(live, maps, weight, cot, bias, mix, mix_in)
 
 
 def turn_mix(wide):
@@ -825,62 +858,150 @@
     return jnp.sum(jnp.where(rows == cols, wide[:, :chans], 0.0), axis=0, keepdims=True)
 
 
-def update_kernel(ft_ref, s_ref, m_ref, w_ref, sums_ref, mixed_ref, bias_ref, bias_m_ref, in_ref, in_m_ref,
-                  out_ref, out_m_ref, grad_ref, next_ref, moment_ref, bias_g, bias_n, bias_mn,
-                  in_g, in_n, in_mn, out_g, out_n, out_mn):
-    @pl.when((pl.program_id(0) == 0) & (pl.program_id(1) == 0))
-    def _():
-        def step(grad, value, moment, rate, at, grad_to, next_to, moment_to):
-            after = MOMENTUM * moment[at] + grad
-            grad_to[at] = grad
-            moment_to[at] = after
-            next_to[at] = value[at] - rate * after
-
-        for i in range(2):
-            at = (pl.ds(i, 1), slice(None))
-            step(sums_ref[4 + i], bias_ref, bias_m_ref, DENSE_RATE, at, bias_g, bias_n, bias_mn)
-            for j in range(2):
-                at = (i, pl.ds(j, 1), slice(None))
-                step(sums_ref[2 * i + j], out_ref, out_m_ref, STITCH_RATE, at, out_g, out_n, out_mn)
-                step(turn_mix(mixed_ref[2 * i + j]), in_ref, in_m_ref, STITCH_RATE, at, in_g, in_n, in_mn)
-
-    groups, _, _, rows, tile = s_ref.shape
-    grad = jnp.dot(ft_ref[0], s_ref[...].reshape(groups * rows, tile), preferred_element_type=F32)
-    grad_ref[0] = grad
-    moment = MOMENTUM * m_ref[0] + grad
-    moment_ref[0] = moment
-    next_ref[0] = (w_ref[0].astype(F32) - DENSE_RATE * moment).astype(BF16)
-
-
-def weight_update(ft_all, gathered, moment, weight, sums, mixed, bias, bias_m, mix_in, mix_in_m, mix_out, mix_out_m):
+def update_kernel(chunks, ft_ref, s_ref, m_ref, w_ref, maps_ref, acts_ref, sums_ref, mixed_ref,
+                  bias_ref, bias_m_ref, in_ref, in_m_ref, out_ref, out_m_ref,
+                  grad_to, next_to, moment_to, maps_to, acts_to, bias_g, bias_n, bias_mn,
+                  in_g, in_n, in_mn, out_g, out_n, out_mn,
+                  ft, s_in, m_in, w_in, g_out, n_out, m_out, maps_mid, acts_mid,
+                  ft_sem, in_sem, out_sem, maps_in_sem, maps_out_sem, acts_sem):
+    groups, parts, _, rows, tile = s_ref.shape
+    steps, ahead, behind = 2 * parts, s_in.shape[0], g_out.shape[0]
+    part = maps_mid.shape[0] // chunks
+
+    def loads(i):
+        t, j, slot = i // parts, i % parts, i % ahead
+        lanes = pl.ds(pl.multiple_of(j * tile, tile), tile)
+        return [
+            pltpu.make_async_copy(s_ref.at[:, j, t], s_in.at[slot], in_sem.at[slot, 0]),
+            pltpu.make_async_copy(m_ref.at[t, :, lanes], m_in.at[slot], in_sem.at[slot, 1]),
+            pltpu.make_async_copy(w_ref.at[t, :, lanes], w_in.at[slot], in_sem.at[slot, 2]),
+        ]
+
+    def stores(i):
+        t, j, slot = i // parts, i % parts, i % behind
+        lanes = pl.ds(pl.multiple_of(j * tile, tile), tile)
+        return [
+            pltpu.make_async_copy(g_out.at[slot], grad_to.at[t, :, lanes], out_sem.at[slot, 0]),
+            pltpu.make_async_copy(m_out.at[slot], moment_to.at[t, :, lanes], out_sem.at[slot, 1]),
+            pltpu.make_async_copy(n_out.at[slot], next_to.at[t, :, lanes], out_sem.at[slot, 2]),
+        ]
+
+    def each(copies, act):
+        for copy in copies:
+            act(copy)
+
+    start, wait = lambda copy: copy.start(), lambda copy: copy.wait()
+
+    def maps_load(i):
+        block = pl.ds(pl.multiple_of(i * part, part), part)
+        return pltpu.make_async_copy(maps_ref.at[block], maps_mid.at[block], maps_in_sem.at[i])
+
+    def maps_store(i):
+        block = pl.ds(pl.multiple_of(i * part, part), part)
+        return pltpu.make_async_copy(maps_mid.at[block], maps_to.at[block], maps_out_sem.at[i])
+
+    load_acts = pltpu.make_async_copy(acts_ref, acts_mid, acts_sem.at[0])
+    store_acts = pltpu.make_async_copy(acts_mid, acts_to, acts_sem.at[1])
+    towers = [pltpu.make_async_copy(ft_ref.at[t], ft.at[t], ft_sem.at[t]) for t in range(2)]
+    towers[0].start()
+    for i in range(ahead):
+        each(loads(i), start)
+    towers[1].start()
+
+    def step(grad, value, moment, rate, at, grad_ref, next_ref, moment_ref):
+        after = MOMENTUM * moment[at] + grad
+        grad_ref[at] = grad
+        moment_ref[at] = after
+        next_ref[at] = value[at] - rate * after
+
+    for i in range(2):
+        at = (pl.ds(i, 1), slice(None))
+        step(sums_ref[4 + i], bias_ref, bias_m_ref, DENSE_RATE, at, bias_g, bias_n, bias_mn)
+        for j in range(2):
+            at = (i, pl.ds(j, 1), slice(None))
+            step(sums_ref[2 * i + j], out_ref, out_m_ref, STITCH_RATE, at, out_g, out_n, out_mn)
+            step(turn_mix(mixed_ref[2 * i + j]), in_ref, in_m_ref, STITCH_RATE, at, in_g, in_n, in_mn)
+
+    towers[0].wait()
+
+    def body(i, carry):
+        slot, to = i % ahead, i % behind
+
+        @pl.when(i >= ahead)
+        def _():
+            maps_load(i - ahead).wait()
+            maps_store(i - ahead).start()
+
+        pl.when(i < chunks)(lambda: maps_load(i).start())
+        pl.when(i == 0)(load_acts.start)
+
+        @pl.when(i == ahead)
+        def _():
+            load_acts.wait()
+            store_acts.start()
+
+        pl.when(i == parts)(towers[1].wait)
+        each(loads(i), wait)
+        pl.when(i >= behind)(lambda: each(stores(i - behind), wait))
+        grad = jnp.dot(
+            ft[i // parts], s_in[slot].reshape(groups * rows, tile), preferred_element_type=F32
+        )
+        g_out[to] = grad
+        moment = MOMENTUM * m_in[slot] + grad
+        m_out[to] = moment
+        n_out[to] = (w_in[slot].astype(F32) - DENSE_RATE * moment).astype(BF16)
+        each(stores(i), start)
+        pl.when(i + ahead < steps)(lambda: each(loads(i + ahead), start))
+        return carry
+
+    lax.fori_loop(0, steps, body, 0)
+    for k in range(behind):
+        each(stores(steps - behind + k), wait)
+    for i in range(chunks):
+        maps_store(i).wait()
+    store_acts.wait()
+
+
+def weight_update(ft_all, gathered, moment, weight, maps, acts, sums, mixed, smalls):
     groups, parts, _, rows, outs = gathered.shape
     width = weight.shape[1]
-    tile = 512 if outs % 512 == 0 else 256
-    split = outs // tile
-    wide = pl.BlockSpec((1, width, tile), lambda t, j: (t, 0, j))
-    smalls = [bias, mix_in, mix_out]
+    chunks = 2 * parts - 3
+    here = pl.BlockSpec(memory_space=pltpu.VMEM)
+    far = pl.BlockSpec(memory_space=pl.ANY)
+    ahead, behind = 3, 2
+    vmem, dma = pltpu.VMEM, pltpu.SemaphoreType.DMA
     return pl.pallas_call(
-        update_kernel,
-        grid=(2, parts * split),
-        in_specs=[
-            pl.BlockSpec((1, width, groups * rows), lambda t, j: (t, 0, 0)),
-            pl.BlockSpec((groups, 1, 1, rows, tile), lambda t, j: (0, j // split, t, 0, j % split)),
-            wide,
-            wide,
-            full(sums.shape),
-            full(mixed.shape),
-        ]
-        + [full(a.shape) for a in smalls for _ in range(2)],
-        out_specs=[wide, wide, wide] + [full(a.shape) for a in smalls for _ in range(3)],
+        functools.partial(update_kernel, chunks),
+        in_specs=[far] * 6 + [here] * (2 + len(smalls)),
+        out_specs=[far] * 5 + [here] * 9,
         out_shape=[
             jax.ShapeDtypeStruct(moment.shape, F32),
             jax.ShapeDtypeStruct(moment.shape, BF16),
             jax.ShapeDtypeStruct(moment.shape, F32),
+            jax.ShapeDtypeStruct(maps.shape, BF16),
+            jax.ShapeDtypeStruct(acts.shape, BF16),
         ]
-        + [jax.ShapeDtypeStruct(a.shape, F32) for a in smalls for _ in range(3)],
+        + [jax.ShapeDtypeStruct(a.shape, F32) for a in smalls[::2] for _ in range(3)],
+        scratch_shapes=[
+            vmem((2, width, groups * rows), BF16),
+            vmem((ahead, groups, rows, outs), BF16),
+            vmem((ahead, width, outs), F32),
+            vmem((ahead, width, outs), BF16),
+            vmem((behind, width, outs), F32),
+            vmem((behind, width, outs), BF16),
+            vmem((behind, width, outs), F32),
+            vmem(maps.shape, BF16),
+            vmem(acts.shape, BF16),
+            dma((2,)),
+            dma((ahead, 3)),
+            dma((behind, 3)),
+            dma((chunks,)),
+            dma((chunks,)),
+            dma((2,)),
+        ],
         compiler_params=params(),
         name="weight_update",
-    )(ft_all, gathered, moment, weight, sums, mixed, bias, bias_m, mix_in, mix_in_m, mix_out, mix_out_m)
+    )(ft_all, gathered, moment, weight, maps, acts, sums, mixed, *smalls)
 
 
 def fast_shards(
@@ -898,18 +1019,18 @@
     live_rows,
 ):
     maps = jnp.transpose(input_maps, (1, 3, 2, 0))
-    cot = jnp.transpose(cotangent, (1, 0, 2))
-    ft, f = pool_forward(maps, stitch_in)
     ft_all, grads, acts, sums = forward_all(
-        mesh, live_rows, f, ft, dense_weight, cot, dense_bias, stitch_out
-    )
-    activations = jnp.transpose(acts, (1, 0, 2))
-    gathered, maps_out, sums, mixed = gather_all(mesh, grads, sums, dense_weight, maps, stitch_in)
-    maps_grad = jnp.transpose(maps_out, (3, 0, 2, 1))
+        mesh, live_rows, maps, dense_weight, cotangent, dense_bias, stitch_out, stitch_in
+    )
+    gathered, acts, maps_out, sums, mixed = gather_all(
+        mesh, grads, acts, sums, dense_weight, maps, stitch_in
+    )
     (
         weight_grad,
         weight_next,
         weight_moment_next,
+        maps_grad,
+        activations,
         bias_grad,
         bias_next,
         bias_moment_next,
@@ -924,15 +1045,13 @@
         gathered,
         weight_moment,
         dense_weight,
+        maps_out.reshape((-1,) + maps_out.shape[2:]),
+        acts,
         sums,
         mixed,
-        dense_bias,
-        bias_moment,
-        stitch_in,
-        stitch_in_moment,
-        stitch_out,
-        stitch_out_moment,
-    )
+        [dense_bias, bias_moment, stitch_in, stitch_in_moment, stitch_out, stitch_out_moment],
+    )
+    maps_grad = jnp.transpose(maps_grad.reshape(maps.shape), (3, 0, 2, 1))
     return (
         activations,
         maps_grad,

time: 320 us -> 291 us (0.909)
  local copies, waits for them, and re-layouts: 16.1 us -> 0 us
  Pallas kernels: 303 us -> 290 us
    pallas_call x2 -> x1, Pallas kernels: 95.2 us -> 74.9 us  [weight_update(): pl.pallas_call(functools.partial(update_kernel, chunks), in_specs=[far] *...]
    unnamed x3 -> x0, local copies, waits for them, and re-layouts: 16.1 us -> none
    pallas_call x1, Pallas kernels: 85 us -> 89.9 us  [forward_all(): pl.pallas_call(functools.partial(forward_kernel, nz), in_specs=[pl.BlockS...]
where the time goes in v3:
time: 291 us
  Pallas kernels  290 us (100%)
    pallas_call x1, Pallas kernels, gather_all(): pl.pallas_call(functools.partial(gather_kernel, nz, cut), in_specs=[far,...  125 us
    pallas_call x1, Pallas kernels, forward_all(): pl.pallas_call(functools.partial(forward_kernel, nz), in_specs=[pl.BlockS...  89.9 us
    pallas_call x1, Pallas kernels, weight_update(): pl.pallas_call(functools.partial(update_kernel, chunks), in_specs=[far] *...  74.9 us

profile of v3, /device:TPU:0, one launch (start us, length us, event | category | flops | bytes accessed | tf_op | source)
XLA Modules:
  0.0 290.7 jit_solution(2795148027938183607)
XLA Ops:
  0.6 89.9 %forward_all.1 = (bf16[2,1152,2048]{2,1,0:T(8,128)(2,1)}, bf16[2,512,512]{2,1,0:T(8,128)(2,1)}, bf16[2,512,512]{2,1,0:T(8,128)(2,1)}, f32[6,1,512]{2,1,0:T(1,128)}) custom-call(s32[4]{0:T(128)} %live_ref.1, bf16[2,169,32,512]{3,2,1,0:T(8,128)(2,1)} %bitcast.5, bf16[2,1152,4096]{2,1,0:T(8,128)(2,1)} %w_ref.5, bf16[512,2,512]{2,1,0:T(2,128)(2,1)} %cot_raw.1, ...), custom_call_target="tpu_custom_call" | custom-call | tf_op jit(solution)/shard_map/forward_all/pallas_call | solution.py:810
  90.6 125.0 %gather_all.1 = (bf16[4,8,2,512,512]{4,3,2,1,0:T(8,128)(2,1)}, bf16[512,2,512]{2,1,0:T(2,128)(2,1)}, bf16[2,169,32,512]{3,2,1,0:T(8,128)(2,1)}, f32[6,1,512]{2,1,0:T(1,128)}, f32[4,32,128]{2,1,0:T(8,128)}) custom-call(bf16[2,512,512]{2,1,0:T(8,128)(2,1)} %get-tuple-element.38.s_ref, bf16[2,512,512]{2,1,0:T(8,128)(2,1)} %get-tuple-element.39.acts_ref, ...), custom_call_target="tpu_custom_call" | custom-call | tf_op jit(solution)/shard_map/gather_all/pallas_call | solution.py:515
  215.6 74.9 %weight_update.1 = (f32[2,1152,4096]{2,1,0:T(8,128)}, bf16[2,1152,4096]{2,1,0:T(8,128)(2,1)}, f32[2,1152,4096]{2,1,0:T(8,128)}, bf16[338,32,512]{2,1,0:T(8,128)(...) custom-call(bf16[2,1152,2048]{2,1,0:T(8,128)(2,1)} %get-tuple-elemen, ...), custom_call_target="tpu_custom_call" | custom-call | tf_op jit(solution)/shard_map/weight_update/pallas_call | solution.py:973

commit v4 on v3

--- a/solution.py
+++ b/solution.py
@@ -251,22 +251,16 @@
             above[t, x, :, lanes] = value
 
 
-def gather_kernel(nz, cut, s_ref, acts_ref, sums_ref, w_ref, maps_ref, mix_ref,
-                  g_ref, acts_to, out_ref, total_ref, mixed_ref,
-                  keep_sem, line_send, line_recv, cross_send, cross_recv,
-                  half_send, half_recv, core_send, core_recv, small_send, small_recv,
-                  maps_sem, out_sem, w_sem, col_sem, acts_sem, acts_in, acts_out,
-                  maps_in, maps_out, wbuf, col, grads, cells, order, above, mix_total, wide,
-                  sums_in, sums_mid, mix_in, mix_mid):
+def gather_phase(nz, cut, s_ref, acts_in, sums_ref, w_ref, maps_in, wide,
+                 g_ref, acts_to, out_ref, total_ref, mixed_ref, sums_in, mix_in, sems,
+                 keep_sem, out_sem, w_sem, col_sem, acts_sem,
+                 acts_out, maps_out, wbuf, col, grads, cells, order, above, mix_total):
+    (line_send, line_recv, cross_send, cross_recv, half_send, half_recv, core_send, core_recv,
+     small_send, small_recv, sums_mid, mix_mid) = sems
     b, m, z, c, columns = neighbours()
     rows = s_ref.shape[1]
     spans = (pl.ds(0, cut), pl.ds(cut, rows - cut))
     sibling = m + 1 - 2 * c
-    load_maps = pltpu.make_async_copy(maps_ref, maps_in, maps_sem)
-    load_acts = pltpu.make_async_copy(acts_ref, acts_in, acts_sem.at[0])
-    load_acts.start()
-    load_maps.start()
-    greet(columns, m, z, c, nz)
 
     def small(kind, axis, src, dst):
         return remote(src, dst, small_send.at[kind, axis], small_recv.at[kind, axis], (columns[1 + axis], m))
@@ -381,9 +375,8 @@
         return carry
 
     pass_cross(1, z)
-    load_acts.wait()
     lax.fori_loop(0, rows // 16, join_towers, 0)
-    store_acts = pltpu.make_async_copy(acts_out, acts_to, acts_sem.at[1])
+    store_acts = pltpu.make_async_copy(acts_out, acts_to, acts_sem)
     store_acts.start()
     sides(1, arrive)
     pass_cross(0, z)
@@ -393,7 +386,7 @@
         if d == 2:
             spread()
     mine.wait()
-    width, chans = w_ref.shape[1], maps_ref.shape[2]
+    width, chans = w_ref.shape[1], maps_in.shape[2]
     outs = s_ref.shape[2]
     piece = wbuf.shape[1]
     pieces = width // piece
@@ -431,7 +424,6 @@
 
     weights(0).start()
     fill_order(order, chans, True)
-    spread_mix(mix_ref, wide)
     above[...] = jnp.zeros_like(above)
     mix_total[...] = jnp.zeros_like(mix_total)
     first_sums.wait()
@@ -450,7 +442,6 @@
     sides(1, late)
     features_grad(1)
     end_diagonal(0, z)
-    load_maps.wait()
     outer = (z == 0) | (z == nz - 1)
     inner = (z > 0) & (z < nz - 1)
     pl.when(inner)(lambda: sides(2, late))
@@ -501,69 +492,6 @@
         diagonal(1, axis, z).wait_send()
 
 
-def gather_all(mesh, grads, acts, sums, weight, maps, mix):
-    groups, parts = mesh.shape["batch"], mesh.shape["mp"]
-    nz = parts // 2
-    _, rows, outs = grads.shape
-    _, cells, chans, _ = maps.shape
-    width = weight.shape[1]
-    piece = width // 3
-    cut = rows * 25 // 32
-    dma = pltpu.SemaphoreType.DMA
-    here = pl.BlockSpec(memory_space=pltpu.VMEM)
-    far = pl.BlockSpec(memory_space=pl.ANY)
-    return pl.pallas_call(
-        functools.partial(gather_kernel, nz, cut),
-        in_specs=[far, far, here, far, far, here],
-        out_specs=[far, far, far, here, here],
-        out_shape=[
-            jax.ShapeDtypeStruct((groups, parts) + grads.shape, BF16),
-            jax.ShapeDtypeStruct((rows, 2, outs), BF16),
-            jax.ShapeDtypeStruct(maps.shape, BF16),
-            jax.ShapeDtypeStruct(sums.shape, F32),
-            jax.ShapeDtypeStruct((4, chans, 128), F32),
-        ],
-        scratch_shapes=[
-            dma,
-            dma((2, 5, nz)),
-            dma((5, nz)),
-            dma((2, nz + 1)),
-            dma((2, nz + 1)),
-            dma((2, nz + 1)),
-            dma((2, nz + 1)),
-            dma((2, 4, nz)),
-            dma((2, 4, nz)),
-            dma((2, 2)),
-            dma((2, 2)),
-            dma,
-            dma,
-            dma((2,)),
-            dma((parts,)),
-            dma((2,)),
-            pltpu.VMEM((2, rows, outs), BF16),
-            pltpu.VMEM((rows, 2, outs), BF16),
-            pltpu.VMEM(maps.shape, BF16),
-            pltpu.VMEM(maps.shape, BF16),
-            pltpu.VMEM((2, piece, parts * outs), BF16),
-            pltpu.VMEM((rows, parts * outs), BF16),
-            pltpu.VMEM((width, rows), BF16),
-            pltpu.VMEM((2, width, rows), F32),
-            pltpu.VMEM((width, width), BF16),
-            pltpu.VMEM((2, 13, chans, rows), F32),
-            pltpu.VMEM((4, chans, 128), F32),
-            pltpu.VMEM((4, chans, 128), F32),
-            pltpu.VMEM((2,) + sums.shape, F32),
-            pltpu.VMEM(sums.shape, F32),
-            pltpu.VMEM((3, 4, chans, 128), F32),
-            pltpu.VMEM((4, chans, 128), F32),
-        ],
-        compiler_params=pltpu.CompilerParams(
-            collective_id=1, has_side_effects=True, vmem_limit_bytes=VMEM_LIMIT
-        ),
-        name="gather_all",
-    )(grads, acts, sums, weight, maps, mix)
-
-
 def head_rows(hidden, cot, keep, mix, act_ref, grad_ref, here, lanes):
     active, slope, pulled = [], [], []
     for t in range(2):
@@ -582,272 +510,332 @@
     return terms
 
 
-def forward_kernel(nz, live_ref, maps_ref, w_ref, cot_raw, bias_ref, mix_ref, mix_in_ref,
-                   fta_ref, grad_ref, act_ref, sums_ref,
-                   maps_in, cells, order, wide, f_ref, ft_ref, cot_in, cot_ref, wbuf, pb, sb, rb, inb,
-                   maps_sem, cot_sem, w_sem, core_send, core_recv, line_send, line_recv,
-                   cross_send, cross_recv, half_send, half_recv, keep_sem):
+def step_kernel(nz, cut, live_ref, maps_ref, w_ref, cot_raw, bias_ref, mix_ref, mix_in_ref,
+                g_ref, fta_ref, acts_to, out_ref, total_ref, mixed_ref,
+                maps_in, rb, inb, ft_ref, s_ref, acts_in, sums_ref, wide, sums_in, mix_in,
+                maps_sem, swap_send, swap_recv, hop_send, hop_recv,
+                feat_send, feat_recv, turn_send, turn_recv, feat_keep, *rest):
     b, m, z, c, columns = neighbours()
     sibling = m + 1 - 2 * c
-    rows, outs = f_ref.shape[1], pb.shape[3]
-    live = live_ref[b]
-
-    chans, span = maps_in.shape[2], cells.shape[2]
-    halves = rows // span
+    chans, rows = maps_in.shape[2:]
+    width, outs = w_ref.shape[1], s_ref.shape[2]
+    span = rows // 2
+
+    def load_maps(h):
+        lanes = pl.ds(h * span, span)
+        return pltpu.make_async_copy(maps_ref.at[:, :, :, lanes], maps_in.at[:, :, :, lanes], maps_sem.at[h])
+
+    for h in range(2):
+        load_maps(h).start()
 
     def features(r, t, h):
         start = pl.multiple_of(columns[r] * rows + h * span, span)
         return fta_ref.at[t, :, pl.ds(start, span)]
 
-    def load_maps(h):
-        lanes = pl.ds(h * span, span)
-        return pltpu.make_async_copy(maps_ref.at[:, :, :, lanes], maps_in.at[:, :, :, lanes], maps_sem.at[h])
-
-    near = jnp.where(z < nz // 2, 1, 0)
-
-    def weights(i, t, own):
-        zd = near * (nz - 1 - i) + (1 - near) * i
-        j = 2 * zd + (c if own else 1 - c)
-        lanes = pl.ds(pl.multiple_of(j * outs, outs), outs)
-        k = 2 * t + own
-        return pltpu.make_async_copy(w_ref.at[t, :, lanes], wbuf.at[k], w_sem.at[k])
-
-    for h in range(halves):
-        load_maps(h).start()
-    for t in range(2):
-        for own in range(2):
-            weights(0, t, own).start()
-    load_cot = pltpu.make_async_copy(cot_raw, cot_in, cot_sem)
-    load_cot.start()
-    fill_order(order, chans, False)
-    spread_mix(mix_in_ref, wide)
-    greet(columns, m, z, c, nz)
-
     def mine(t, h):
-        return pltpu.make_async_copy(ft_ref.at[t, :, pl.ds(h * span, span)], features(0, t, h), keep_sem.at[t, h])
-
-    def cross(axis, t, h):
-        return remote(ft_ref.at[t, :, pl.ds(h * span, span)], features(0, t, h), cross_send.at[axis, t, h],
-                      cross_recv.at[axis, t, h], (columns[1 + axis], m))
-
-    def cross_wait(axis, t, h):
+        return pltpu.make_async_copy(ft_ref.at[t, :, pl.ds(h * span, span)], features(0, t, h), feat_keep.at[t, h])
+
+    def feature(axis, t, h):
+        return remote(ft_ref.at[t, :, pl.ds(h * span, span)], features(0, t, h), feat_send.at[axis, t, h],
+                      feat_recv.at[axis, t, h], (columns[1 + axis], m))
+
+    def feature_wait(axis, t, h):
         here = features(1 + axis, t, h)
-        remote(here, here, cross_send.at[axis, t, h], cross_recv.at[axis, t, h], (columns[1 + axis], m)).wait_recv()
-
-    def diagonal(axis, h):
+        remote(here, here, feat_send.at[axis, t, h], feat_recv.at[axis, t, h], (columns[1 + axis], m)).wait_recv()
+
+    def turn(axis, h):
         here = features(2 - axis, 1 - axis, h)
-        return remote(here, here, half_send.at[axis, h], half_recv.at[axis, h], (columns[1 + axis], m))
-
-    def diagonal_wait(axis, h):
+        return remote(here, here, turn_send.at[axis, h], turn_recv.at[axis, h], (columns[1 + axis], m))
+
+    def turn_wait(axis, h):
         here = features(3, 1 - axis, h)
-        remote(here, here, half_send.at[axis, h], half_recv.at[axis, h], (columns[1 + axis], m)).wait_recv()
-
-    def onward(h):
-        for axis in range(2):
-            cross_wait(1 - axis, 1 - axis, h)
-            diagonal(axis, h).start()
-
-    narrow = span // 128
-    for h in range(halves):
-
-        def pool_row(step, carry, h=h):
-            i = step // narrow
-            at = pl.multiple_of(step % narrow * 128, 128)
-            lanes = pl.ds(pl.multiple_of(h * span + at, 128), 128)
-            first = pooled_row(maps_in, 0, i, lanes)
-            second = pooled_row(maps_in, 1, i, lanes)
-            for t in range(2):
-                for j in range(6):
-                    value = wide[2 * t] * first[j] + wide[2 * t + 1] * second[j]
-                    start = pl.multiple_of((6 * i + j) * chans, chans)
-                    cells[t, pl.ds(start, chans), pl.ds(at, 128)] = value.astype(BF16)
-            return carry
-
-        load_maps(h).wait()
-        lax.fori_loop(0, 6 * narrow, pool_row, 0)
-        for t in range(2):
-            moved = jnp.dot(order[...], cells[t], preferred_element_type=F32).astype(BF16)
-            ft_ref[t, :, pl.ds(h * span, span)] = moved
-            f_ref[t, pl.ds(h * span, span), :] = moved.T
-        for k in range(2):
-            cross(0, k, h).start()
-            cross(1, 1 - k, h).start()
-
-    def swap(d, t):
-        return remote(sb.at[d, t], rb.at[d, t], core_send.at[d, t], core_recv.at[d, t], (b, sibling))
-
-    def hop(up, d, t):
-        return remote(rb.at[d, t], inb.at[up, d, t], line_send.at[d, t], line_recv.at[up, d, t],
-                      (b, m + 4 * up - 2))
-
-    step = 64
-
-    def relay(up, dm, t, first):
-        zm = up * z + (1 - up) * (nz - 1 - z)
-        d = up * dm + (1 - up) * (nz - 1 - dm)
-
-        def go():
-            swap(d, t).wait_recv()
-            if not first:
-                hop(up, d, t).wait_recv()
-
-            def add(k, carry):
-                here = pl.ds(pl.multiple_of(k * step, step), step)
-                value = pb[d, t, here, :] + rb[d, t, here, :].astype(F32)
-                if not first:
-                    value += inb[up, d, t, here, :].astype(F32)
-                rb[d, t, here, :] = value.astype(BF16)
-                return carry
-
-            lax.fori_loop(0, rows // step, add, 0)
-            hop(up, d, t).start()
-
-        pl.when((zm == 0 if first else zm > 0) & (zm < dm))(go)
-
-    def produce(i, carry):
-        zd = near * (nz - 1 - i) + (1 - near) * i
+        remote(here, here, turn_send.at[axis, h], turn_recv.at[axis, h], (columns[1 + axis], m)).wait_recv()
+
+    def forward(cells, order, f_ref, cot_in, cot_ref, wbuf, pb, sb, cot_sem, w_sem):
+        live = live_ref[b]
+        near = jnp.where(z < nz // 2, 1, 0)
+
+        def weights(i, t, own):
+            zd = near * (nz - 1 - i) + (1 - near) * i
+            j = 2 * zd + (c if own else 1 - c)
+            lanes = pl.ds(pl.multiple_of(j * outs, outs), outs)
+            k = 2 * t + own
+            return pltpu.make_async_copy(w_ref.at[t, :, lanes], wbuf.at[k], w_sem.at[k])
+
         for t in range(2):
             for own in range(2):
-                weights(i, t, own).wait()
-                part = jnp.dot(f_ref[t], wbuf[2 * t + own], preferred_element_type=F32)
-                if own:
-                    pb[zd, t] = part
-                else:
-                    sb[zd, t] = part.astype(BF16)
-                    swap(zd, t).start()
-                pl.when(i < nz - 1)(lambda t=t, own=own: weights(i + 1, t, own).start())
-            relay(near, nz - 1 - i, t, True)
-        return carry
-
-    lax.fori_loop(0, nz, produce, 0)
-    onward(0)
-    for t in range(2):
-        for h in range(halves):
-            mine(t, h).start()
-    load_cot.wait()
-
-    def part_towers(k, carry):
-        here = pl.ds(pl.multiple_of(k * 16, 16), 16)
-        both = cot_in[here, :, :].astype(F32)
+                weights(0, t, own).start()
+        load_cot = pltpu.make_async_copy(cot_raw, cot_in, cot_sem)
+        load_cot.start()
+        fill_order(order, chans, False)
+        spread_mix(mix_in_ref, wide)
+        greet(columns, m, z, c, nz)
+
+        def swap(d, t, h):
+            here = pl.ds(h * span, span)
+            return remote(sb.at[d, t, here], rb.at[d, t, here], swap_send.at[d, t, h], swap_recv.at[d, t, h], (b, sibling))
+
+        def hop(up, d, t, h):
+            here = pl.ds(h * span, span)
+            return remote(rb.at[d, t, here], inb.at[d + up, t, here], hop_send.at[d, t, h], hop_recv.at[up, d, t, h],
+                          (b, m + 4 * up - 2))
+
+        step = 64
+
+        def relay(up, dm, t, h, first):
+            zm = up * z + (1 - up) * (nz - 1 - z)
+            d = up * dm + (1 - up) * (nz - 1 - dm)
+
+            def go():
+                swap(d, t, h).wait_recv()
+                if not first:
+                    hop(up, d, t, h).wait_recv()
+
+                def add(k, carry):
+                    here = pl.ds(pl.multiple_of(h * span + k * step, step), step)
+                    value = pb[d, t, here, :] + rb[d, t, here, :].astype(F32)
+                    if not first:
+                        value += inb[d + up, t, here, :].astype(F32)
+                    rb[d, t, here, :] = value.astype(BF16)
+                    return carry
+
+                lax.fori_loop(0, span // step, add, 0)
+                hop(up, d, t, h).start()
+
+            pl.when((zm == 0 if first else zm > 0) & (zm < dm))(go)
+
+        narrow = span // 128
+
+        def pool(h):
+            def pool_row(step, carry):
+                i = step // narrow
+                at = pl.multiple_of(step % narrow * 128, 128)
+                lanes = pl.ds(pl.multiple_of(h * span + at, 128), 128)
+                first = pooled_row(maps_in, 0, i, lanes)
+                second = pooled_row(maps_in, 1, i, lanes)
+                for t in range(2):
+                    for j in range(6):
+                        value = wide[2 * t] * first[j] + wide[2 * t + 1] * second[j]
+                        start = pl.multiple_of((6 * i + j) * chans, chans)
+                        cells[t, pl.ds(start, chans), pl.ds(at, 128)] = value.astype(BF16)
+                return carry
+
+            load_maps(h).wait()
+            lax.fori_loop(0, 6 * narrow, pool_row, 0)
+            for t in range(2):
+                moved = jnp.dot(order[...], cells[t], preferred_element_type=F32).astype(BF16)
+                ft_ref[t, :, pl.ds(h * span, span)] = moved
+                f_ref[t, pl.ds(h * span, span), :] = moved.T
+            for k in range(2):
+                feature(0, k, h).start()
+                feature(1, 1 - k, h).start()
+
+        def produce(i, h):
+            zd = near * (nz - 1 - i) + (1 - near) * i
+            here = pl.ds(h * span, span)
+            for t in range(2):
+                for own in range(2):
+                    if h == 0:
+                        weights(i, t, own).wait()
+                    part = jnp.dot(f_ref[t, here, :], wbuf[2 * t + own], preferred_element_type=F32)
+                    if own:
+                        pb[zd, t, here, :] = part
+                    else:
+                        sb[zd, t, here, :] = part.astype(BF16)
+                        swap(zd, t, h).start()
+                    if h == 1:
+                        pl.when(i < nz - 1)(lambda t=t, own=own: weights(i + 1, t, own).start())
+                relay(near, nz - 1 - i, t, h, True)
+
+        for h in range(2):
+            pool(h)
+            produce(0, h)
+
+        def both(i, carry):
+            for h in range(2):
+                produce(i, h)
+            return carry
+
+        lax.fori_loop(1, nz, both, 0)
+
+        def onward(h):
+            for axis in range(2):
+                feature_wait(1 - axis, 1 - axis, h)
+                turn(axis, h).start()
+
+        onward(0)
         for t in range(2):
-            cot_ref[t, here, :] = both[:, t, :].astype(BF16)
-        return carry
-
-    lax.fori_loop(0, rows // 16, part_towers, 0)
-    for dm in range(nz - 1, 0, -1):
-        for t in range(2):
-            relay(near, dm, t, False)
-            relay(1 - near, dm, t, False)
-        if dm == nz - 1:
-            for h in range(1, halves):
-                onward(h)
-
-    for t in range(2):
-        swap(z, t).wait_recv()
-        pl.when(z > 0)(lambda t=t: hop(1, z, t).wait_recv())
-        pl.when(z < nz - 1)(lambda t=t: hop(0, z, t).wait_recv())
-
-        def gather(k, carry, t=t):
-            here = pl.ds(pl.multiple_of(k * step, step), step)
-            pb[z, t, here, :] += rb[z, t, here, :].astype(F32)
-            for up in range(2):
-                inside = z > 0 if up else z < nz - 1
-
-                @pl.when(inside)
-                def _(up=up):
-                    pb[z, t, here, :] += inb[up, z, t, here, :].astype(F32)
-
+            for h in range(2):
+                mine(t, h).start()
+        load_cot.wait()
+
+        def part_towers(k, carry):
+            here = pl.ds(pl.multiple_of(k * 16, 16), 16)
+            both = cot_in[here, :, :].astype(F32)
+            for t in range(2):
+                cot_ref[t, here, :] = both[:, t, :].astype(BF16)
             return carry
 
-        lax.fori_loop(0, rows // step, gather, 0)
-    tile, high = 256, 16
-    for lane in range(outs // tile):
-        lanes = pl.ds(lane * tile, tile)
-        bias = [bias_ref[pl.ds(t, 1), lanes] for t in range(2)]
-        mix = [mix_ref[k // 2, pl.ds(k % 2, 1), lanes] for k in range(4)]
-
-        def block(k, totals, lanes=lanes, bias=bias, mix=mix):
-            here = pl.ds(pl.multiple_of(k * high, high), high)
-            hidden = [pb[z, t, here, lanes] + bias[t] for t in range(2)]
-            cot = [cot_ref[t, here, lanes].astype(F32) for t in range(2)]
-            place = k * high + lax.broadcasted_iota(jnp.int32, (high, tile), 0)
-            keep = jnp.where(place < live, 1.0, 0.0)
-            terms = head_rows(hidden, cot, keep, mix, act_ref, grad_ref, here, lanes)
-            return tuple(a + v[:8] + v[8:] for a, v in zip(totals, terms))
-
-        zero = jnp.zeros((8, tile), F32)
-        totals = lax.fori_loop(0, rows // high, block, (zero,) * 6)
-        for k in range(6):
-            sums_ref[k, :, lanes] = jnp.sum(totals[k], axis=0, keepdims=True)
-
-    for h in range(halves):
+        lax.fori_loop(0, rows // 16, part_towers, 0)
+        for dm in range(nz - 1, 0, -1):
+            for h in range(2):
+                for t in range(2):
+                    relay(near, dm, t, h, False)
+                    relay(1 - near, dm, t, h, False)
+            if dm == nz - 1:
+                onward(1)
+
+        tile, high = 256, 16
+        for h in range(2):
+            for t in range(2):
+                swap(z, t, h).wait_recv()
+                pl.when(z > 0)(lambda t=t, h=h: hop(1, z, t, h).wait_recv())
+                pl.when(z < nz - 1)(lambda t=t, h=h: hop(0, z, t, h).wait_recv())
+
+                def gather(k, carry, t=t, h=h):
+                    here = pl.ds(pl.multiple_of(h * span + k * step, step), step)
+                    pb[z, t, here, :] += rb[z, t, here, :].astype(F32)
+                    for up in range(2):
+                        inside = z > 0 if up else z < nz - 1
+
+                        @pl.when(inside)
+                        def _(up=up):
+                            pb[z, t, here, :] += inb[z + up, t, here, :].astype(F32)
+
+                    return carry
+
+                lax.fori_loop(0, span // step, gather, 0)
+            for lane in range(outs // tile):
+                lanes = pl.ds(lane * tile, tile)
+                bias = [bias_ref[pl.ds(t, 1), lanes] for t in range(2)]
+                mix = [mix_ref[k // 2, pl.ds(k % 2, 1), lanes] for k in range(4)]
+
+                def block(k, totals, lanes=lanes, bias=bias, mix=mix):
+                    here = pl.ds(pl.multiple_of(k * high, high), high)
+                    hidden = [pb[z, t, here, lanes] + bias[t] for t in range(2)]
+                    cot = [cot_ref[t, here, lanes].astype(F32) for t in range(2)]
+                    place = k * high + lax.broadcasted_iota(jnp.int32, (high, tile), 0)
+                    keep = jnp.where(place < live, 1.0, 0.0)
+                    terms = head_rows(hidden, cot, keep, mix, acts_in, s_ref, here, lanes)
+                    return tuple(a + v[:8] + v[8:] for a, v in zip(totals, terms))
+
+                zero = jnp.zeros((8, tile), F32)
+                count = span // high
+                totals = lax.fori_loop(h * count, (h + 1) * count, block, (zero,) * 6)
+                for k in range(6):
+                    value = jnp.sum(totals[k], axis=0, keepdims=True)
+                    sums_ref[k, :, lanes] = value if h == 0 else sums_ref[k, :, lanes] + value
+        for d in range(nz):
+            for t in range(2):
+                for h in range(2):
+                    swap(d, t, h).wait_send()
+                    pl.when(z < d)(lambda d=d, t=t, h=h: hop(1, d, t, h).wait_send())
+                    pl.when(z > d)(lambda d=d, t=t, h=h: hop(0, d, t, h).wait_send())
+
+    vmem, dma = pltpu.VMEM, pltpu.SemaphoreType.DMA
+    pl.run_scoped(
+        forward,
+        vmem((2, width, span), BF16),
+        vmem((width, width), BF16),
+        vmem((2, rows, width), BF16),
+        vmem(cot_raw.shape, BF16),
+        vmem((2, rows, outs), BF16),
+        vmem((4, width, outs), BF16),
+        vmem((nz, 2, rows, outs), F32),
+        vmem((nz, 2, rows, outs), BF16),
+        dma,
+        dma((4,)),
+    )
+    pl.run_scoped(
+        functools.partial(gather_phase, nz, cut, s_ref, acts_in, sums_ref, w_ref, maps_in, wide,
+                          g_ref, acts_to, out_ref, total_ref, mixed_ref, sums_in, mix_in, rest),
+        dma,
+        dma,
+        dma((2,)),
+        dma((2 * nz,)),
+        dma,
+        vmem((rows, 2, outs), BF16),
+        vmem(maps_in.shape, BF16),
+        vmem((2, width // 3, 2 * nz * outs), BF16),
+        vmem((rows, 2 * nz * outs), BF16),
+        vmem((width, rows), BF16),
+        vmem((2, width, rows), F32),
+        vmem((width, width), BF16),
+        vmem((2, 13, chans, rows), F32),
+        vmem((4, chans, 128), F32),
+    )
+    for h in range(2):
         for axis in range(2):
-            cross_wait(axis, 1 - axis, h)
-            diagonal_wait(axis, h)
-            diagonal(axis, h).wait_send()
+            feature_wait(axis, 1 - axis, h)
+            turn_wait(axis, h)
+            turn(axis, h).wait_send()
             for t in range(2):
-                cross(axis, t, h).wait_send()
+                feature(axis, t, h).wait_send()
         for t in range(2):
             mine(t, h).wait()
-    for d in range(nz):
-        for t in range(2):
-            swap(d, t).wait_send()
-            pl.when(z < d)(lambda d=d, t=t: hop(1, d, t).wait_send())
-            pl.when(z > d)(lambda d=d, t=t: hop(0, d, t).wait_send())
-
-
-def forward_all(mesh, live, maps, weight, cot, bias, mix, mix_in):
+
+
+def step_all(mesh, live, maps, weight, cot, bias, mix, mix_in):
     groups, parts = mesh.shape["batch"], mesh.shape["mp"]
     nz = parts // 2
     chans, rows = maps.shape[2:]
     width = weight.shape[1]
     outs = weight.shape[2] // parts
-    span = 256
-    halves = rows // span
-    dma = pltpu.SemaphoreType.DMA
+    cut = rows * 25 // 32
+    vmem, dma = pltpu.VMEM, pltpu.SemaphoreType.DMA
     here = pl.BlockSpec(memory_space=pltpu.VMEM)
     far = pl.BlockSpec(memory_space=pl.ANY)
+    sums = (6, 1, outs)
     return pl.pallas_call(
-        functools.partial(forward_kernel, nz),
+        functools.partial(step_kernel, nz, cut),
         in_specs=[pl.BlockSpec(memory_space=pltpu.SMEM), far, far, far, here, here, here],
-        out_specs=[far, here, here, here],
+        out_specs=[far, far, far, far, here, here],
         out_shape=[
+            jax.ShapeDtypeStruct((groups, parts, 2, rows, outs), BF16),
             jax.ShapeDtypeStruct((2, width, groups * rows), BF16),
-            jax.ShapeDtypeStruct((2, rows, outs), BF16),
-            jax.ShapeDtypeStruct((2, rows, outs), BF16),
-            jax.ShapeDtypeStruct((6, 1, outs), F32),
+            jax.ShapeDtypeStruct((rows, 2, outs), BF16),
+            jax.ShapeDtypeStruct(maps.shape, BF16),
+            jax.ShapeDtypeStruct(sums, F32),
+            jax.ShapeDtypeStruct((4, chans, 128), F32),
         ],
         scratch_shapes=[
-            pltpu.VMEM(maps.shape, BF16),
-            pltpu.VMEM((2, width, span), BF16),
-            pltpu.VMEM((width, width), BF16),
-            pltpu.VMEM((4, chans, 128), F32),
-            pltpu.VMEM((2, rows, width), BF16),
-            pltpu.VMEM((2, width, rows), BF16),
-            pltpu.VMEM(cot.shape, BF16),
-            pltpu.VMEM((2, rows, outs), BF16),
-            pltpu.VMEM((4, width, outs), BF16),
-            pltpu.VMEM((nz, 2, rows, outs), F32),
-            pltpu.VMEM((nz, 2, rows, outs), BF16),
-            pltpu.VMEM((nz, 2, rows, outs), BF16),
-            pltpu.VMEM((2, nz, 2, rows, outs), BF16),
-            dma((halves,)),
-            dma,
-            dma((4,)),
-            dma((nz, 2)),
-            dma((nz, 2)),
-            dma((nz, 2)),
-            dma((2, nz, 2)),
-            dma((2, 2, halves)),
-            dma((2, 2, halves)),
-            dma((2, halves)),
-            dma((2, halves)),
-            dma((2, halves)),
+            vmem(maps.shape, BF16),
+            vmem((nz, 2, rows, outs), BF16),
+            vmem((nz + 1, 2, rows, outs), BF16),
+            vmem((2, width, rows), BF16),
+            vmem((2, rows, outs), BF16),
+            vmem((2, rows, outs), BF16),
+            vmem(sums, F32),
+            vmem((4, chans, 128), F32),
+            vmem((2,) + sums, F32),
+            vmem((3, 4, chans, 128), F32),
+            dma((2,)),
+            dma((nz, 2, 2)),
+            dma((nz, 2, 2)),
+            dma((nz, 2, 2)),
+            dma((2, nz, 2, 2)),
+            dma((2, 2, 2)),
+            dma((2, 2, 2)),
+            dma((2, 2)),
+            dma((2, 2)),
+            dma((2, 2)),
+            dma((2, 5, nz)),
+            dma((5, nz)),
+            dma((2, nz + 1)),
+            dma((2, nz + 1)),
+            dma((2, nz + 1)),
+            dma((2, nz + 1)),
+            dma((2, 4, nz)),
+            dma((2, 4, nz)),
+            dma((2, 2)),
+            dma((2, 2)),
+            vmem(sums, F32),
+            vmem((4, chans, 128), F32),
         ],
         compiler_params=pltpu.CompilerParams(
             collective_id=0, has_side_effects=True, vmem_limit_bytes=VMEM_LIMIT
         ),
-        name="forward_all",
+        name="step_all",
     )(live, maps, weight, cot, bias, mix, mix_in)
 
 
@@ -1019,11 +1007,8 @@
     live_rows,
 ):
     maps = jnp.transpose(input_maps, (1, 3, 2, 0))
-    ft_all, grads, acts, sums = forward_all(
+    gathered, ft_all, acts, maps_out, sums, mixed = step_all(
         mesh, live_rows, maps, dense_weight, cotangent, dense_bias, stitch_out, stitch_in
-    )
-    gathered, acts, maps_out, sums, mixed = gather_all(
-        mesh, grads, acts, sums, dense_weight, maps, stitch_in
     )
     (
         weight_grad,

time: 291 us -> 282 us (0.969)
  Pallas kernels: 290 us -> 281 us
    pallas_call x2 -> x1, Pallas kernels: 215 us -> 206 us  [step_all(): pl.pallas_call(functools.partial(step_kernel, nz, cut), in_specs=[pl.Bloc...]
where the time goes in v4:
time: 282 us
  Pallas kernels  281 us (100%)
    pallas_call x1, Pallas kernels, step_all(): pl.pallas_call(functools.partial(step_kernel, nz, cut), in_specs=[pl.Bloc...  206 us
    pallas_call x1, Pallas kernels, weight_update(): pl.pallas_call(functools.partial(update_kernel, chunks), in_specs=[far] *...  74.9 us

profile of v4, /device:TPU:0, one launch (start us, length us, event | category | flops | bytes accessed | tf_op | source)
XLA Modules:
  0.0 282.1 jit_solution(14147974000534484344)
XLA Ops:
  0.6 206.3 %step_all.1 = (bf16[4,8,2,512,512]{4,3,2,1,0:T(8,128)(2,1)}, bf16[2,1152,2048]{2,1,0:T(8,128)(2,1)}, bf16[512,2,512]{2,1,0:T(2,128)(2,1)}, bf16[2,169,32,512]{3,...) custom-call(s32[4]{0:T(128)} %live_ref.1, bf16[2,169,32,512]{3,2,1,0:T(8,128)(2,1)} %bitcast.5, ...), custom_call_target="tpu_custom_call" | custom-call | tf_op jit(solution)/shard_map/step_all/pallas_call | solution.py:789
  207.0 74.9 %weight_update.1 = (f32[2,1152,4096]{2,1,0:T(8,128)}, bf16[2,1152,4096]{2,1,0:T(8,128)(2,1)}, f32[2,1152,4096]{2,1,0:T(8,128)}, bf16[338,32,512]{2,1,0:T(8,128)(...) custom-call(bf16[2,1152,2048]{2,1,0:T(8,128)(2,1)} %get-tuple-elemen, ...), custom_call_target="tpu_custom_call" | custom-call | tf_op jit(solution)/shard_map/weight_update/pallas_call | solution.py:961

commit v5 on v4

--- a/solution.py
+++ b/solution.py
@@ -251,7 +251,27 @@
             above[t, x, :, lanes] = value
 
 
-def gather_phase(nz, cut, s_ref, acts_in, sums_ref, w_ref, maps_in, wide,
+def shares(live_ref, groups, base):
+    counts = [live_ref[k] for k in range(groups)]
+    excess, free = [], []
+    taken = given = 0
+    for count in counts:
+        excess.append(taken)
+        free.append(given)
+        taken = taken + jnp.maximum(count - base, 0)
+        given = given + jnp.maximum(base - count, 0)
+    return counts, excess, free
+
+
+def picks(count, free, other, excess, base, spare, slots_in_lanes):
+    shape = (spare, base) if slots_in_lanes else (base, spare)
+    slot = lax.broadcasted_iota(jnp.int32, shape, 1 if slots_in_lanes else 0)
+    row = lax.broadcasted_iota(jnp.int32, shape, 0 if slots_in_lanes else 1)
+    hit = (slot - count + free == row + excess) & (slot >= count) & (row < other - base)
+    return jnp.where(hit, 1.0, 0.0).astype(BF16)
+
+
+def gather_phase(nz, cut, base, features_on, live_ref, pool_ref, pool, s_ref, acts_in, sums_ref, w_ref, maps_in, wide,
                  g_ref, acts_to, out_ref, total_ref, mixed_ref, sums_in, mix_in, sems,
                  keep_sem, out_sem, w_sem, col_sem, acts_sem,
                  acts_out, maps_out, wbuf, col, grads, cells, order, above, mix_total):
@@ -259,7 +279,8 @@
      small_send, small_recv, sums_mid, mix_mid) = sems
     b, m, z, c, columns = neighbours()
     rows = s_ref.shape[1]
-    spans = (pl.ds(0, cut), pl.ds(cut, rows - cut))
+    spans = (pl.ds(0, cut), pl.ds(cut, base - cut), pl.ds(base, rows - base))
+    spare = rows - base
     sibling = m + 1 - 2 * c
 
     def small(kind, axis, src, dst):
@@ -272,7 +293,7 @@
         return g_ref.at[columns[r], 2 * zz + c, t, spans[p], :]
 
     def line(k, zz, up, own=False):
-        p, r = (0, 0) if k == 0 else (1, k - 1)
+        p, r = {0: (0, 0), 5: (2, 0)}.get(k, (1, k - 1))
         src = s_ref.at[:, spans[p], :] if own else place(p, r, zz)
         side = 1 if up else 0
         to = m + 2 if up else m - 2
@@ -322,18 +343,40 @@
             pl.when(z > 0)(lambda: line(k, zz, False).start())
 
     mine = pltpu.make_async_copy(s_ref, g_ref.at[b, m], keep_sem)
+
+    def launch(k):
+        pl.when(z < nz - 1)(lambda: line(k, z, True, True).start())
+        pl.when(z > 0)(lambda: line(k, z, False, True).start())
+
+    first_sums = small(0, 0, sums_ref, sums_in.at[0])
+    first_sums.start()
+    for axis in range(2):
+        pool.come(axis)
+        pool.turn(1 - axis).start()
+    launch(5)
+    core(2, 0, z, True).start()
+    counts, excess, free = shares(live_ref, 4, base)
+    live = live_ref[b]
+    offset = 0
+    for k in range(1, 4):
+        offset = offset + jnp.where(b >= k, jnp.maximum(base - counts[k - 1], 0), 0)
+    chosen = jnp.concatenate(
+        [picks(live, offset, counts[k], excess[k], base, spare, False) for k in range(4)], axis=1
+    )
+    for axis in range(2):
+        pool.end(axis)
+    for t in range(2):
+        moved = jnp.dot(chosen, pool_ref[t], preferred_element_type=F32)
+        s_ref[t, :base, :] = (s_ref[t, :base, :].astype(F32) + moved).astype(BF16)
     cross(1, 0, z, True).start()
     cross(1, 1, z, True).start()
-    pl.when(z < nz - 1)(lambda: line(0, z, True, True).start())
-    pl.when(z > 0)(lambda: line(0, z, False, True).start())
+    launch(0)
     cross(0, 0, z, True).start()
     cross(0, 1, z, True).start()
-    pl.when(z < nz - 1)(lambda: line(1, z, True, True).start())
-    pl.when(z > 0)(lambda: line(1, z, False, True).start())
-    first_sums = small(0, 0, sums_ref, sums_in.at[0])
-    first_sums.start()
+    launch(1)
     core(0, 0, z, True).start()
     core(1, 0, z, True).start()
+    features_on(0)
     mine.start()
 
     def pass_cross(p, zz):
@@ -353,9 +396,10 @@
         cross(0, 0, zz).start()
         cross(0, 1, zz).start()
         core(0, 0, zz).start()
-        line(1, zz, up).wait_recv()
-        onward(1, zz, up)
-        core(1, 0, zz).start()
+        for k, p in ((1, 1), (5, 2)):
+            line(k, zz, up).wait_recv()
+            onward(k, zz, up)
+            core(p, 0, zz).start()
 
     def late(zz, up):
         for k in range(2, 5):
@@ -381,11 +425,7 @@
     sides(1, arrive)
     pass_cross(0, z)
     end_diagonal(1, z)
-    for d in range(2, nz):
-        sides(d, arrive)
-        if d == 2:
-            spread()
-    mine.wait()
+    sides(2, arrive)
     width, chans = w_ref.shape[1], maps_in.shape[2]
     outs = s_ref.shape[2]
     piece = wbuf.shape[1]
@@ -411,7 +451,8 @@
             value = lax.dot_general(
                 wbuf[k % 2], col[...], (((1,), (1,)), ((), ())), preferred_element_type=F32
             )
-            grads[pl.ds(k % pieces * piece, piece), :] = value.astype(BF16)
+            lane = lax.broadcasted_iota(jnp.int32, value.shape, 1)
+            grads[pl.ds(k % pieces * piece, piece), :] = jnp.where(lane < live, value, 0.0).astype(BF16)
         cells[t] = jnp.dot(order[...], grads[...], preferred_element_type=F32)
 
     blocks = rows // 128
@@ -430,20 +471,34 @@
     sums_mid[...] = sums_ref[...] + sums_in[0]
     second_sums = small(0, 1, sums_mid, sums_in.at[1])
     second_sums.start()
-    sides(1, lambda zz, up: pass_cross(0, zz))
+    outer = (z == 0) | (z == nz - 1)
+    inner = (z > 0) & (z < nz - 1)
+
+    @pl.when(outer)
+    def _():
+        sides(1, lambda zz, up: pass_cross(0, zz))
+        sides(3, arrive)
+        spread()
+
+    mine.wait()
     for zz in range(nz):
-        for p in range(2):
+        for p in range(3):
             core_wait(p, 0, zz)
     for j in range(2 * nz):
         column(0, j).start()
     features_grad(0)
     for j in range(2 * nz):
         column(1, j).start()
-    sides(1, late)
+    pl.when(inner)(spread)
+    pl.when(outer)(lambda: sides(1, late))
     features_grad(1)
+
+    @pl.when(inner)
+    def _():
+        sides(1, lambda zz, up: pass_cross(0, zz))
+        sides(1, late)
+
     end_diagonal(0, z)
-    outer = (z == 0) | (z == nz - 1)
-    inner = (z > 0) & (z < nz - 1)
     pl.when(inner)(lambda: sides(2, late))
     pl.when(outer)(lambda: sides(2, lambda zz, up: pass_cross(0, zz)))
     lax.fori_loop(0, 3 * blocks, maps_back, 0)
@@ -481,10 +536,11 @@
                 if r > 0:
                     core_wait(p, r, zz)
                 core(p, r, zz).wait_send()
+        core(2, 0, zz).wait_send()
         for axis in range(2):
             cross(0, axis, zz).wait_send()
             diagonal(0, axis, zz).wait_send()
-        for k in range(5):
+        for k in range(6):
             pl.when((z < nz - 1) & (z >= zz))(lambda k=k, zz=zz: line(k, zz, True).wait_send())
             pl.when((z > 0) & (z <= zz))(lambda k=k, zz=zz: line(k, zz, False).wait_send())
     for axis in range(2):
@@ -510,11 +566,12 @@
     return terms
 
 
-def step_kernel(nz, cut, live_ref, maps_ref, w_ref, cot_raw, bias_ref, mix_ref, mix_in_ref,
+def step_kernel(nz, cut, base, live_ref, maps_ref, w_ref, cot_raw, bias_ref, mix_ref, mix_in_ref,
                 g_ref, fta_ref, acts_to, out_ref, total_ref, mixed_ref,
                 maps_in, rb, inb, ft_ref, s_ref, acts_in, sums_ref, wide, sums_in, mix_in,
                 maps_sem, swap_send, swap_recv, hop_send, hop_recv,
-                feat_send, feat_recv, turn_send, turn_recv, feat_keep, *rest):
+                feat_send, feat_recv, turn_send, turn_recv, feat_keep,
+                pool_ref, pool_send, pool_recv, pool_turn_send, pool_turn_recv, *rest):
     b, m, z, c, columns = neighbours()
     sibling = m + 1 - 2 * c
     chans, rows = maps_in.shape[2:]
@@ -525,7 +582,7 @@
         lanes = pl.ds(h * span, span)
         return pltpu.make_async_copy(maps_ref.at[:, :, :, lanes], maps_in.at[:, :, :, lanes], maps_sem.at[h])
 
-    for h in range(2):
+    for h in (1, 0):
         load_maps(h).start()
 
     def features(r, t, h):
@@ -550,6 +607,34 @@
     def turn_wait(axis, h):
         here = features(3, 1 - axis, h)
         remote(here, here, turn_send.at[axis, h], turn_recv.at[axis, h], (columns[1 + axis], m)).wait_recv()
+
+    def features_on(h):
+        for axis in range(2):
+            feature_wait(1 - axis, 1 - axis, h)
+            turn(axis, h).start()
+
+    spare = rows - base
+
+    class pool:
+        def slot(r, t=None):
+            start = pl.ds(pl.multiple_of(columns[r] * spare, spare), spare)
+            return pool_ref.at[:, start, :] if t is None else pool_ref.at[t, start, :]
+
+        def go(axis):
+            return remote(s_ref.at[:, pl.ds(base, spare), :], pool.slot(0), pool_send.at[axis], pool_recv.at[axis],
+                          (columns[1 + axis], m))
+
+        def come(axis):
+            here = pool.slot(1 + axis)
+            remote(here, here, pool_send.at[axis], pool_recv.at[axis], (columns[1 + axis], m)).wait_recv()
+
+        def turn(axis):
+            here = pool.slot(2 - axis, 1 - axis)
+            return remote(here, here, pool_turn_send.at[axis], pool_turn_recv.at[axis], (columns[1 + axis], m))
+
+        def end(axis):
+            here = pool.slot(3, 1 - axis)
+            remote(here, here, pool_turn_send.at[axis], pool_turn_recv.at[axis], (columns[1 + axis], m)).wait_recv()
 
     def forward(cells, order, f_ref, cot_in, cot_ref, wbuf, pb, sb, cot_sem, w_sem):
         live = live_ref[b]
@@ -606,7 +691,7 @@
 
         narrow = span // 128
 
-        def pool(h):
+        def pool_maps(h):
             def pool_row(step, carry):
                 i = step // narrow
                 at = pl.multiple_of(step % narrow * 128, 128)
@@ -635,7 +720,7 @@
             here = pl.ds(h * span, span)
             for t in range(2):
                 for own in range(2):
-                    if h == 0:
+                    if h == 1:
                         weights(i, t, own).wait()
                     part = jnp.dot(f_ref[t, here, :], wbuf[2 * t + own], preferred_element_type=F32)
                     if own:
@@ -643,27 +728,22 @@
                     else:
                         sb[zd, t, here, :] = part.astype(BF16)
                         swap(zd, t, h).start()
-                    if h == 1:
+                    if h == 0:
                         pl.when(i < nz - 1)(lambda t=t, own=own: weights(i + 1, t, own).start())
                 relay(near, nz - 1 - i, t, h, True)
 
-        for h in range(2):
-            pool(h)
+        for h in (1, 0):
+            pool_maps(h)
             produce(0, h)
 
         def both(i, carry):
-            for h in range(2):
+            for h in (1, 0):
                 produce(i, h)
             return carry
 
         lax.fori_loop(1, nz, both, 0)
 
-        def onward(h):
-            for axis in range(2):
-                feature_wait(1 - axis, 1 - axis, h)
-                turn(axis, h).start()
-
-        onward(0)
+        features_on(1)
         for t in range(2):
             for h in range(2):
                 mine(t, h).start()
@@ -678,15 +758,13 @@
 
         lax.fori_loop(0, rows // 16, part_towers, 0)
         for dm in range(nz - 1, 0, -1):
-            for h in range(2):
+            for h in (1, 0):
                 for t in range(2):
                     relay(near, dm, t, h, False)
                     relay(1 - near, dm, t, h, False)
-            if dm == nz - 1:
-                onward(1)
 
         tile, high = 256, 16
-        for h in range(2):
+        for h in (1, 0):
             for t in range(2):
                 swap(z, t, h).wait_recv()
                 pl.when(z > 0)(lambda t=t, h=h: hop(1, z, t, h).wait_recv())
@@ -724,7 +802,12 @@
                 totals = lax.fori_loop(h * count, (h + 1) * count, block, (zero,) * 6)
                 for k in range(6):
                     value = jnp.sum(totals[k], axis=0, keepdims=True)
-                    sums_ref[k, :, lanes] = value if h == 0 else sums_ref[k, :, lanes] + value
+                    sums_ref[k, :, lanes] = value if h == 1 else sums_ref[k, :, lanes] + value
+            if h == 1:
+                here = pl.ds(pl.multiple_of(b * spare, spare), spare)
+                pool_ref[:, here, :] = s_ref[:, base:, :]
+                for axis in range(2):
+                    pool.go(axis).start()
         for d in range(nz):
             for t in range(2):
                 for h in range(2):
@@ -747,7 +830,7 @@
         dma((4,)),
     )
     pl.run_scoped(
-        functools.partial(gather_phase, nz, cut, s_ref, acts_in, sums_ref, w_ref, maps_in, wide,
+        functools.partial(gather_phase, nz, cut, base, features_on, live_ref, pool_ref, pool, s_ref, acts_in, sums_ref, w_ref, maps_in, wide,
                           g_ref, acts_to, out_ref, total_ref, mixed_ref, sums_in, mix_in, rest),
         dma,
         dma,
@@ -773,6 +856,9 @@
                 feature(axis, t, h).wait_send()
         for t in range(2):
             mine(t, h).wait()
+    for axis in range(2):
+        pool.go(axis).wait_send()
+        pool.turn(axis).wait_send()
 
 
 def step_all(mesh, live, maps, weight, cot, bias, mix, mix_in):
@@ -781,13 +867,14 @@
     chans, rows = maps.shape[2:]
     width = weight.shape[1]
     outs = weight.shape[2] // parts
-    cut = rows * 25 // 32
+    base = rows * 3 // 4
+    cut = rows * 19 // 32
     vmem, dma = pltpu.VMEM, pltpu.SemaphoreType.DMA
     here = pl.BlockSpec(memory_space=pltpu.VMEM)
     far = pl.BlockSpec(memory_space=pl.ANY)
     sums = (6, 1, outs)
     return pl.pallas_call(
-        functools.partial(step_kernel, nz, cut),
+        functools.partial(step_kernel, nz, cut, base),
         in_specs=[pl.BlockSpec(memory_space=pltpu.SMEM), far, far, far, here, here, here],
         out_specs=[far, far, far, far, here, here],
         out_shape=[
@@ -819,14 +906,19 @@
             dma((2, 2)),
             dma((2, 2)),
             dma((2, 2)),
-            dma((2, 5, nz)),
-            dma((5, nz)),
+            vmem((2, groups * (rows - base), outs), BF16),
+            dma((2,)),
+            dma((2,)),
+            dma((2,)),
+            dma((2,)),
+            dma((2, 6, nz)),
+            dma((6, nz)),
             dma((2, nz + 1)),
             dma((2, nz + 1)),
             dma((2, nz + 1)),
             dma((2, nz + 1)),
-            dma((2, 4, nz)),
-            dma((2, 4, nz)),
+            dma((3, 4, nz)),
+            dma((3, 4, nz)),
             dma((2, 2)),
             dma((2, 2)),
             vmem(sums, F32),
@@ -846,13 +938,14 @@
     return jnp.sum(jnp.where(rows == cols, wide[:, :chans], 0.0), axis=0, keepdims=True)
 
 
-def update_kernel(chunks, ft_ref, s_ref, m_ref, w_ref, maps_ref, acts_ref, sums_ref, mixed_ref,
+def update_kernel(chunks, base, live_ref, ft_ref, s_ref, m_ref, w_ref, maps_ref, acts_ref, sums_ref, mixed_ref,
                   bias_ref, bias_m_ref, in_ref, in_m_ref, out_ref, out_m_ref,
                   grad_to, next_to, moment_to, maps_to, acts_to, bias_g, bias_n, bias_mn,
                   in_g, in_n, in_mn, out_g, out_n, out_mn,
-                  ft, s_in, m_in, w_in, g_out, n_out, m_out, maps_mid, acts_mid,
+                  raw, chosen, ft, s_in, m_in, w_in, g_out, n_out, m_out, maps_mid, acts_mid,
                   ft_sem, in_sem, out_sem, maps_in_sem, maps_out_sem, acts_sem):
     groups, parts, _, rows, tile = s_ref.shape
+    spare = rows - base
     steps, ahead, behind = 2 * parts, s_in.shape[0], g_out.shape[0]
     part = maps_mid.shape[0] // chunks
 
@@ -860,7 +953,7 @@
         t, j, slot = i // parts, i % parts, i % ahead
         lanes = pl.ds(pl.multiple_of(j * tile, tile), tile)
         return [
-            pltpu.make_async_copy(s_ref.at[:, j, t], s_in.at[slot], in_sem.at[slot, 0]),
+            pltpu.make_async_copy(s_ref.at[:, j, t, pl.ds(0, base), :], s_in.at[slot], in_sem.at[slot, 0]),
             pltpu.make_async_copy(m_ref.at[t, :, lanes], m_in.at[slot], in_sem.at[slot, 1]),
             pltpu.make_async_copy(w_ref.at[t, :, lanes], w_in.at[slot], in_sem.at[slot, 2]),
         ]
@@ -890,11 +983,25 @@
 
     load_acts = pltpu.make_async_copy(acts_ref, acts_mid, acts_sem.at[0])
     store_acts = pltpu.make_async_copy(acts_mid, acts_to, acts_sem.at[1])
-    towers = [pltpu.make_async_copy(ft_ref.at[t], ft.at[t], ft_sem.at[t]) for t in range(2)]
+    towers = [pltpu.make_async_copy(ft_ref.at[t], raw, ft_sem.at[t]) for t in range(2)]
     towers[0].start()
-    for i in range(ahead):
-        each(loads(i), start)
-    towers[1].start()
+    each(loads(0), start)
+    counts, excess, free = shares(live_ref, groups, base)
+    for k in range(groups):
+        for n in range(groups):
+            chosen[pl.ds(n * spare, spare), pl.ds(k * base, base)] = picks(
+                counts[k], free[k], counts[n], excess[n], base, spare, True
+            )
+
+    def pack(t):
+        towers[t].wait()
+        last = jnp.concatenate([raw[:, k * rows + base : (k + 1) * rows] for k in range(groups)], axis=1)
+        for k in range(groups):
+            lanes = pl.ds(k * base, base)
+            moved = jnp.dot(last, chosen[:, lanes], preferred_element_type=F32)
+            lane = lax.broadcasted_iota(jnp.int32, moved.shape, 1)
+            kept = raw[:, k * rows : k * rows + base].astype(F32)
+            ft[:, lanes] = jnp.where(lane < counts[k], kept, moved).astype(BF16)
 
     def step(grad, value, moment, rate, at, grad_ref, next_ref, moment_ref):
         after = MOMENTUM * moment[at] + grad
@@ -910,7 +1017,10 @@
             step(sums_ref[2 * i + j], out_ref, out_m_ref, STITCH_RATE, at, out_g, out_n, out_mn)
             step(turn_mix(mixed_ref[2 * i + j]), in_ref, in_m_ref, STITCH_RATE, at, in_g, in_n, in_mn)
 
-    towers[0].wait()
+    pack(0)
+    towers[1].start()
+    for i in range(1, ahead):
+        each(loads(i), start)
 
     def body(i, carry):
         slot, to = i % ahead, i % behind
@@ -928,11 +1038,11 @@
             load_acts.wait()
             store_acts.start()
 
-        pl.when(i == parts)(towers[1].wait)
+        pl.when(i == parts)(lambda: pack(1))
         each(loads(i), wait)
         pl.when(i >= behind)(lambda: each(stores(i - behind), wait))
         grad = jnp.dot(
-            ft[i // parts], s_in[slot].reshape(groups * rows, tile), preferred_element_type=F32
+            ft[...], s_in[slot].reshape(groups * base, tile), preferred_element_type=F32
         )
         g_out[to] = grad
         moment = MOMENTUM * m_in[slot] + grad
@@ -950,17 +1060,18 @@
     store_acts.wait()
 
 
-def weight_update(ft_all, gathered, moment, weight, maps, acts, sums, mixed, smalls):
+def weight_update(live, ft_all, gathered, moment, weight, maps, acts, sums, mixed, smalls):
     groups, parts, _, rows, outs = gathered.shape
     width = weight.shape[1]
     chunks = 2 * parts - 3
+    base = rows * 3 // 4
     here = pl.BlockSpec(memory_space=pltpu.VMEM)
     far = pl.BlockSpec(memory_space=pl.ANY)
     ahead, behind = 3, 2
     vmem, dma = pltpu.VMEM, pltpu.SemaphoreType.DMA
     return pl.pallas_call(
-        functools.partial(update_kernel, chunks),
-        in_specs=[far] * 6 + [here] * (2 + len(smalls)),
+        functools.partial(update_kernel, chunks, base),
+        in_specs=[pl.BlockSpec(memory_space=pltpu.SMEM)] + [far] * 6 + [here] * (2 + len(smalls)),
         out_specs=[far] * 5 + [here] * 9,
         out_shape=[
             jax.ShapeDtypeStruct(moment.shape, F32),
@@ -971,8 +1082,10 @@
         ]
         + [jax.ShapeDtypeStruct(a.shape, F32) for a in smalls[::2] for _ in range(3)],
         scratch_shapes=[
-            vmem((2, width, groups * rows), BF16),
-            vmem((ahead, groups, rows, outs), BF16),
+            vmem((width, groups * rows), BF16),
+            vmem((groups * (rows - base), groups * base), BF16),
+            vmem((width, groups * base), BF16),
+            vmem((ahead, groups, base, outs), BF16),
             vmem((ahead, width, outs), F32),
             vmem((ahead, width, outs), BF16),
             vmem((behind, width, outs), F32),
@@ -989,7 +1102,7 @@
         ],
         compiler_params=params(),
         name="weight_update",
-    )(ft_all, gathered, moment, weight, maps, acts, sums, mixed, *smalls)
+    )(live, ft_all, gathered, moment, weight, maps, acts, sums, mixed, *smalls)
 
 
 def fast_shards(
@@ -1026,6 +1139,7 @@
         stitch_out_next,
         stitch_out_moment_next,
     ) = weight_update(
+        live_rows,
         ft_all,
         gathered,
         weight_moment,
@@ -1059,7 +1173,7 @@
     rows, _, chans, _ = args[0].shape
     outs = args[2].shape[1]
     shape = mesh.shape["batch"] == 4 and mesh.shape["mp"] == 8
-    if shape and rows % 512 == 0 and outs % 256 == 0 and chans == 32:
+    if shape and rows == 512 and outs == 512 and chans == 32:
         return fast_shards(mesh, *args)
     return shards(*args)
 

time: 282 us -> 268 us (0.950)
  Pallas kernels: 281 us -> 267 us
    pallas_call x2, Pallas kernels: 281 us -> 267 us  [the longest x1 196 us: step_all(): pl.pallas_call(functools.partial(step_kernel, nz, cut, base), in_specs=[p...]
where the time goes in v5:
time: 268 us; the launch traced here: 267 us
  Pallas kernels  267 us (100%)
    pallas_call x1, Pallas kernels, step_all(): pl.pallas_call(functools.partial(step_kernel, nz, cut, base), in_specs=[p...  196 us
    pallas_call x1, Pallas kernels, weight_update(): pl.pallas_call(functools.partial(update_kernel, chunks, base), in_specs=[...  70.3 us

profile of v5, /device:TPU:0, one launch (start us, length us, event | category | flops | bytes accessed | tf_op | source)
XLA Modules:
  0.0 267.4 jit_solution(2132892290670797415)
XLA Ops:
  0.6 196.3 %step_all.1 = (bf16[4,8,2,512,512]{4,3,2,1,0:T(8,128)(2,1)}, bf16[2,1152,2048]{2,1,0:T(8,128)(2,1)}, bf16[512,2,512]{2,1,0:T(2,128)(2,1)}, bf16[2,169,32,512]{3,...) custom-call(s32[4]{0:T(128)} %live_ref.3, bf16[2,169,32,512]{3,2,1,0:T(8,128)(2,1)} %bitcast.5, ...), custom_call_target="tpu_custom_call" | custom-call | tf_op jit(solution)/shard_map/step_all/pallas_call | solution.py:876
  196.9 70.3 %weight_update.1 = (f32[2,1152,4096]{2,1,0:T(8,128)}, bf16[2,1152,4096]{2,1,0:T(8,128)(2,1)}, f32[2,1152,4096]{2,1,0:T(8,128)}, bf16[338,32,512]{2,1,0:T(8,128)(...) custom-call(s32[4]{0:T(128)} %live_ref.3, ...), custom_call_target="tpu_custom_call" | custom-call | tf_op jit(solution)/shard_map/weight_update/pallas_call | solution.py:1072

commit v6 on v5

--- a/solution.py
+++ b/solution.py
@@ -223,22 +223,28 @@
     )
 
 
-def unpool_row(chans, i, lanes, maps_ref, out_ref, cells, above, total, wide):
-    spans = [pl.ds(pl.multiple_of((6 * i + j) * chans, chans), chans) for j in range(6)]
+def mix_row(chans, i, lanes, maps_ref, cells, total):
     pooled = [pooled_row(maps_ref, t, i, lanes) for t in range(2)]
     sums = [total[k] for k in range(4)]
     for j in range(6):
+        span = pl.ds(pl.multiple_of((6 * i + j) * chans, chans), chans)
         for t in range(2):
-            grad = cells[t, spans[j], lanes]
+            grad = cells[t, span, lanes].astype(F32)
             for s in range(2):
                 sums[2 * t + s] += grad * pooled[s][j]
     for k in range(4):
         total[k] = sums[k]
+
+
+def unpool_row(chans, i, channels, lanes, cells, above, wide, out_ref):
+    start, count = channels
+    rows = pl.ds(start, count)
     for t in range(2):
         mixed = []
         for j in range(6):
-            value = wide[t] * cells[0, spans[j], lanes] + wide[2 + t] * cells[1, spans[j], lanes]
-            mixed.append(value * (1.0 / 9.0))
+            span = pl.ds(pl.multiple_of((6 * i + j) * chans + start, count), count)
+            first, second = (cells[k, span, lanes].astype(F32) for k in range(2))
+            mixed.append((wide[t, rows] * first + wide[2 + t, rows] * second) * (1.0 / 9.0))
         for x in range(13):
             if x % 2 == 1 or x == 0:
                 value = mixed[x // 2]
@@ -246,8 +252,8 @@
                 value = mixed[5]
             else:
                 value = mixed[x // 2 - 1] + mixed[x // 2]
-            out_ref[t, 26 * i + x, :, lanes] = (value + above[t, x, :, lanes]).astype(BF16)
-            out_ref[t, 26 * i + 13 + x, :, lanes] = value.astype(BF16)
+            out_ref[t, 26 * i + x, rows, lanes] = (value + above[t, x, :, lanes]).astype(BF16)
+            out_ref[t, 26 * i + 13 + x, rows, lanes] = value.astype(BF16)
             above[t, x, :, lanes] = value
 
 
@@ -274,7 +280,7 @@
 def gather_phase(nz, cut, base, features_on, live_ref, pool_ref, pool, s_ref, acts_in, sums_ref, w_ref, maps_in, wide,
                  g_ref, acts_to, out_ref, total_ref, mixed_ref, sums_in, mix_in, sems,
                  keep_sem, out_sem, w_sem, col_sem, acts_sem,
-                 acts_out, maps_out, wbuf, col, grads, cells, order, above, mix_total):
+                 acts_out, wbuf, col, grads, cells, order, mix_total):
     (line_send, line_recv, cross_send, cross_recv, half_send, half_recv, core_send, core_recv,
      small_send, small_recv, sums_mid, mix_mid) = sems
     b, m, z, c, columns = neighbours()
@@ -350,9 +356,6 @@
 
     first_sums = small(0, 0, sums_ref, sums_in.at[0])
     first_sums.start()
-    for axis in range(2):
-        pool.come(axis)
-        pool.turn(1 - axis).start()
     launch(5)
     core(2, 0, z, True).start()
     counts, excess, free = shares(live_ref, 4, base)
@@ -376,7 +379,6 @@
     launch(1)
     core(0, 0, z, True).start()
     core(1, 0, z, True).start()
-    features_on(0)
     mine.start()
 
     def pass_cross(p, zz):
@@ -453,19 +455,18 @@
             )
             lane = lax.broadcasted_iota(jnp.int32, value.shape, 1)
             grads[pl.ds(k % pieces * piece, piece), :] = jnp.where(lane < live, value, 0.0).astype(BF16)
-        cells[t] = jnp.dot(order[...], grads[...], preferred_element_type=F32)
+        cells[t] = jnp.dot(order[...], grads[...], preferred_element_type=F32).astype(BF16)
 
     blocks = rows // 128
 
     def maps_back(step, carry):
         i = step // blocks
         lanes = pl.ds(pl.multiple_of(step % blocks * 128, 128), 128)
-        unpool_row(chans, i, lanes, maps_in, maps_out, cells, above, mix_total, wide)
+        mix_row(chans, i, lanes, maps_in, cells, mix_total)
         return carry
 
     weights(0).start()
     fill_order(order, chans, True)
-    above[...] = jnp.zeros_like(above)
     mix_total[...] = jnp.zeros_like(mix_total)
     first_sums.wait()
     sums_mid[...] = sums_ref[...] + sums_in[0]
@@ -480,6 +481,7 @@
         sides(3, arrive)
         spread()
 
+    features_on(0)
     mine.wait()
     for zz in range(nz):
         for p in range(3):
@@ -504,11 +506,8 @@
     lax.fori_loop(0, 3 * blocks, maps_back, 0)
     pl.when(outer)(lambda: sides(2, late))
     lax.fori_loop(3 * blocks, 6 * blocks, maps_back, 0)
-    for t in range(2):
-        for x in range(13):
-            maps_out[t, 156 + x] = above[t, x].astype(BF16)
-    store_maps = pltpu.make_async_copy(maps_out, out_ref, out_sem)
-    store_maps.start()
+    store_cells = pltpu.make_async_copy(cells, out_ref, out_sem)
+    store_cells.start()
     for k in range(4):
         mix_in[0, k] = jnp.broadcast_to(jnp.sum(mix_total[k], axis=1, keepdims=True), (chans, 128))
     first_mix = small(1, 0, mix_in.at[0], mix_in.at[1])
@@ -527,7 +526,7 @@
     total_ref[...] = sums_mid[...] + sums_in[1]
     second_mix.wait()
     mixed_ref[...] = mix_mid[...] + mix_in[2]
-    store_maps.wait()
+    store_cells.wait()
     store_acts.wait()
 
     for zz in range(nz):
@@ -783,6 +782,10 @@
                     return carry
 
                 lax.fori_loop(0, span // step, gather, 0)
+            if h == 0:
+                for axis in range(2):
+                    pool.come(axis)
+                    pool.turn(1 - axis).start()
             for lane in range(outs // tile):
                 lanes = pl.ds(lane * tile, tile)
                 bias = [bias_ref[pl.ds(t, 1), lanes] for t in range(2)]
@@ -838,13 +841,11 @@
         dma((2 * nz,)),
         dma,
         vmem((rows, 2, outs), BF16),
-        vmem(maps_in.shape, BF16),
         vmem((2, width // 3, 2 * nz * outs), BF16),
         vmem((rows, 2 * nz * outs), BF16),
         vmem((width, rows), BF16),
-        vmem((2, width, rows), F32),
+        vmem((2, width, rows), BF16),
         vmem((width, width), BF16),
-        vmem((2, 13, chans, rows), F32),
         vmem((4, chans, 128), F32),
     )
     for h in range(2):
@@ -881,7 +882,7 @@
             jax.ShapeDtypeStruct((groups, parts, 2, rows, outs), BF16),
             jax.ShapeDtypeStruct((2, width, groups * rows), BF16),
             jax.ShapeDtypeStruct((rows, 2, outs), BF16),
-            jax.ShapeDtypeStruct(maps.shape, BF16),
+            jax.ShapeDtypeStruct((2, width, rows), BF16),
             jax.ShapeDtypeStruct(sums, F32),
             jax.ShapeDtypeStruct((4, chans, 128), F32),
         ],
@@ -938,16 +939,17 @@
     return jnp.sum(jnp.where(rows == cols, wide[:, :chans], 0.0), axis=0, keepdims=True)
 
 
-def update_kernel(chunks, base, live_ref, ft_ref, s_ref, m_ref, w_ref, maps_ref, acts_ref, sums_ref, mixed_ref,
+def update_kernel(base, live_ref, ft_ref, s_ref, m_ref, w_ref, cells_ref, acts_ref, sums_ref, mixed_ref,
                   bias_ref, bias_m_ref, in_ref, in_m_ref, out_ref, out_m_ref,
                   grad_to, next_to, moment_to, maps_to, acts_to, bias_g, bias_n, bias_mn,
                   in_g, in_n, in_mn, out_g, out_n, out_mn,
-                  raw, chosen, ft, s_in, m_in, w_in, g_out, n_out, m_out, maps_mid, acts_mid,
-                  ft_sem, in_sem, out_sem, maps_in_sem, maps_out_sem, acts_sem):
+                  raw, chosen, ft, s_in, m_in, w_in, g_out, n_out, m_out, maps_out, cells, above, wide, acts_mid,
+                  ft_sem, in_sem, out_sem, cells_sem, maps_sem, acts_sem):
     groups, parts, _, rows, tile = s_ref.shape
     spare = rows - base
     steps, ahead, behind = 2 * parts, s_in.shape[0], g_out.shape[0]
-    part = maps_mid.shape[0] // chunks
+    chans, lanes_all = maps_out.shape[2:]
+    share = chans // 2
 
     def loads(i):
         t, j, slot = i // parts, i % parts, i % ahead
@@ -973,13 +975,41 @@
 
     start, wait = lambda copy: copy.start(), lambda copy: copy.wait()
 
-    def maps_load(i):
-        block = pl.ds(pl.multiple_of(i * part, part), part)
-        return pltpu.make_async_copy(maps_ref.at[block], maps_mid.at[block], maps_in_sem.at[i])
-
-    def maps_store(i):
-        block = pl.ds(pl.multiple_of(i * part, part), part)
-        return pltpu.make_async_copy(maps_mid.at[block], maps_to.at[block], maps_out_sem.at[i])
+    load_cells = pltpu.make_async_copy(cells_ref, cells, cells_sem)
+
+    def maps_store(unit, t):
+        rows_two = pl.ds(pl.multiple_of(unit % 6 * 26, 26), 26)
+        block = (t, rows_two, pl.ds(pl.multiple_of(unit // 6 * share, share), share))
+        return pltpu.make_async_copy(maps_out.at[block], maps_to.at[block], maps_sem.at[unit, t])
+
+    def last_store(half, t):
+        block = (t, pl.ds(156, 13), pl.ds(half * share, share))
+        return pltpu.make_async_copy(maps_out.at[block], maps_to.at[block], maps_sem.at[12 + half, t])
+
+    def unpool(unit):
+        i = unit % 6
+        start = pl.multiple_of(unit // 6 * share, share)
+
+        @pl.when(i == 0)
+        def _():
+            above[...] = jnp.zeros_like(above)
+
+        def lane_block(k, carry):
+            lanes = pl.ds(pl.multiple_of(k * 128, 128), 128)
+            unpool_row(chans, i, (start, share), lanes, cells, above, wide, maps_out)
+            return carry
+
+        lax.fori_loop(0, lanes_all // 128, lane_block, 0)
+        for t in range(2):
+            maps_store(unit, t).start()
+        for half in range(2):
+
+            @pl.when(unit == 6 * half + 5)
+            def _(half=half):
+                for t in range(2):
+                    for x in range(13):
+                        maps_out[t, 156 + x, pl.ds(half * share, share)] = above[t, x].astype(BF16)
+                    last_store(half, t).start()
 
     load_acts = pltpu.make_async_copy(acts_ref, acts_mid, acts_sem.at[0])
     store_acts = pltpu.make_async_copy(acts_mid, acts_to, acts_sem.at[1])
@@ -1017,6 +1047,7 @@
             step(sums_ref[2 * i + j], out_ref, out_m_ref, STITCH_RATE, at, out_g, out_n, out_mn)
             step(turn_mix(mixed_ref[2 * i + j]), in_ref, in_m_ref, STITCH_RATE, at, in_g, in_n, in_mn)
 
+    spread_mix(in_ref, wide)
     pack(0)
     towers[1].start()
     for i in range(1, ahead):
@@ -1025,13 +1056,10 @@
     def body(i, carry):
         slot, to = i % ahead, i % behind
 
-        @pl.when(i >= ahead)
-        def _():
-            maps_load(i - ahead).wait()
-            maps_store(i - ahead).start()
-
-        pl.when(i < chunks)(lambda: maps_load(i).start())
         pl.when(i == 0)(load_acts.start)
+        pl.when(i == 0)(load_cells.start)
+        pl.when(i == 2)(load_cells.wait)
+        pl.when((i >= 2) & (i < 14))(lambda: unpool(i - 2))
 
         @pl.when(i == ahead)
         def _():
@@ -1055,29 +1083,32 @@
     lax.fori_loop(0, steps, body, 0)
     for k in range(behind):
         each(stores(steps - behind + k), wait)
-    for i in range(chunks):
-        maps_store(i).wait()
+    for t in range(2):
+        for unit in range(12):
+            maps_store(unit, t).wait()
+        for half in range(2):
+            last_store(half, t).wait()
     store_acts.wait()
 
 
-def weight_update(live, ft_all, gathered, moment, weight, maps, acts, sums, mixed, smalls):
+def weight_update(live, ft_all, gathered, moment, weight, maps_shape, cells, acts, sums, mixed, smalls):
     groups, parts, _, rows, outs = gathered.shape
     width = weight.shape[1]
-    chunks = 2 * parts - 3
+    chans = maps_shape[2]
     base = rows * 3 // 4
     here = pl.BlockSpec(memory_space=pltpu.VMEM)
     far = pl.BlockSpec(memory_space=pl.ANY)
     ahead, behind = 3, 2
     vmem, dma = pltpu.VMEM, pltpu.SemaphoreType.DMA
     return pl.pallas_call(
-        functools.partial(update_kernel, chunks, base),
+        functools.partial(update_kernel, base),
         in_specs=[pl.BlockSpec(memory_space=pltpu.SMEM)] + [far] * 6 + [here] * (2 + len(smalls)),
         out_specs=[far] * 5 + [here] * 9,
         out_shape=[
             jax.ShapeDtypeStruct(moment.shape, F32),
             jax.ShapeDtypeStruct(moment.shape, BF16),
             jax.ShapeDtypeStruct(moment.shape, F32),
-            jax.ShapeDtypeStruct(maps.shape, BF16),
+            jax.ShapeDtypeStruct(maps_shape, BF16),
             jax.ShapeDtypeStruct(acts.shape, BF16),
         ]
         + [jax.ShapeDtypeStruct(a.shape, F32) for a in smalls[::2] for _ in range(3)],
@@ -1091,18 +1122,21 @@
             vmem((behind, width, outs), F32),
             vmem((behind, width, outs), BF16),
             vmem((behind, width, outs), F32),
-            vmem(maps.shape, BF16),
+            vmem(maps_shape, BF16),
+            vmem(cells.shape, BF16),
+            vmem((2, 13, chans // 2, rows), F32),
+            vmem((4, chans, 128), F32),
             vmem(acts.shape, BF16),
             dma((2,)),
             dma((ahead, 3)),
             dma((behind, 3)),
-            dma((chunks,)),
-            dma((chunks,)),
+            dma,
+            dma((14, 2)),
             dma((2,)),
         ],
         compiler_params=params(),
         name="weight_update",
-    )(live, ft_all, gathered, moment, weight, maps, acts, sums, mixed, *smalls)
+    )(live, ft_all, gathered, moment, weight, cells, acts, sums, mixed, *smalls)
 
 
 def fast_shards(
@@ -1120,7 +1154,7 @@
     live_rows,
 ):
     maps = jnp.transpose(input_maps, (1, 3, 2, 0))
-    gathered, ft_all, acts, maps_out, sums, mixed = step_all(
+    gathered, ft_all, acts, cells, sums, mixed = step_all(
         mesh, live_rows, maps, dense_weight, cotangent, dense_bias, stitch_out, stitch_in
     )
     (
@@ -1144,13 +1178,14 @@
         gathered,
         weight_moment,
         dense_weight,
-        maps_out.reshape((-1,) + maps_out.shape[2:]),
+        maps.shape,
+        cells,
         acts,
         sums,
         mixed,
         [dense_bias, bias_moment, stitch_in, stitch_in_moment, stitch_out, stitch_out_moment],
     )
-    maps_grad = jnp.transpose(maps_grad.reshape(maps.shape), (3, 0, 2, 1))
+    maps_grad = jnp.transpose(maps_grad, (3, 0, 2, 1))
     return (
         activations,
         maps_grad,

time: 268 us -> 263 us (0.981)
  Pallas kernels: 267 us -> 262 us
where the time goes in v6:
time: 263 us
  Pallas kernels  262 us (100%)
    pallas_call x1, Pallas kernels, step_all(): pl.pallas_call(functools.partial(step_kernel, nz, cut, base), in_specs=[p...  194 us
    pallas_call x1, Pallas kernels, weight_update(): pl.pallas_call(functools.partial(update_kernel, base), in_specs=[pl.Block...  67.9 us

profile of v6, /device:TPU:0, one launch (start us, length us, event | category | flops | bytes accessed | tf_op | source)
XLA Modules:
  0.0 263.2 jit_solution(4098563880415110046)
XLA Ops:
  0.6 194.5 %step_all.1 = (bf16[4,8,2,512,512]{4,3,2,1,0:T(8,128)(2,1)}, bf16[2,1152,2048]{2,1,0:T(8,128)(2,1)}, bf16[512,2,512]{2,1,0:T(2,128)(2,1)}, bf16[2,1152,512]{2,1,...) custom-call(s32[4]{0:T(128)} %live_ref.3, bf16[2,169,32,512]{3,2,1,0:T(8,128)(2,1)} %bitcast.2, ...), custom_call_target="tpu_custom_call" | custom-call | tf_op jit(solution)/shard_map/step_all/pallas_call | solution.py:877
  195.1 67.9 %weight_update.1 = (f32[2,1152,4096]{2,1,0:T(8,128)}, bf16[2,1152,4096]{2,1,0:T(8,128)(2,1)}, f32[2,1152,4096]{2,1,0:T(8,128)}, bf16[2,169,32,512]{3,2,1,0:T(8,1...) custom-call(s32[4]{0:T(128)} %live_ref.3, ...), custom_call_target="tpu_custom_call" | custom-call | tf_op jit(solution)/shard_map/weight_update/pallas_call | solution.py:1103

commit v7 on v6

--- a/solution.py
+++ b/solution.py
@@ -492,7 +492,12 @@
     for j in range(2 * nz):
         column(1, j).start()
     pl.when(inner)(spread)
-    pl.when(outer)(lambda: sides(1, late))
+
+    @pl.when(outer)
+    def _():
+        sides(1, late)
+        sides(2, lambda zz, up: pass_cross(0, zz))
+
     features_grad(1)
 
     @pl.when(inner)
@@ -502,9 +507,9 @@
 
     end_diagonal(0, z)
     pl.when(inner)(lambda: sides(2, late))
-    pl.when(outer)(lambda: sides(2, lambda zz, up: pass_cross(0, zz)))
     lax.fori_loop(0, 3 * blocks, maps_back, 0)
     pl.when(outer)(lambda: sides(2, late))
+    sides(3, lambda zz, up: pass_cross(0, zz))
     lax.fori_loop(3 * blocks, 6 * blocks, maps_back, 0)
     store_cells = pltpu.make_async_copy(cells, out_ref, out_sem)
     store_cells.start()
@@ -514,7 +519,6 @@
     first_mix.start()
     pl.when(inner)(lambda: sides(2, lambda zz, up: pass_cross(0, zz)))
     sides(1, lambda zz, up: end_diagonal(0, zz))
-    sides(3, lambda zz, up: pass_cross(0, zz))
     first_mix.wait()
     mix_mid[...] = mix_in[0] + mix_in[1]
     second_mix = small(1, 1, mix_mid, mix_in.at[2])
@@ -1024,7 +1028,6 @@
             )
 
     def pack(t):
-        towers[t].wait()
         last = jnp.concatenate([raw[:, k * rows + base : (k + 1) * rows] for k in range(groups)], axis=1)
         for k in range(groups):
             lanes = pl.ds(k * base, base)
@@ -1048,10 +1051,11 @@
             step(turn_mix(mixed_ref[2 * i + j]), in_ref, in_m_ref, STITCH_RATE, at, in_g, in_n, in_mn)
 
     spread_mix(in_ref, wide)
+    towers[0].wait()
+    for i in range(1, ahead):
+        each(loads(i), start)
     pack(0)
     towers[1].start()
-    for i in range(1, ahead):
-        each(loads(i), start)
 
     def body(i, carry):
         slot, to = i % ahead, i % behind
@@ -1066,7 +1070,12 @@
             load_acts.wait()
             store_acts.start()
 
-        pl.when(i == parts)(lambda: pack(1))
+
+        @pl.when(i == parts)
+        def _():
+            towers[1].wait()
+            pack(1)
+
         each(loads(i), wait)
         pl.when(i >= behind)(lambda: each(stores(i - behind), wait))
         grad = jnp.dot(

time: 263 us -> 262 us (level)
  no operation moved by 1% of the time
where the time goes in v7:
time: 262 us; the launch traced here: 261 us
  Pallas kernels  260 us (99%)
    pallas_call x1, Pallas kernels, step_all(): pl.pallas_call(functools.partial(step_kernel, nz, cut, base), in_specs=[p...  192 us
    pallas_call x1, Pallas kernels, weight_update(): pl.pallas_call(functools.partial(update_kernel, base), in_specs=[pl.Block...  67.9 us

profile of v7, /device:TPU:0, one launch (start us, length us, event | category | flops | bytes accessed | tf_op | source)
XLA Modules:
  0.0 261.1 jit_solution(13370936661584498493)
XLA Ops:
  0.6 192.4 %step_all.1 = (bf16[4,8,2,512,512]{4,3,2,1,0:T(8,128)(2,1)}, bf16[2,1152,2048]{2,1,0:T(8,128)(2,1)}, bf16[512,2,512]{2,1,0:T(2,128)(2,1)}, bf16[2,1152,512]{2,1,...) custom-call(s32[4]{0:T(128)} %live_ref.3, bf16[2,169,32,512]{3,2,1,0:T(8,128)(2,1)} %bitcast.2, ...), custom_call_target="tpu_custom_call" | custom-call | tf_op jit(solution)/shard_map/step_all/pallas_call | solution.py:881
  193.0 67.9 %weight_update.1 = (f32[2,1152,4096]{2,1,0:T(8,128)}, bf16[2,1152,4096]{2,1,0:T(8,128)(2,1)}, f32[2,1152,4096]{2,1,0:T(8,128)}, bf16[2,169,32,512]{3,2,1,0:T(8,1...) custom-call(s32[4]{0:T(128)} %live_ref.3, ...), custom_call_target="tpu_custom_call" | custom-call | tf_op jit(solution)/shard_map/weight_update/pallas_call | solution.py:1112

commit v8 on v7

--- a/solution.py
+++ b/solution.py
@@ -488,10 +488,10 @@
             core_wait(p, 0, zz)
     for j in range(2 * nz):
         column(0, j).start()
+    pl.when(inner)(spread)
     features_grad(0)
     for j in range(2 * nz):
         column(1, j).start()
-    pl.when(inner)(spread)
 
     @pl.when(outer)
     def _():

time: 262 us -> 262 us (level)
  no operation moved by 1% of the time
where the time goes in v8:
time: 262 us; the launch traced here: 261 us
  Pallas kernels  260 us (99%)
    pallas_call x1, Pallas kernels, step_all(): pl.pallas_call(functools.partial(step_kernel, nz, cut, base), in_specs=[p...  192 us
    pallas_call x1, Pallas kernels, weight_update(): pl.pallas_call(functools.partial(update_kernel, base), in_specs=[pl.Block...  67.9 us

profile of v8, /device:TPU:0, one launch (start us, length us, event | category | flops | bytes accessed | tf_op | source)
XLA Modules:
  0.0 261.1 jit_solution(3771636774040980929)
XLA Ops:
  0.6 192.4 %step_all.1 = (bf16[4,8,2,512,512]{4,3,2,1,0:T(8,128)(2,1)}, bf16[2,1152,2048]{2,1,0:T(8,128)(2,1)}, bf16[512,2,512]{2,1,0:T(2,128)(2,1)}, bf16[2,1152,512]{2,1,...) custom-call(s32[4]{0:T(128)} %live_ref.3, bf16[2,169,32,512]{3,2,1,0:T(8,128)(2,1)} %bitcast.2, ...), custom_call_target="tpu_custom_call" | custom-call | tf_op jit(solution)/shard_map/step_all/pallas_call | solution.py:881
  193.0 67.9 %weight_update.1 = (f32[2,1152,4096]{2,1,0:T(8,128)}, bf16[2,1152,4096]{2,1,0:T(8,128)(2,1)}, f32[2,1152,4096]{2,1,0:T(8,128)}, bf16[2,169,32,512]{3,2,1,0:T(8,1...) custom-call(s32[4]{0:T(128)} %live_ref.3, ...), custom_call_target="tpu_custom_call" | custom-call | tf_op jit(solution)/shard_map/weight_update/pallas_call | solution.py:1112
